TPU v7x, 256 devices: a whole 4x4x8 slice. The times are simulated.
256 devices in a mesh: freq: 16 (over y, x), beam: 16 (over z, core).
Axes of the slice: x: 4, y: 4, z: 8, core: 2. Of those that a mesh axis runs over, the one named last changes fastest.
Arguments:
- voltages: bfloat16 [2, 256, 16, 16384], P(None, 'beam', None, 'freq'), may hold values from -6 to 6
- gains: float32 [2, 256, 16384], P(None, 'beam', 'freq'), may hold values from -6 to 6
- shifts: int32 [12, 4096], P(None, 'freq'), may hold values from 0 to 8, as said below
- widths: int32 [8], replicated, may hold values from 1 to 16, as said below
Outputs:
- dedispersed: bfloat16 [256, 16, 4096], P('beam', None, 'freq')
- peaks: float32 [8, 256, 4096], P(None, 'beam', 'freq')
Inputs may be any that keep to these rules, and one draw needn't show every extreme that they name: shifts[s, r] lies between 0 and min(2^s, 8); the last section reaches 8. widths[0] is 1, widths[k] lies between 2^(k-1) + 1 and 2^k capped at 16, and the last is 16.
All inputs are finite; a program needn't handle non-finite values.
Results may differ from a plain program's by a relative error of at most 0.0091.
Values may be sent and summed in bfloat16 or wider, within the bound.
No kernel may reach another device: no remote copies, remote signals or barrier semaphores. Data moves between devices by JAX's collectives and lax.ppermute only.
A program may use at most 128 MiB of HBM per device.

v0:
```python
import functools
import math

import jax
import jax.numpy as jnp
from jax import lax
from jax.experimental import pallas as pl
from jax.experimental.pallas import tpu as pltpu
from jax.sharding import PartitionSpec as P

FEEDS = 256
CHAN_SUM = 4
NSUB = 4096
TIME = 16
LANES = 128
MIB = 1024 * 1024


def steering(groups):
    size = FEEDS // groups
    row = lax.broadcasted_iota(jnp.int32, (2 * FEEDS, 2 * FEEDS), 0)
    col = lax.broadcasted_iota(jnp.int32, (2 * FEEDS, 2 * FEEDS), 1)
    beam, out_part = row % FEEDS, row // FEEDS
    feed = col // (2 * size) * size + col % size
    in_part = col // size % 2
    angles = (beam * feed % FEEDS).astype(jnp.float32) * (2.0 * math.pi / FEEDS)
    factor = 1.0 / math.sqrt(FEEDS)
    cosine = jnp.cos(angles) * factor
    sine = jnp.sin(angles) * factor
    value = jnp.where(in_part == out_part, cosine, jnp.where(out_part == 0, sine, -sine))
    return value.astype(jnp.bfloat16)


def calibrate_kernel(volt_ref, gain_ref, out_ref, scratch):
    feeds, samples, width = volt_ref.shape[1:]
    for j in range(width // LANES):
        lanes = slice(j * LANES, (j + 1) * LANES)
        for part in range(2):
            block = volt_ref[part, :, :, lanes].astype(jnp.float32)
            scratch[part, j] = block.reshape(feeds * samples, LANES)
        gain_re = gain_ref[0, :, lanes]
        gain_im = gain_ref[1, :, lanes]
        for t in range(samples):
            volt_re = scratch[0, j, pl.ds(t, feeds, stride=samples), :]
            volt_im = scratch[1, j, pl.ds(t, feeds, stride=samples), :]
            real = gain_re * volt_re - gain_im * volt_im
            imag = gain_re * volt_im + gain_im * volt_re
            out_ref[t, :feeds, lanes] = real.astype(jnp.bfloat16)
            out_ref[t, feeds:, lanes] = imag.astype(jnp.bfloat16)


def calibrate(voltages, gains):
    _, feeds, samples, width = voltages.shape
    step = 256
    return pl.pallas_call(
        calibrate_kernel,
        grid=(width // step,),
        in_specs=[
            pl.BlockSpec((2, feeds, samples, step), lambda i: (0, 0, 0, i)),
            pl.BlockSpec((2, feeds, step), lambda i: (0, 0, i)),
        ],
        out_specs=pl.BlockSpec((samples, 2 * feeds, step), lambda i: (0, 0, i)),
        out_shape=jax.ShapeDtypeStruct((samples, 2 * feeds, width), jnp.bfloat16),
        scratch_shapes=[pltpu.VMEM((2, step // LANES, feeds * samples, LANES), jnp.float32)],
        compiler_params=pltpu.CompilerParams(vmem_limit_bytes=8 * MIB),
        name="calibrate",
    )(voltages, gains)


def detect_kernel(matrix_ref, x_ref, out_ref):
    width = x_ref.shape[1]
    step = 256
    total = jnp.zeros((FEEDS, width // CHAN_SUM), jnp.float32)
    channel = lax.broadcasted_iota(jnp.int32, (step, width // CHAN_SUM), 0)
    group = lax.broadcasted_iota(jnp.int32, (step, width // CHAN_SUM), 1)
    for j in range(width // step):
        cols = slice(j * step, (j + 1) * step)
        formed = jnp.dot(matrix_ref[...], x_ref[:, cols], preferred_element_type=jnp.float32)
        power = formed[:FEEDS] * formed[:FEEDS] + formed[FEEDS:] * formed[FEEDS:]
        high = power.astype(jnp.bfloat16)
        low = (power - high.astype(jnp.float32)).astype(jnp.bfloat16)
        pooling = ((channel + j * step) // CHAN_SUM == group).astype(jnp.bfloat16)
        total += jnp.dot(high, pooling, preferred_element_type=jnp.float32)
        total += jnp.dot(low, pooling, preferred_element_type=jnp.float32)
    out_ref[...] = total.astype(jnp.bfloat16)


def detect(received, matrix):
    rows, width = received.shape
    return pl.pallas_call(
        detect_kernel,
        out_shape=jax.ShapeDtypeStruct((FEEDS, width // CHAN_SUM), jnp.bfloat16),
        compiler_params=pltpu.CompilerParams(vmem_limit_bytes=16 * MIB),
        name="detect",
    )(matrix, received)


def shifted(rows, bits):
    zero = jnp.zeros_like(rows[0])
    count = len(rows)
    for position, chosen in enumerate(bits):
        step = 1 << position
        rows = [jnp.where(chosen, rows[t + step] if t + step < count else zero, rows[t]) for t in range(count)]
    return rows


def digits(offsets, most, shape):
    wide = jnp.broadcast_to(offsets, shape)
    return [(wide >> position & 1) == 1 for position in range(most.bit_length())]


def tree_kernel(detected_ref, shifts_ref, own_ref, send_ref):
    samples, beams, width = detected_ref.shape
    lane = lax.broadcasted_iota(jnp.int32, (8, LANES), 1)
    blocks = width // LANES
    for b in range(0, beams, 8):
        values = []
        for j in range(blocks):
            lanes = slice(j * LANES, (j + 1) * LANES)
            rows = [detected_ref[t, :, lanes].astype(jnp.float32)[b : b + 8] for t in range(samples)]
            mean = functools.reduce(jnp.add, rows) * (1.0 / samples)
            values.append([row - mean for row in rows])
        for s in range(width.bit_length() - 1):
            half = 1 << s
            after = []
            for j in range(blocks):
                lanes = slice(j * LANES, (j + 1) * LANES)
                bits = digits(shifts_ref[s : s + 1, lanes], min(half, 8), (8, LANES))
                if half < LANES:
                    upper = (lane & half) != 0
                    lower_rows = [jnp.where(upper, pltpu.roll(x, half, 1), x) for x in values[j]]
                    higher_rows = [jnp.where(upper, x, pltpu.roll(x, LANES - half, 1)) for x in values[j]]
                else:
                    step = half // LANES
                    lower_rows = values[j & ~step]
                    higher_rows = values[j | step]
                moved = shifted(higher_rows, bits)
                after.append([x + y for x, y in zip(lower_rows, moved)])
            values = after
        for j in range(blocks):
            lanes = slice(j * LANES, (j + 1) * LANES)
            for t in range(samples):
                own_ref[t, b : b + 8, lanes] = values[j][t]
    send_ref[...] = own_ref[...].astype(jnp.bfloat16)


def tree(detected, shifts):
    return pl.pallas_call(
        tree_kernel,
        out_shape=[
            jax.ShapeDtypeStruct(detected.shape, jnp.float32),
            jax.ShapeDtypeStruct(detected.shape, jnp.bfloat16),
        ],
        compiler_params=pltpu.CompilerParams(vmem_limit_bytes=8 * MIB),
        name="tree",
    )(detected, shifts)


def merged(upper_ref, own_ref, partner_ref, shifts_ref, section, store):
    samples, beams, width = own_ref.shape
    upper = upper_ref[0] == 1
    for j in range(width // LANES):
        lanes = slice(j * LANES, (j + 1) * LANES)
        bits = digits(shifts_ref[section : section + 1, lanes], 8, (beams, LANES))
        own = [own_ref[t, :, lanes] for t in range(samples)]
        partner = [partner_ref[t, :, lanes].astype(jnp.float32) for t in range(samples)]
        lower_rows = [jnp.where(upper, y, x) for x, y in zip(own, partner)]
        higher_rows = [jnp.where(upper, x, y) for x, y in zip(own, partner)]
        moved = shifted(higher_rows, bits)
        for t in range(samples):
            store(t, lanes, lower_rows[t] + moved[t])


def merge_kernel(section, upper_ref, own_ref, partner_ref, shifts_ref, next_ref, send_ref):
    def store(t, lanes, value):
        next_ref[t, :, lanes] = value
        send_ref[t, :, lanes] = value.astype(jnp.bfloat16)

    merged(upper_ref, own_ref, partner_ref, shifts_ref, section, store)


def merge(section, upper, own, partner, shifts):
    return pl.pallas_call(
        functools.partial(merge_kernel, section),
        in_specs=[pl.BlockSpec(memory_space=pltpu.SMEM)] + [pl.BlockSpec(memory_space=pltpu.VMEM)] * 3,
        out_shape=[
            jax.ShapeDtypeStruct(own.shape, jnp.float32),
            jax.ShapeDtypeStruct(own.shape, jnp.bfloat16),
        ],
        compiler_params=pltpu.CompilerParams(vmem_limit_bytes=8 * MIB),
        name="merge",
    )(upper, own, partner, shifts)


def finish_kernel(section, upper_ref, widths_ref, own_ref, partner_ref, shifts_ref, series_ref, peaks_ref, sums, turned):
    samples, beams, width = own_ref.shape
    scale = 1.0 / (8.0 * math.sqrt(NSUB))

    def store(t, lanes, value):
        scaled = value * scale
        turned[lanes.start // LANES, pl.ds(t, beams, stride=samples), :] = scaled
        sums[t + 1, :, lanes] = scaled

    merged(upper_ref, own_ref, partner_ref, shifts_ref, section, store)
    for j in range(width // LANES):
        lanes = slice(j * LANES, (j + 1) * LANES)
        series_ref[:, :, lanes] = turned[j].reshape(beams, samples, LANES).astype(jnp.bfloat16)
    sums[0] = jnp.zeros((beams, width), jnp.float32)
    for t in range(2, samples + 1):
        sums[t] += sums[t - 1]
    for k in range(peaks_ref.shape[0]):
        reach = widths_ref[k]

        def widen(t, best):
            return jnp.maximum(best, sums[t + reach] - sums[t])

        best = lax.fori_loop(1, samples + 1 - reach, widen, sums[reach])
        peaks_ref[k] = best / jnp.sqrt(jnp.full((beams, width), reach).astype(jnp.float32))


def finish(section, upper, widths, own, partner, shifts):
    samples, beams, width = own.shape
    return pl.pallas_call(
        functools.partial(finish_kernel, section),
        in_specs=[pl.BlockSpec(memory_space=pltpu.SMEM)] * 2 + [pl.BlockSpec(memory_space=pltpu.VMEM)] * 3,
        out_shape=[
            jax.ShapeDtypeStruct((beams, samples, width), jnp.bfloat16),
            jax.ShapeDtypeStruct((widths.shape[0], beams, width), jnp.float32),
        ],
        scratch_shapes=[
            pltpu.VMEM((samples + 1, beams, width), jnp.float32),
            pltpu.VMEM((width // LANES, beams * samples, LANES), jnp.float32),
        ],
        compiler_params=pltpu.CompilerParams(vmem_limit_bytes=8 * MIB),
        name="finish",
    )(upper, widths, own, partner, shifts)


def swapped(block, axis, distance):
    count = lax.axis_size(axis)
    return lax.ppermute(block, axis, [(i, i ^ distance) for i in range(count)])


def shards(voltages, gains, shifts, widths):
    groups = lax.axis_size("beam")
    cross = lax.axis_size("freq").bit_length() - 1
    position = lax.axis_index("freq").astype(jnp.int32)
    matrix = steering(groups)
    calibrated = calibrate(voltages, gains)
    received = lax.all_to_all(calibrated, "beam", split_axis=0, concat_axis=0, tiled=True)
    detected = detect(received.reshape(2 * FEEDS, received.shape[2]), matrix)
    detected = detected.reshape(groups, FEEDS // groups, detected.shape[1])
    detected = lax.all_to_all(detected, "beam", split_axis=0, concat_axis=0, tiled=True)
    own, send = tree(detected, shifts)
    local = shifts.shape[1].bit_length() - 1
    for bit in range(cross):
        partner = swapped(send, "freq", 1 << bit)
        upper = (position >> bit & 1).reshape(1)
        if bit < cross - 1:
            own, send = merge(local + bit, upper, own, partner, shifts)
    return finish(local + cross - 1, upper, widths, own, partner, shifts)


def solution(mesh):
    return jax.shard_map(
        shards,
        mesh=mesh,
        in_specs=(P(None, "beam", None, "freq"), P(None, "beam", "freq"), P(None, "freq"), P()),
        out_specs=(P("beam", None, "freq"), P(None, "beam", "freq")),
        check_vma=False,
    )
```

profile of v0, /device:TPU:24, one launch (start us, length us, event | category | flops | bytes accessed | tf_op | source)
XLA Modules:
  0.0 84.8 jit_solution(6260918110984039713)
XLA Ops:
  0.6 0.0 copy-start
  0.6 1.2 %copy-done = bf16[2,16,16,1024]{3,2,1,0:T(8,128)(2,1)S(1)} copy-done((bf16[2,16,16,1024]{3,2,1,0:T(8,128)(2,1)S(1)}, bf16[2,16,16,1024]{3,2,1,0:T(8,128)(2,1)}, u32[]{:S(2)}) %copy-start) | copy-done | bytes 1048600
  1.9 0.9 %copy-done.2 = f32[2,16,1024]{2,1,0:T(8,128)S(1)} copy-done((f32[2,16,1024]{2,1,0:T(8,128)S(1)}, f32[2,16,1024]{2,1,0:T(8,128)}, u32[]{:S(2)}) %copy-start.2) | copy-done | bytes 131096
  2.8 2.2 %calibrate.1 = bf16[16,32,1024]{2,1,0:T(8,128)(2,1)} custom-call(bf16[2,16,16,1024]{3,2,1,0:T(8,128)(2,1)S(1)} %copy-done, f32[2,16,1024]{2,1,0:T(8,128)S(1)} %copy-done.2), custom_call_target="tpu_custom_call" | custom-call | tf_op jit(solution)/shard_map/calibrate/pallas_call | solution.py:55
  5.0 8.6 %all-to-all-start = ((bf16[16,32,1024]{2,1,0:T(8,128)(2,1)}), bf16[16,32,1024]{2,1,0:T(8,128)(2,1)S(1)}, u32[]{:S(2)}, u32[]{:S(2)}) async-start(bf16[16,32,1024]{2,1,0:T(8,128)(2,1)} %calibrate.1), calls=%async_computation | async-start | bytes 2097152 | tf_op jit(solution)/shard_map/all_to_all | solution.py:250
  13.7 5.7 %fusion.4.matrix_ref = bf16[512,512]{1,0:T(8,128)(2,1)S(1)} fusion(s32[512]{0:T(512)S(1)} %get-tuple-element.20, s32[512]{0:T(512)S(1)} %get-tuple-element.24, s32[512]{0:T(512)S(1)} %get-tuple-element.18, s32[512]{0:T(512)S(1)} %get-tuple-element.25, s32[512]{0:T(512)S(1)} %get-tuple-element.22, s32[512]{0:T(512)S(1)} %get-tuple-element.23, ...), kind=kLoop, calls=%fused_computation.15 | loop fusion | flops 10485760 | bytes 547328 | tf_op jit(solution)/shard_map/convert_element_type | solution.py:31
  19.4 20.8 %all-to-all-done = bf16[16,32,1024]{2,1,0:T(8,128)(2,1)S(1)} async-done(((bf16[16,32,1024]{2,1,0:T(8,128)(2,1)}), bf16[16,32,1024]{2,1,0:T(8,128)(2,1)S(1)}, u32[]{:S(2)}, u32[]{:S(2)}) %all-to-all-start) | async-done | bytes 1048608 | tf_op jit(solution)/shard_map/all_to_all | solution.py:250
  40.2 1.9 %detect.1 = bf16[256,256]{1,0:T(8,128)(2,1)S(1)} custom-call(bf16[512,512]{1,0:T(8,128)(2,1)S(1)} %fusion.4.matrix_ref, bf16[512,1024]{1,0:T(8,128)(2,1)S(1)} %bitcast.6), custom_call_target="tpu_custom_call" | custom-call | tf_op jit(solution)/shard_map/detect/pallas_call | solution.py:90
  42.1 0.0 copy-start.1
  42.1 13.3 %all_to_all.10.detected_ref = bf16[16,16,256]{2,1,0:T(8,128)(2,1)S(1)} all-to-all(bf16[16,16,256]{2,1,0:T(8,128)(2,1)S(1)} %bitcast.7), channel_id=1, replica_groups=mesh['freq'=16,'beam'=16] {'beam'}, dimensions={0} | all-to-all | bytes 262144 | tf_op jit(solution)/shard_map/all_to_all | solution.py:253
  55.4 1.4 %tree.1 = (f32[16,16,256]{2,1,0:T(8,128)S(1)}, bf16[16,16,256]{2,1,0:T(8,128)(2,1)S(1)}) custom-call(bf16[16,16,256]{2,1,0:T(8,128)(2,1)S(1)} %all_to_all.10.detected_ref, s32[12,256]{1,0:T(8,128)S(1)} %copy-done.1), custom_call_target="tpu_custom_call" | custom-call | tf_op jit(solution)/shard_map/tree/pallas_call | solution.py:148
  56.9 1.6 %collective-permute-start = (bf16[16,16,256]{2,1,0:T(8,128)(2,1)S(1)}, bf16[16,16,256]{2,1,0:T(8,128)(2,1)S(1)}, u32[]{:S(2)}, u32[]{:S(2)}) collective-permute-start(bf16[16,16,256]{2,1,0:T(8,128)(2,1)S(1)} %get-tuple-element.11), channel_id=1, source_target_pairs={{0,16},{16,0},{32,48},{48,32},{64,80},{80,64},{96,112},{112,96},{1... | collective-permute-start | bytes 393224 | tf_op jit(solution)/shard_map/ppermute | solution.py:241
  58.5 4.7 %collective-permute-done.partner_ref = bf16[16,16,256]{2,1,0:T(8,128)(2,1)S(1)} collective-permute-done((bf16[16,16,256]{2,1,0:T(8,128)(2,1)S(1)}, bf16[16,16,256]{2,1,0:T(8,128)(2,1)S(1)}, u32[]{:S(2)}, u32[]{:S(2)}) %collective-permute-start) | collective-permute-done | bytes 131104 | tf_op jit(solution)/shard_map/ppermute | solution.py:241
  63.2 0.1 merge.3
  63.3 3.1 %collective-permute-start.1 = (bf16[16,16,256]{2,1,0:T(8,128)(2,1)S(1)}, bf16[16,16,256]{2,1,0:T(8,128)(2,1)S(1)}, u32[]{:S(2)}, u32[]{:S(2)}) collective-permute-start(bf16[16,16,256]{2,1,0:T(8,128)(2,1)S(1)} %get-tuple-element.13), channel_id=1, source_target_pairs={{0,32},{16,48},{32,0},{48,16},{64,96},{80,112},{96,64},{112,80},{1... | collective-permute-start | bytes 393224 | tf_op jit(solution)/shard_map/ppermute | solution.py:241
  66.4 3.9 %collective-permute-done.1.partner_ref = bf16[16,16,256]{2,1,0:T(8,128)(2,1)S(1)} collective-permute-done((bf16[16,16,256]{2,1,0:T(8,128)(2,1)S(1)}, bf16[16,16,256]{2,1,0:T(8,128)(2,1)S(1)}, u32[]{:S(2)}, u32[]{:S(2)}) %collective-permute-start.1) | collective-permute-done | bytes 131104 | tf_op jit(solution)/shard_map/ppermute | solution.py:241
  70.3 0.1 merge.4
  70.4 0.8 collective-permute-start.2
  71.2 4.4 %collective-permute-done.2.partner_ref = bf16[16,16,256]{2,1,0:T(8,128)(2,1)S(1)} collective-permute-done((bf16[16,16,256]{2,1,0:T(8,128)(2,1)S(1)}, bf16[16,16,256]{2,1,0:T(8,128)(2,1)S(1)}, u32[]{:S(2)}, u32[]{:S(2)}) %collective-permute-start.2) | collective-permute-done | bytes 131104 | tf_op jit(solution)/shard_map/ppermute | solution.py:241
  75.6 0.1 merge.5
  75.7 1.2 %collective-permute-start.3 = (bf16[16,16,256]{2,1,0:T(8,128)(2,1)S(1)}, bf16[16,16,256]{2,1,0:T(8,128)(2,1)S(1)}, u32[]{:S(2)}, u32[]{:S(2)}) collective-permute-start(bf16[16,16,256]{2,1,0:T(8,128)(2,1)S(1)} %get-tuple-element.17), channel_id=1, source_target_pairs={{0,128},{16,144},{32,160},{48,176},{64,192},{80,208},{96,224},{112... | collective-permute-start | bytes 393224 | tf_op jit(solution)/shard_map/ppermute | solution.py:241
  76.9 5.4 %collective-permute-done.3.partner_ref = bf16[16,16,256]{2,1,0:T(8,128)(2,1)S(1)} collective-permute-done((bf16[16,16,256]{2,1,0:T(8,128)(2,1)S(1)}, bf16[16,16,256]{2,1,0:T(8,128)(2,1)S(1)}, u32[]{:S(2)}, u32[]{:S(2)}) %collective-permute-start.3) | collective-permute-done | bytes 131104 | tf_op jit(solution)/shard_map/ppermute | solution.py:241
  82.3 0.7 copy-done.3
  82.9 1.9 %finish.1 = (bf16[16,16,256]{2,1,0:T(8,128)(2,1)}, f32[8,16,256]{2,1,0:T(8,128)}) custom-call(s32[1]{0:T(128)} %bitcast.upper_ref, s32[8]{0:T(128)S(1)} %copy-done.3, f32[16,16,256]{2,1,0:T(8,128)S(1)} %get-tuple-element.16.own_ref, bf16[16,16,256]{2,1,0:T(8,128)(2,1)S(1)} %collective-permute-done.3.partner_ref, s32[12,256]{1,0:T(8,128)S(1)} %copy-done.1), custom_call_target="tpu_custom_call" | custom-call | tf_op jit(solution)/shard_map/finish/pallas_call | solution.py:223
  (11 shorter events, 0.1 us)
Async XLA Ops:
  0.6 1.2 %copy-start = (bf16[2,16,16,1024]{3,2,1,0:T(8,128)(2,1)S(1)}, bf16[2,16,16,1024]{3,2,1,0:T(8,128)(2,1)}, u32[]{:S(2)}) copy-start(bf16[2,16,16,1024]{3,2,1,0:T(8,128)(2,1)} %volt_ref.1) | copy-start | bytes 3145732
  1.9 0.9 %copy-start.2 = (f32[2,16,1024]{2,1,0:T(8,128)S(1)}, f32[2,16,1024]{2,1,0:T(8,128)}, u32[]{:S(2)}) copy-start(f32[2,16,1024]{2,1,0:T(8,128)} %gain_ref.1) | copy-start | bytes 393220
  5.0 35.2 %all-to-all-start = ((bf16[16,32,1024]{2,1,0:T(8,128)(2,1)}), bf16[16,32,1024]{2,1,0:T(8,128)(2,1)S(1)}, u32[]{:S(2)}, u32[]{:S(2)}) async-start(bf16[16,32,1024]{2,1,0:T(8,128)(2,1)} %calibrate.1), calls=%async_computation | async-start | bytes 2097152 | tf_op jit(solution)/shard_map/all_to_all | solution.py:250
  42.1 13.3 %copy-start.1 = (s32[12,256]{1,0:T(8,128)S(1)}, s32[12,256]{1,0:T(8,128)}, u32[]{:S(2)}) copy-start(s32[12,256]{1,0:T(8,128)} %shifts_ref.9) | copy-start | bytes 36868
  56.9 6.3 %collective-permute-start = (bf16[16,16,256]{2,1,0:T(8,128)(2,1)S(1)}, bf16[16,16,256]{2,1,0:T(8,128)(2,1)S(1)}, u32[]{:S(2)}, u32[]{:S(2)}) collective-permute-start(bf16[16,16,256]{2,1,0:T(8,128)(2,1)S(1)} %get-tuple-element.11), channel_id=1, source_target_pairs={{0,16},{16,0},{32,48},{48,32},{64,80},{80,64},{96,112},{112,96},{1... | collective-permute-start | bytes 393224 | tf_op jit(solution)/shard_map/ppermute | solution.py:241
  63.3 7.0 %collective-permute-start.1 = (bf16[16,16,256]{2,1,0:T(8,128)(2,1)S(1)}, bf16[16,16,256]{2,1,0:T(8,128)(2,1)S(1)}, u32[]{:S(2)}, u32[]{:S(2)}) collective-permute-start(bf16[16,16,256]{2,1,0:T(8,128)(2,1)S(1)} %get-tuple-element.13), channel_id=1, source_target_pairs={{0,32},{16,48},{32,0},{48,16},{64,96},{80,112},{96,64},{112,80},{1... | collective-permute-start | bytes 393224 | tf_op jit(solution)/shard_map/ppermute | solution.py:241
  70.4 5.2 %collective-permute-start.2 = (bf16[16,16,256]{2,1,0:T(8,128)(2,1)S(1)}, bf16[16,16,256]{2,1,0:T(8,128)(2,1)S(1)}, u32[]{:S(2)}, u32[]{:S(2)}) collective-permute-start(bf16[16,16,256]{2,1,0:T(8,128)(2,1)S(1)} %get-tuple-element.15), channel_id=1, source_target_pairs={{0,64},{16,80},{32,96},{48,112},{64,0},{80,16},{96,32},{112,48},{1... | collective-permute-start | bytes 393224 | tf_op jit(solution)/shard_map/ppermute | solution.py:241
  75.7 6.6 %collective-permute-start.3 = (bf16[16,16,256]{2,1,0:T(8,128)(2,1)S(1)}, bf16[16,16,256]{2,1,0:T(8,128)(2,1)S(1)}, u32[]{:S(2)}, u32[]{:S(2)}) collective-permute-start(bf16[16,16,256]{2,1,0:T(8,128)(2,1)S(1)} %get-tuple-element.17), channel_id=1, source_target_pairs={{0,128},{16,144},{32,160},{48,176},{64,192},{80,208},{96,224},{112... | collective-permute-start | bytes 393224 | tf_op jit(solution)/shard_map/ppermute | solution.py:241
  82.3 0.7 copy-start.3
where the time goes:
time: 85.1 us; the launch traced here: 84.8 us
  waiting for transfers between devices  39.2 us (46%)
  starting transfers between devices  15.2 us (18%)
  blocking collectives  13.3 us (16%)
  Pallas kernels  7.69 us (9%)
  other arithmetic  5.79 us (7%)
  local copies, waits for them, and re-layouts  2.78 us (3%)
    all_to_all x1, waiting for transfers between devices, shards(): lax.all_to_all(calibrated, 'beam', split_axis=0, concat_axis=0, tiled=True)  20.8 us
    ppermute x4, waiting for transfers between devices, swapped(): return lax.ppermute(block, axis, [(i, i ^ distance) for i in range(count)])  18.4 us
    all_to_all x1, blocking collectives, shards(): lax.all_to_all(detected, 'beam', split_axis=0, concat_axis=0, tiled=True)  13.3 us
    all_to_all x1, starting transfers between devices, shards(): lax.all_to_all(calibrated, 'beam', split_axis=0, concat_axis=0, tiled=True)  8.57 us
    ppermute x4, starting transfers between devices, swapped(): return lax.ppermute(block, axis, [(i, i ^ distance) for i in range(count)])  6.68 us
    convert_element_type x1, other arithmetic, steering(): return value.astype(jnp.bfloat16)  5.74 us
    unnamed x8, local copies, waits for them, and re-layouts  2.78 us
    pallas_call x1, Pallas kernels, calibrate(): pl.pallas_call(calibrate_kernel, grid=(width // step,), in_specs=[pl.Bloc...  2.23 us
  transfers between devices with their start and end apart: 5, of which 5 were waited for; matrix products, arithmetic and copies ran while one was open for 7% of the time, Pallas kernels for 0%

commit v1 on v0

v1 whole, which is shorter than its diff:
```python
import functools
import math

import jax
import jax.numpy as jnp
from jax import lax
from jax.experimental import pallas as pl
from jax.experimental.pallas import tpu as pltpu
from jax.sharding import PartitionSpec as P

FEEDS = 256
CHAN_SUM = 4
NSUB = 4096
TIME = 16
LANES = 128
MIB = 1024 * 1024


def steering(groups):
    size = FEEDS // groups
    row = lax.broadcasted_iota(jnp.int32, (2 * FEEDS, 2 * FEEDS), 0)
    col = lax.broadcasted_iota(jnp.int32, (2 * FEEDS, 2 * FEEDS), 1)
    out_part = row // FEEDS
    beam = row % groups * size + row % FEEDS // groups
    feed = col // (2 * size) * size + col % size
    in_part = col // size % 2
    angles = (beam * feed % FEEDS).astype(jnp.float32) * (2.0 * math.pi / FEEDS)
    factor = 1.0 / math.sqrt(FEEDS)
    cosine = jnp.cos(angles) * factor
    sine = jnp.sin(angles) * factor
    value = jnp.where(in_part == out_part, cosine, jnp.where(out_part == 0, sine, -sine))
    return value.astype(jnp.bfloat16)


def calibrate_kernel(volt_ref, gain_ref, out_ref, scratch):
    feeds, samples, width = volt_ref.shape[1:]
    for j in range(width // LANES):
        lanes = slice(j * LANES, (j + 1) * LANES)
        for part in range(2):
            block = volt_ref[part, :, :, lanes].astype(jnp.float32)
            scratch[part, j] = block.reshape(feeds * samples, LANES)
        gain_re = gain_ref[0, :, lanes]
        gain_im = gain_ref[1, :, lanes]
        for t in range(samples):
            volt_re = scratch[0, j, pl.ds(t, feeds, stride=samples), :]
            volt_im = scratch[1, j, pl.ds(t, feeds, stride=samples), :]
            real = gain_re * volt_re - gain_im * volt_im
            imag = gain_re * volt_im + gain_im * volt_re
            out_ref[t, :feeds, lanes] = real.astype(jnp.bfloat16)
            out_ref[t, feeds:, lanes] = imag.astype(jnp.bfloat16)


def calibrate(voltages, gains):
    _, feeds, samples, width = voltages.shape
    step = 256
    return pl.pallas_call(
        calibrate_kernel,
        grid=(width // step,),
        in_specs=[
            pl.BlockSpec((2, feeds, samples, step), lambda i: (0, 0, 0, i)),
            pl.BlockSpec((2, feeds, step), lambda i: (0, 0, i)),
        ],
        out_specs=pl.BlockSpec((samples, 2 * feeds, step), lambda i: (0, 0, i)),
        out_shape=jax.ShapeDtypeStruct((samples, 2 * feeds, width), jnp.bfloat16),
        scratch_shapes=[pltpu.VMEM((2, step // LANES, feeds * samples, LANES), jnp.float32)],
        compiler_params=pltpu.CompilerParams(vmem_limit_bytes=60 * MIB),
        name="calibrate",
    )(voltages, gains)


def detect_kernel(matrix_ref, x_ref, out_ref, scratch):
    width = x_ref.shape[1]
    step = 256
    total = jnp.zeros((FEEDS, width // CHAN_SUM), jnp.float32)
    channel = lax.broadcasted_iota(jnp.int32, (step, width // CHAN_SUM), 0)
    group = lax.broadcasted_iota(jnp.int32, (step, width // CHAN_SUM), 1)
    for j in range(width // step):
        cols = slice(j * step, (j + 1) * step)
        formed = jnp.dot(matrix_ref[...], x_ref[:, cols], preferred_element_type=jnp.float32)
        power = formed[:FEEDS] * formed[:FEEDS] + formed[FEEDS:] * formed[FEEDS:]
        high = power.astype(jnp.bfloat16)
        low = (power - high.astype(jnp.float32)).astype(jnp.bfloat16)
        pooling = ((channel + j * step) // CHAN_SUM == group).astype(jnp.bfloat16)
        total += jnp.dot(high, pooling, preferred_element_type=jnp.float32)
        total += jnp.dot(low, pooling, preferred_element_type=jnp.float32)
    pieces = width // CHAN_SUM // LANES
    for h in range(pieces):
        scratch[pl.ds(h, FEEDS, stride=pieces), :] = total[:, h * LANES : (h + 1) * LANES]
    out_ref[...] = scratch[...].astype(jnp.bfloat16)


def detect(received, matrix):
    shape = (FEEDS * received.shape[1] // CHAN_SUM // LANES, LANES)
    return pl.pallas_call(
        detect_kernel,
        out_shape=jax.ShapeDtypeStruct(shape, jnp.bfloat16),
        scratch_shapes=[pltpu.VMEM(shape, jnp.float32)],
        compiler_params=pltpu.CompilerParams(vmem_limit_bytes=16 * MIB),
        name="detect",
    )(matrix, received)


def shifted(rows, bits):
    zero = jnp.zeros_like(rows[0])
    count = len(rows)
    for position, chosen in enumerate(bits):
        step = 1 << position
        rows = [jnp.where(chosen, rows[t + step] if t + step < count else zero, rows[t]) for t in range(count)]
    return rows


def digits(offsets, most):
    return [(offsets >> position & 1) == 1 for position in range(most.bit_length())]


def merged(lower_rows, higher_rows, bits):
    return [x + y for x, y in zip(lower_rows, shifted(higher_rows, bits))]


def folded(rows, axis, half, bits):
    size = rows[0].shape[axis]
    upper = (lax.broadcasted_iota(jnp.int32, rows[0].shape, axis) & half) != 0
    lower_rows = [jnp.where(upper, pltpu.roll(x, half, axis), x) for x in rows]
    higher_rows = [jnp.where(upper, x, pltpu.roll(x, size - half, axis)) for x in rows]
    return merged(lower_rows, higher_rows, bits)


def tree_kernel(detected_ref, shifts_ref, out_ref, wide, held, turned):
    blocks, samples, width = out_ref.shape
    pieces = width // LANES
    scale = 1.0 / (8.0 * math.sqrt(NSUB))
    wide[...] = detected_ref[...].astype(jnp.float32)

    def bits_of(section, group, piece):
        offsets = shifts_ref[section, group * 8 : (group + 1) * 8, piece * LANES : (piece + 1) * LANES]
        return digits(offsets, min(1 << section, 8))

    lane_bits = LANES.bit_length() - 1
    for group in range(blocks // 8):
        for piece in range(pieces):
            rows = []
            for t in range(samples):
                first = group * 8 * samples * pieces + t * pieces + piece
                rows.append(wide[pl.ds(first, 8, stride=samples * pieces), :])
            mean = functools.reduce(jnp.add, rows) * (1.0 / samples)
            rows = [row - mean for row in rows]
            for section in range(lane_bits):
                rows = folded(rows, 1, 1 << section, bits_of(section, group, piece))
            for t in range(samples):
                held[piece, group, t] = rows[t]
    for group in range(blocks // 8):
        for piece in range(pieces):
            lower_rows = [held[0, group, t] for t in range(samples)]
            higher_rows = [held[1, group, t] for t in range(samples)]
            rows = merged(lower_rows, higher_rows, bits_of(lane_bits, group, piece))
            for bit in range(3):
                section = lane_bits + 1 + bit
                rows = folded(rows, 0, 1 << bit, bits_of(section, group, piece))
            for t in range(samples):
                first = (group * pieces + piece) * samples * 8 + t * 8
                wide[first : first + 8, :] = rows[t]
    for piece in range(pieces):
        parts = []
        for group in range(2):
            first = (group * pieces + piece) * samples * 8
            parts.append([wide[first + t * 8 : first + t * 8 + 8, :] for t in range(samples)])
        for group in range(2):
            rows = merged(parts[0], parts[1], bits_of(lane_bits + 4, group, piece))
            for t in range(samples):
                turned[piece, pl.ds(group * 8 * samples + t, 8, stride=samples), :] = rows[t] * scale
        block = turned[piece].reshape(blocks, samples, LANES)
        out_ref[:, :, piece * LANES : (piece + 1) * LANES] = block.astype(jnp.bfloat16)


def tree(detected, shifts):
    sections, blocks, width = shifts.shape
    pieces = width // LANES
    rows = detected.shape[0]
    return pl.pallas_call(
        tree_kernel,
        out_shape=jax.ShapeDtypeStruct((blocks, TIME, width), jnp.bfloat16),
        scratch_shapes=[
            pltpu.VMEM((rows, LANES), jnp.float32),
            pltpu.VMEM((pieces, blocks // 8, TIME, 8, LANES), jnp.float32),
            pltpu.VMEM((pieces, blocks * TIME, LANES), jnp.float32),
        ],
        compiler_params=pltpu.CompilerParams(vmem_limit_bytes=8 * MIB),
        name="tree",
    )(detected, shifts)


def peaks_kernel(widths_ref, series_ref, same_ref, peaks_ref, wide, sums):
    beams, samples, width = series_ref.shape
    same_ref[...] = series_ref[...]
    for j in range(width // LANES):
        lanes = slice(j * LANES, (j + 1) * LANES)
        wide[j] = series_ref[:, :, lanes].astype(jnp.float32).reshape(beams * samples, LANES)
        total = jnp.zeros((beams, LANES), jnp.float32)
        sums[0, :, lanes] = total
        for t in range(samples):
            total = total + wide[j, pl.ds(t, beams, stride=samples), :]
            sums[t + 1, :, lanes] = total
    for k in range(peaks_ref.shape[0]):
        reach = widths_ref[k]

        def widen(t, best):
            return jnp.maximum(best, sums[t + reach] - sums[t])

        best = lax.fori_loop(1, samples + 1 - reach, widen, sums[reach])
        peaks_ref[k] = best / jnp.sqrt(jnp.full((beams, width), reach).astype(jnp.float32))


def peaks(widths, series):
    beams, samples, width = series.shape
    return pl.pallas_call(
        peaks_kernel,
        in_specs=[pl.BlockSpec(memory_space=pltpu.SMEM), pl.BlockSpec(memory_space=pltpu.VMEM)],
        out_shape=[
            jax.ShapeDtypeStruct(series.shape, series.dtype),
            jax.ShapeDtypeStruct((widths.shape[0], beams, width), jnp.float32),
        ],
        scratch_shapes=[
            pltpu.VMEM((width // LANES, beams * samples, LANES), jnp.float32),
            pltpu.VMEM((samples + 1, beams, width), jnp.float32),
        ],
        compiler_params=pltpu.CompilerParams(vmem_limit_bytes=8 * MIB),
        name="peaks",
    )(widths, series)


def gathered(block, axis):
    count = lax.axis_size(axis)
    position = lax.axis_index(axis)
    whole = block[None]
    for bit in range(count.bit_length() - 1):
        other = lax.ppermute(whole, axis, [(i, i ^ 1 << bit) for i in range(count)])
        upper = (position >> bit & 1) == 1
        whole = jnp.concatenate([jnp.where(upper, other, whole), jnp.where(upper, whole, other)])
    return whole


def exchanged(block, axes):
    return lax.all_to_all(block, axes, split_axis=0, concat_axis=0, tiled=True)


def shards(voltages, gains, shifts, widths):
    groups = lax.axis_size("beam")
    received = exchanged(calibrate(voltages, gains), "beam")
    table = jnp.transpose(gathered(shifts, "freq"), (1, 0, 2))
    early = (steering(groups), table, jnp.maximum(widths, 1))
    received, matrix, table, reach = lax.optimization_barrier((received, *early))
    detected = detect(received.reshape(2 * FEEDS, received.shape[2]), matrix)
    spread = exchanged(detected.reshape(FEEDS, -1, LANES), ("freq", "beam"))
    series = exchanged(tree(spread.reshape(detected.shape), table), "freq")
    return tuple(peaks(reach, series))


def solution(mesh):
    return jax.shard_map(
        shards,
        mesh=mesh,
        in_specs=(P(None, "beam", None, "freq"), P(None, "beam", "freq"), P(None, "freq"), P()),
        out_specs=(P("beam", None, "freq"), P(None, "beam", "freq")),
        check_vma=False,
    )
```

time: 85.1 us -> 80.5 us (0.946)
  the two profiles are of different devices: /device:TPU:24 before, /device:TPU:1 now
where the time goes in v1:
time: 80.5 us; the launch traced here: 80.1 us
  blocking collectives  31.7 us (39%)
  starting transfers between devices  18.4 us (23%)
  waiting for transfers between devices  13.3 us (17%)
  Pallas kernels  9.74 us (12%)
  other arithmetic  6.28 us (8%)
    all_to_all x2, blocking collectives, exchanged(): return lax.all_to_all(block, axes, split_axis=0, concat_axis=0, tiled=True)  31.7 us
    all_to_all x1, starting transfers between devices, exchanged(): return lax.all_to_all(block, axes, split_axis=0, concat_axis=0, tiled=True)  10.1 us
    ppermute x4, starting transfers between devices, gathered(): other = lax.ppermute(whole, axis, [(i, i ^ 1 << bit) for i in range(count)])  8.24 us
    all_to_all x1, waiting for transfers between devices, exchanged(): return lax.all_to_all(block, axes, split_axis=0, concat_axis=0, tiled=True)  7.63 us
    convert_element_type x1, other arithmetic, steering(): return value.astype(jnp.bfloat16)  6.04 us
    ppermute x4, waiting for transfers between devices, gathered(): other = lax.ppermute(whole, axis, [(i, i ^ 1 << bit) for i in range(count)])  5.63 us
    pallas_call x1, Pallas kernels, calibrate(): pl.pallas_call(calibrate_kernel, grid=(width // step,), in_specs=[pl.Bloc...  3.82 us
    pallas_call x1, Pallas kernels, tree(): pl.pallas_call(tree_kernel, out_shape=jax.ShapeDtypeStruct((blocks, TIME,...  2.22 us
  transfers between devices with their start and end apart: 5, of which 4 were waited for; matrix products, arithmetic and copies ran while one was open for 8% of the time, Pallas kernels for 0%

profile of v1, /device:TPU:1, one launch (start us, length us, event | category | flops | bytes accessed | tf_op | source)
XLA Modules:
  0.0 80.1 jit_solution(13380691164767933437)
XLA Ops:
  0.6 3.8 %calibrate.1 = bf16[16,32,1024]{2,1,0:T(8,128)(2,1)} custom-call(bf16[2,16,16,1024]{3,2,1,0:T(8,128)(2,1)} %volt_ref.1, f32[2,16,1024]{2,1,0:T(8,128)} %gain_ref.1), custom_call_target="tpu_custom_call" | custom-call | tf_op jit(solution)/shard_map/calibrate/pallas_call | solution.py:56
  4.4 0.0 copy-start
  4.4 10.1 %all-to-all-start = ((bf16[16,32,1024]{2,1,0:T(8,128)(2,1)}), bf16[16,32,1024]{2,1,0:T(8,128)(2,1)S(1)}, u32[]{:S(2)}, u32[]{:S(2)}) async-start(bf16[16,32,1024]{2,1,0:T(8,128)(2,1)} %calibrate.1), calls=%async_computation | async-start | bytes 2097152 | tf_op jit(solution)/shard_map/all_to_all | solution.py:243
  14.6 0.0 copy-done
  14.6 1.3 %collective-permute-start = (s32[1,12,256]{2,0,1:T(1,128)S(1)}, s32[1,12,256]{2,0,1:T(1,128)S(1)}, u32[]{:S(2)}, u32[]{:S(2)}) collective-permute-start(s32[1,12,256]{2,0,1:T(1,128)S(1)} %broadcast_in_dim.3), channel_id=1, source_target_pairs={{0,16},{16,0},{32,48},{48,32},{64,80},{80,64},{96,112},{112,96},{1... | collective-permute-start | bytes 36872 | tf_op jit(solution)/shard_map/ppermute | solution.py:236
  16.0 1.3 %collective-permute-done = s32[1,12,256]{2,0,1:T(1,128)S(1)} collective-permute-done((s32[1,12,256]{2,0,1:T(1,128)S(1)}, s32[1,12,256]{2,0,1:T(1,128)S(1)}, u32[]{:S(2)}, u32[]{:S(2)}) %collective-permute-start) | collective-permute-done | bytes 12320 | tf_op jit(solution)/shard_map/ppermute | solution.py:236
  17.3 2.8 %collective-permute-start.1 = (s32[2,12,256]{2,0,1:T(2,128)S(1)}, s32[2,12,256]{2,0,1:T(2,128)S(1)}, u32[]{:S(2)}, u32[]{:S(2)}) collective-permute-start(s32[2,12,256]{2,0,1:T(2,128)S(1)} %pad_add_fusion.2), channel_id=1, source_target_pairs={{0,32},{16,48},{32,0},{48,16},{64,96},{80,112},{96,64},{112,80},{1... | collective-permute-start | bytes 73736 | tf_op jit(solution)/shard_map/ppermute | solution.py:236
  20.1 1.7 %collective-permute-done.1 = s32[2,12,256]{2,0,1:T(2,128)S(1)} collective-permute-done((s32[2,12,256]{2,0,1:T(2,128)S(1)}, s32[2,12,256]{2,0,1:T(2,128)S(1)}, u32[]{:S(2)}, u32[]{:S(2)}) %collective-permute-start.1) | collective-permute-done | bytes 24608 | tf_op jit(solution)/shard_map/ppermute | solution.py:236
  21.9 1.4 %collective-permute-start.2 = (s32[4,12,256]{2,0,1:T(4,128)S(1)}, s32[4,12,256]{2,0,1:T(4,128)S(1)}, u32[]{:S(2)}, u32[]{:S(2)}) collective-permute-start(s32[4,12,256]{2,0,1:T(4,128)S(1)} %pad_add_fusion.1), channel_id=1, source_target_pairs={{0,64},{16,80},{32,96},{48,112},{64,0},{80,16},{96,32},{112,48},{1... | collective-permute-start | bytes 147464 | tf_op jit(solution)/shard_map/ppermute | solution.py:236
  23.3 6.0 %fusion.7.matrix_ref = bf16[512,512]{1,0:T(8,128)(2,1)S(1)} fusion(s32[512]{0:T(512)S(1)} %get-tuple-element.20, s32[512]{0:T(512)S(1)} %get-tuple-element.24, s32[512]{0:T(512)S(1)} %get-tuple-element.18, s32[512]{0:T(512)S(1)} %get-tuple-element.25, s32[512]{0:T(512)S(1)} %get-tuple-element.22, s32[512]{0:T(512)S(1)} %get-tuple-element.23, ...), kind=kLoop, calls=%fused_computation.25 | loop fusion | flops 15204352 | bytes 547328 | tf_op jit(solution)/shard_map/convert_element_type | solution.py:32
  29.4 0.0 collective-permute-done.2
  29.4 0.0 copy-start.1
  29.5 2.7 %collective-permute-start.3 = (s32[8,12,256]{2,0,1:T(8,128)S(1)}, s32[8,12,256]{2,0,1:T(8,128)S(1)}, u32[]{:S(2)}, u32[]{:S(2)}) collective-permute-start(s32[8,12,256]{2,0,1:T(8,128)S(1)} %pad_add_fusion), channel_id=1, source_target_pairs={{0,128},{16,144},{32,160},{48,176},{64,192},{80,208},{96,224},{112... | collective-permute-start | bytes 294920 | tf_op jit(solution)/shard_map/ppermute | solution.py:236
  32.2 0.0 copy-done.1
  32.2 2.6 %collective-permute-done.3 = s32[8,12,256]{2,0,1:T(8,128)S(1)} collective-permute-done((s32[8,12,256]{2,0,1:T(8,128)S(1)}, s32[8,12,256]{2,0,1:T(8,128)S(1)}, u32[]{:S(2)}, u32[]{:S(2)}) %collective-permute-start.3) | collective-permute-done | bytes 98336 | tf_op jit(solution)/shard_map/ppermute | solution.py:236
  34.9 7.6 %all-to-all-done = bf16[16,32,1024]{2,1,0:T(8,128)(2,1)S(1)} async-done(((bf16[16,32,1024]{2,1,0:T(8,128)(2,1)}), bf16[16,32,1024]{2,1,0:T(8,128)(2,1)S(1)}, u32[]{:S(2)}, u32[]{:S(2)}) %all-to-all-start) | async-done | bytes 1048608 | tf_op jit(solution)/shard_map/all_to_all | solution.py:243
  42.5 1.9 %detect.1 = bf16[512,128]{1,0:T(8,128)(2,1)S(1)} custom-call(bf16[512,512]{1,0:T(8,128)(2,1)S(1)} %fusion.7.matrix_ref, bf16[512,1024]{1,0:T(8,128)(2,1)S(1)} %bitcast.5), custom_call_target="tpu_custom_call" | custom-call | tf_op jit(solution)/shard_map/detect/pallas_call | solution.py:94
  44.4 21.9 %all_to_all.15 = bf16[256,2,128]{2,1,0:T(2,128)(2,1)S(1)} all-to-all(bf16[256,2,128]{2,1,0:T(2,128)(2,1)S(1)} %bitcast.7), channel_id=1, replica_groups=mesh['freq'=16,'beam'=16] {'freq','beam'}, dimensions={0} | all-to-all | bytes 262144 | tf_op jit(solution)/shard_map/all_to_all | solution.py:243
  66.3 2.2 %tree.1 = bf16[16,16,256]{2,1,0:T(8,128)(2,1)S(1)} custom-call(bf16[512,128]{1,0:T(8,128)(2,1)S(1)} %bitcast.6, s32[12,16,256]{2,1,0:T(8,128)S(1)} %add_bitcast_fusion.shifts_ref), custom_call_target="tpu_custom_call" | custom-call | tf_op jit(solution)/shard_map/tree/pallas_call | solution.py:179
  68.5 9.8 %all_to_all.16.series_ref = bf16[16,16,256]{2,1,0:T(8,128)(2,1)S(1)} all-to-all(bf16[16,16,256]{2,1,0:T(8,128)(2,1)S(1)} %tree.1), channel_id=1, replica_groups=mesh['freq'=16,'beam'=16] {'freq'}, dimensions={0} | all-to-all | bytes 262144 | tf_op jit(solution)/shard_map/all_to_all | solution.py:243
  78.3 1.8 %peaks.1 = (bf16[16,16,256]{2,1,0:T(8,128)(2,1)}, f32[8,16,256]{2,1,0:T(8,128)}) custom-call(s32[8]{0:T(128)S(1)} %broadcast_maximum_fusion.widths_ref, bf16[16,16,256]{2,1,0:T(8,128)(2,1)S(1)} %all_to_all.16.series_ref), custom_call_target="tpu_custom_call" | custom-call | tf_op jit(solution)/shard_map/peaks/pallas_call | solution.py:215
  (18 shorter events, 0.3 us)
Async XLA Ops:
  4.4 10.1 %copy-start = (s32[12,256]{1,0:T(8,128)S(1)}, s32[12,256]{1,0:T(8,128)}, u32[]{:S(2)}) copy-start(s32[12,256]{1,0:T(8,128)} %param.6) | copy-start | bytes 36868
  4.4 38.0 %all-to-all-start = ((bf16[16,32,1024]{2,1,0:T(8,128)(2,1)}), bf16[16,32,1024]{2,1,0:T(8,128)(2,1)S(1)}, u32[]{:S(2)}, u32[]{:S(2)}) async-start(bf16[16,32,1024]{2,1,0:T(8,128)(2,1)} %calibrate.1), calls=%async_computation | async-start | bytes 2097152 | tf_op jit(solution)/shard_map/all_to_all | solution.py:243
  14.6 2.7 %collective-permute-start = (s32[1,12,256]{2,0,1:T(1,128)S(1)}, s32[1,12,256]{2,0,1:T(1,128)S(1)}, u32[]{:S(2)}, u32[]{:S(2)}) collective-permute-start(s32[1,12,256]{2,0,1:T(1,128)S(1)} %broadcast_in_dim.3), channel_id=1, source_target_pairs={{0,16},{16,0},{32,48},{48,32},{64,80},{80,64},{96,112},{112,96},{1... | collective-permute-start | bytes 36872 | tf_op jit(solution)/shard_map/ppermute | solution.py:236
  17.3 4.6 %collective-permute-start.1 = (s32[2,12,256]{2,0,1:T(2,128)S(1)}, s32[2,12,256]{2,0,1:T(2,128)S(1)}, u32[]{:S(2)}, u32[]{:S(2)}) collective-permute-start(s32[2,12,256]{2,0,1:T(2,128)S(1)} %pad_add_fusion.2), channel_id=1, source_target_pairs={{0,32},{16,48},{32,0},{48,16},{64,96},{80,112},{96,64},{112,80},{1... | collective-permute-start | bytes 73736 | tf_op jit(solution)/shard_map/ppermute | solution.py:236
  21.9 7.4 %collective-permute-start.2 = (s32[4,12,256]{2,0,1:T(4,128)S(1)}, s32[4,12,256]{2,0,1:T(4,128)S(1)}, u32[]{:S(2)}, u32[]{:S(2)}) collective-permute-start(s32[4,12,256]{2,0,1:T(4,128)S(1)} %pad_add_fusion.1), channel_id=1, source_target_pairs={{0,64},{16,80},{32,96},{48,112},{64,0},{80,16},{96,32},{112,48},{1... | collective-permute-start | bytes 147464 | tf_op jit(solution)/shard_map/ppermute | solution.py:236
  29.4 2.8 %copy-start.1 = (s32[8]{0:T(128)S(1)}, s32[8]{0:T(128)}, u32[]{:S(2)}) copy-start(s32[8]{0:T(128)} %param.7) | copy-start | bytes 100
  29.5 5.4 %collective-permute-start.3 = (s32[8,12,256]{2,0,1:T(8,128)S(1)}, s32[8,12,256]{2,0,1:T(8,128)S(1)}, u32[]{:S(2)}, u32[]{:S(2)}) collective-permute-start(s32[8,12,256]{2,0,1:T(8,128)S(1)} %pad_add_fusion), channel_id=1, source_target_pairs={{0,128},{16,144},{32,160},{48,176},{64,192},{80,208},{96,224},{112... | collective-permute-start | bytes 294920 | tf_op jit(solution)/shard_map/ppermute | solution.py:236

commit v2 on v1

--- a/solution.py
+++ b/solution.py
@@ -13,6 +13,7 @@
 NSUB = 4096
 TIME = 16
 LANES = 128
+CORES = 2
 MIB = 1024 * 1024
 
 
@@ -32,65 +33,94 @@
     return value.astype(jnp.bfloat16)
 
 
-def calibrate_kernel(volt_ref, gain_ref, out_ref, scratch):
-    feeds, samples, width = volt_ref.shape[1:]
-    for j in range(width // LANES):
-        lanes = slice(j * LANES, (j + 1) * LANES)
+def calibrate_kernel(core_ref, volt_hbm, gain_hbm, *rest, other):
+    out_hbm, volt, gain, wide, done, in_sems, out_sems = rest[-7:]
+    chunks, _, feeds, samples, _ = volt.shape
+    core = core_ref[0]
+    slot = 1 - core if other else core
+
+    def arriving(j):
+        lanes = pl.ds(pl.multiple_of((core * chunks + j) * LANES, LANES), LANES)
+        return (
+            pltpu.make_async_copy(volt_hbm.at[:, :, :, lanes], volt.at[j], in_sems.at[0, j]),
+            pltpu.make_async_copy(gain_hbm.at[:, :, lanes], gain.at[j], in_sems.at[1, j]),
+        )
+
+    def leaving(j):
+        there = out_hbm.at[:, slot, :, pl.ds(j * LANES, LANES)]
+        return pltpu.make_async_copy(done.at[j], there, out_sems.at[j])
+
+    for j in range(chunks):
+        for copy in arriving(j):
+            copy.start()
+    for j in range(chunks):
+        for copy in arriving(j):
+            copy.wait()
         for part in range(2):
-            block = volt_ref[part, :, :, lanes].astype(jnp.float32)
-            scratch[part, j] = block.reshape(feeds * samples, LANES)
-        gain_re = gain_ref[0, :, lanes]
-        gain_im = gain_ref[1, :, lanes]
+            wide[j, part] = volt[j, part].astype(jnp.float32).reshape(feeds * samples, LANES)
+        gain_re = gain[j, 0]
+        gain_im = gain[j, 1]
         for t in range(samples):
-            volt_re = scratch[0, j, pl.ds(t, feeds, stride=samples), :]
-            volt_im = scratch[1, j, pl.ds(t, feeds, stride=samples), :]
+            volt_re = wide[j, 0, pl.ds(t, feeds, stride=samples), :]
+            volt_im = wide[j, 1, pl.ds(t, feeds, stride=samples), :]
             real = gain_re * volt_re - gain_im * volt_im
             imag = gain_re * volt_im + gain_im * volt_re
-            out_ref[t, :feeds, lanes] = real.astype(jnp.bfloat16)
-            out_ref[t, feeds:, lanes] = imag.astype(jnp.bfloat16)
-
-
-def calibrate(voltages, gains):
+            done[j, t, :feeds] = real.astype(jnp.bfloat16)
+            done[j, t, feeds:] = imag.astype(jnp.bfloat16)
+        leaving(j).start()
+    for j in range(chunks):
+        leaving(j).wait()
+
+
+def calibrate(core, voltages, gains, begun=None):
     _, feeds, samples, width = voltages.shape
+    chunks = width // CORES // LANES
+    shape = (samples, CORES, 2 * feeds, width // CORES)
+    other = begun is not None
+    operands = (core, voltages, gains) + ((begun,) if other else ())
+    return pl.pallas_call(
+        functools.partial(calibrate_kernel, other=other),
+        in_specs=[pl.BlockSpec(memory_space=pltpu.SMEM)]
+        + [pl.BlockSpec(memory_space=pl.ANY if other else pltpu.HBM)] * 2
+        + [pl.BlockSpec(memory_space=pltpu.HBM)] * other,
+        out_specs=pl.BlockSpec(memory_space=pltpu.HBM),
+        out_shape=jax.ShapeDtypeStruct(shape, jnp.bfloat16),
+        scratch_shapes=[
+            pltpu.VMEM((chunks, 2, feeds, samples, LANES), jnp.bfloat16),
+            pltpu.VMEM((chunks, 2, feeds, LANES), jnp.float32),
+            pltpu.VMEM((chunks, 2, feeds * samples, LANES), jnp.float32),
+            pltpu.VMEM((chunks, samples, 2 * feeds, LANES), jnp.bfloat16),
+            pltpu.SemaphoreType.DMA((2, chunks)),
+            pltpu.SemaphoreType.DMA((chunks,)),
+        ],
+        input_output_aliases={3: 0} if other else {},
+        compiler_params=pltpu.CompilerParams(vmem_limit_bytes=(8 if other else 60) * MIB),
+        name="calibrate",
+    )(*operands)
+
+
+def detect_kernel(matrix_ref, x_ref, out_ref, scratch):
+    _, pair, _, _, width = x_ref.shape
     step = 256
-    return pl.pallas_call(
-        calibrate_kernel,
-        grid=(width // step,),
-        in_specs=[
-            pl.BlockSpec((2, feeds, samples, step), lambda i: (0, 0, 0, i)),
-            pl.BlockSpec((2, feeds, step), lambda i: (0, 0, i)),
-        ],
-        out_specs=pl.BlockSpec((samples, 2 * feeds, step), lambda i: (0, 0, i)),
-        out_shape=jax.ShapeDtypeStruct((samples, 2 * feeds, width), jnp.bfloat16),
-        scratch_shapes=[pltpu.VMEM((2, step // LANES, feeds * samples, LANES), jnp.float32)],
-        compiler_params=pltpu.CompilerParams(vmem_limit_bytes=60 * MIB),
-        name="calibrate",
-    )(voltages, gains)
-
-
-def detect_kernel(matrix_ref, x_ref, out_ref, scratch):
-    width = x_ref.shape[1]
-    step = 256
-    total = jnp.zeros((FEEDS, width // CHAN_SUM), jnp.float32)
     channel = lax.broadcasted_iota(jnp.int32, (step, width // CHAN_SUM), 0)
     group = lax.broadcasted_iota(jnp.int32, (step, width // CHAN_SUM), 1)
-    for j in range(width // step):
-        cols = slice(j * step, (j + 1) * step)
-        formed = jnp.dot(matrix_ref[...], x_ref[:, cols], preferred_element_type=jnp.float32)
-        power = formed[:FEEDS] * formed[:FEEDS] + formed[FEEDS:] * formed[FEEDS:]
-        high = power.astype(jnp.bfloat16)
-        low = (power - high.astype(jnp.float32)).astype(jnp.bfloat16)
-        pooling = ((channel + j * step) // CHAN_SUM == group).astype(jnp.bfloat16)
-        total += jnp.dot(high, pooling, preferred_element_type=jnp.float32)
-        total += jnp.dot(low, pooling, preferred_element_type=jnp.float32)
-    pieces = width // CHAN_SUM // LANES
-    for h in range(pieces):
-        scratch[pl.ds(h, FEEDS, stride=pieces), :] = total[:, h * LANES : (h + 1) * LANES]
+    for t in range(pair):
+        total = jnp.zeros((FEEDS, width // CHAN_SUM), jnp.float32)
+        for j in range(width // step):
+            x = x_ref[:, t, :, :, j * step : (j + 1) * step].reshape(2 * FEEDS, step)
+            formed = jnp.dot(matrix_ref[...], x, preferred_element_type=jnp.float32)
+            power = formed[:FEEDS] * formed[:FEEDS] + formed[FEEDS:] * formed[FEEDS:]
+            high = power.astype(jnp.bfloat16)
+            low = (power - high.astype(jnp.float32)).astype(jnp.bfloat16)
+            pooling = ((channel + j * step) // CHAN_SUM == group).astype(jnp.bfloat16)
+            total += jnp.dot(high, pooling, preferred_element_type=jnp.float32)
+            total += jnp.dot(low, pooling, preferred_element_type=jnp.float32)
+        scratch[pl.ds(t, FEEDS, stride=pair), :] = total
     out_ref[...] = scratch[...].astype(jnp.bfloat16)
 
 
 def detect(received, matrix):
-    shape = (FEEDS * received.shape[1] // CHAN_SUM // LANES, LANES)
+    shape = (FEEDS * received.shape[1], received.shape[4] // CHAN_SUM)
     return pl.pallas_call(
         detect_kernel,
         out_shape=jax.ShapeDtypeStruct(shape, jnp.bfloat16),
@@ -140,7 +170,7 @@
         for piece in range(pieces):
             rows = []
             for t in range(samples):
-                first = group * 8 * samples * pieces + t * pieces + piece
+                first = (group * 8 * samples + t // 2 * 2 + piece) * pieces + t % 2
                 rows.append(wide[pl.ds(first, 8, stride=samples * pieces), :])
             mean = functools.reduce(jnp.add, rows) * (1.0 / samples)
             rows = [row - mean for row in rows]
@@ -232,24 +262,37 @@
     count = lax.axis_size(axis)
     position = lax.axis_index(axis)
     whole = block[None]
-    for bit in range(count.bit_length() - 1):
-        other = lax.ppermute(whole, axis, [(i, i ^ 1 << bit) for i in range(count)])
-        upper = (position >> bit & 1) == 1
-        whole = jnp.concatenate([jnp.where(upper, other, whole), jnp.where(upper, whole, other)])
+    step = 1
+    while step < count:
+        parts = [whole]
+        for k in range(1, 4):
+            parts.append(lax.ppermute(whole, axis, [(i, i ^ k * step) for i in range(count)]))
+        for bit in (1, 2):
+            odd = position & bit * step != 0
+            parts = [jnp.where(odd, parts[k ^ bit], parts[k]) for k in range(4)]
+        whole = jnp.concatenate(parts)
+        step *= 4
     return whole
 
 
-def exchanged(block, axes):
-    return lax.all_to_all(block, axes, split_axis=0, concat_axis=0, tiled=True)
+def exchanged(block, axes, groups=None):
+    return lax.all_to_all(block, axes, split_axis=0, concat_axis=0, axis_index_groups=groups, tiled=True)
 
 
 def shards(voltages, gains, shifts, widths):
     groups = lax.axis_size("beam")
-    received = exchanged(calibrate(voltages, gains), "beam")
+    core = (lax.axis_index("beam") & CORES - 1).astype(jnp.int32).reshape(1)
+    swap = [(i, i ^ 1) for i in range(groups)]
+    other = [lax.ppermute(block, "beam", swap) for block in (voltages, gains)]
+    calibrated = calibrate(core, *other, calibrate(core, voltages, gains))
+    calibrated, shifts = lax.optimization_barrier((calibrated, shifts))
+    same_core = [list(range(c, groups, CORES)) for c in range(CORES)]
+    received = exchanged(calibrated, "beam", same_core)
+    received = received.reshape((groups // CORES, CORES) + calibrated.shape[1:])
     table = jnp.transpose(gathered(shifts, "freq"), (1, 0, 2))
     early = (steering(groups), table, jnp.maximum(widths, 1))
     received, matrix, table, reach = lax.optimization_barrier((received, *early))
-    detected = detect(received.reshape(2 * FEEDS, received.shape[2]), matrix)
+    detected = detect(received, matrix)
     spread = exchanged(detected.reshape(FEEDS, -1, LANES), ("freq", "beam"))
     series = exchanged(tree(spread.reshape(detected.shape), table), "freq")
     return tuple(peaks(reach, series))

time: 80.5 us -> 82.2 us (1.021)
  waiting for transfers between devices: 13.3 us -> 16.4 us
  local copies, waits for them, and re-layouts: 0.02 us -> 2.24 us
  starting transfers between devices: 18.4 us -> 16.9 us
  blocking collectives: 31.7 us -> 30.5 us
  Pallas kernels: 9.74 us -> 8.69 us
    all_to_all x1, waiting for transfers between devices: 7.63 us -> 11.9 us  [exchanged(): lax.all_to_all(block, axes, split_axis=0, concat_axis=0, axis_index_group...]
    all_to_all x1, starting transfers between devices: 10.1 us -> 6.58 us  [exchanged(): lax.all_to_all(block, axes, split_axis=0, concat_axis=0, axis_index_group...]
    unnamed x4 -> x8, local copies, waits for them, and re-layouts: 0.01 us -> 2.23 us
    ppermute x4 -> x8, starting transfers between devices: 8.24 us -> 10.3 us  [the longest x6 6.84 us: gathered(): lax.ppermute(whole, axis, [(i, i ^ k * step) for i in range(count)])]
    all_to_all x2, blocking collectives: 31.7 us -> 30.5 us  [exchanged(): lax.all_to_all(block, axes, split_axis=0, concat_axis=0, axis_index_group...]
    ppermute x4 -> x8, waiting for transfers between devices: 5.63 us -> 4.48 us  [the longest x6 4.07 us: gathered(): lax.ppermute(whole, axis, [(i, i ^ k * step) for i in range(count)])]
    pallas_call x1 -> x2, Pallas kernels: 3.82 us -> 2.84 us  [calibrate(): pl.pallas_call(functools.partial(calibrate_kernel, other=other), in_specs...]
  transfers between devices with their start and end apart: 5 -> 9, of which waited for: 4 -> 4; matrix products, arithmetic and copies ran while one was open for 8% -> 8% of each run, Pallas kernels for 0% -> 3%
where the time goes in v2:
time: 82.2 us; the launch traced here: 81.8 us
  blocking collectives  30.5 us (37%)
  starting transfers between devices  16.9 us (21%)
  waiting for transfers between devices  16.4 us (20%)
  Pallas kernels  8.69 us (11%)
  other arithmetic  6.37 us (8%)
  local copies, waits for them, and re-layouts  2.24 us (3%)
    all_to_all x2, blocking collectives, exchanged(): lax.all_to_all(block, axes, split_axis=0, concat_axis=0, axis_index_group...  30.5 us
    all_to_all x1, waiting for transfers between devices, exchanged(): lax.all_to_all(block, axes, split_axis=0, concat_axis=0, axis_index_group...  11.9 us
    ppermute x6, starting transfers between devices, gathered(): lax.ppermute(whole, axis, [(i, i ^ k * step) for i in range(count)])  6.84 us
    all_to_all x1, starting transfers between devices, exchanged(): lax.all_to_all(block, axes, split_axis=0, concat_axis=0, axis_index_group...  6.58 us
    convert_element_type x1, other arithmetic, steering(): return value.astype(jnp.bfloat16)  6.04 us
    ppermute x6, waiting for transfers between devices, gathered(): lax.ppermute(whole, axis, [(i, i ^ k * step) for i in range(count)])  4.07 us
    ppermute x2, starting transfers between devices, shards(): other = [lax.ppermute(block, 'beam', swap) for block in (voltages, gains)]  3.43 us
    pallas_call x2, Pallas kernels, calibrate(): pl.pallas_call(functools.partial(calibrate_kernel, other=other), in_specs...  2.84 us
  transfers between devices with their start and end apart: 9, of which 4 were waited for; matrix products, arithmetic and copies ran while one was open for 8% of the time, Pallas kernels for 3%

profile of v2, /device:TPU:1, one launch (start us, length us, event | category | flops | bytes accessed | tf_op | source)
XLA Modules:
  0.0 81.8 jit_solution(14334308987577261663)
XLA Ops:
  0.6 3.3 %collective-permute-start = (bf16[2,16,16,1024]{3,2,1,0:T(8,128)(2,1)}, bf16[2,16,16,1024]{3,2,1,0:T(8,128)(2,1)S(1)}, u32[]{:S(2)}, u32[]{:S(2)}) collective-permute-start(bf16[2,16,16,1024]{3,2,1,0:T(8,128)(2,1)} %volt_hbm.1), channel_id=1, source_target_pairs={{0,1},{1,0},{2,3},{3,2},{4,5},{5,4},{6,7},{7,6},{8,9},{9,8},{10,11... | collective-permute-start | bytes 3145736 | tf_op jit(solution)/shard_map/ppermute | solution.py:286
  4.0 0.1 collective-permute-start.1
  4.1 2.1 %calibrate.2.rest_0_ = bf16[16,2,32,512]{3,2,1,0:T(8,128)(2,1)} custom-call(s32[1]{0:T(128)} %bitcast.core_ref, bf16[2,16,16,1024]{3,2,1,0:T(8,128)(2,1)} %volt_hbm.1, f32[2,16,1024]{2,1,0:T(8,128)} %gain_hbm.1), custom_call_target="tpu_custom_call" | custom-call | tf_op jit(solution)/shard_map/calibrate/pallas_call | solution.py:81
  6.2 0.4 collective-permute-done.1.gain_hbm
  6.6 1.2 %copy-done = bf16[16,2,32,512]{3,2,1,0:T(8,128)(2,1)S(1)} copy-done((bf16[16,2,32,512]{3,2,1,0:T(8,128)(2,1)S(1)}, bf16[16,2,32,512]{3,2,1,0:T(8,128)(2,1)}, u32[]{:S(2)}) %copy-start) | copy-done | bytes 1048600
  7.9 0.8 calibrate.3
  8.6 1.0 %copy-done.1 = bf16[16,2,32,512]{3,2,1,0:T(8,128)(2,1)} copy-done((bf16[16,2,32,512]{3,2,1,0:T(8,128)(2,1)}, bf16[16,2,32,512]{3,2,1,0:T(8,128)(2,1)S(1)}, u32[]{:S(2)}) %copy-start.1) | copy-done | bytes 1048600
  9.6 6.6 %all-to-all-start = ((bf16[16,2,32,512]{3,2,1,0:T(8,128)(2,1)}), bf16[16,2,32,512]{3,2,1,0:T(8,128)(2,1)S(1)}, u32[]{:S(2)}, u32[]{:S(2)}) async-start(bf16[16,2,32,512]{3,2,1,0:T(8,128)(2,1)} %copy-done.1), calls=%async_computation | async-start | bytes 2097152 | tf_op jit(solution)/shard_map/all_to_all | solution.py:279
  16.3 2.6 %collective-permute-start.2 = (s32[1,12,256]{2,0,1:T(1,128)S(1)}, s32[1,12,256]{2,0,1:T(1,128)S(1)}, u32[]{:S(2)}, u32[]{:S(2)}) collective-permute-start(s32[1,12,256]{2,0,1:T(1,128)S(1)} %broadcast_in_dim.3), channel_id=1, source_target_pairs={{0,48},{16,32},{32,16},{48,0},{64,112},{80,96},{96,80},{112,64},{1... | collective-permute-start | bytes 36872 | tf_op jit(solution)/shard_map/ppermute | solution.py:269
  18.8 0.5 collective-permute-start.3
  19.3 0.3 collective-permute-start.4
  19.6 6.0 %fusion.7.matrix_ref = bf16[512,512]{1,0:T(8,128)(2,1)S(1)} fusion(s32[512]{0:T(512)S(1)} %get-tuple-element.23, s32[512]{0:T(512)S(1)} %get-tuple-element.27, s32[512]{0:T(512)S(1)} %get-tuple-element.21, s32[512]{0:T(512)S(1)} %get-tuple-element.28, s32[512]{0:T(512)S(1)} %get-tuple-element.25, s32[512]{0:T(512)S(1)} %get-tuple-element.26, ...), kind=kLoop, calls=%fused_computation.25 | loop fusion | flops 15204352 | bytes 547328 | tf_op jit(solution)/shard_map/convert_element_type | solution.py:33
  25.8 2.8 %collective-permute-start.5 = (s32[4,12,256]{2,0,1:T(4,128)S(1)}, s32[4,12,256]{2,0,1:T(4,128)S(1)}, u32[]{:S(2)}, u32[]{:S(2)}) collective-permute-start(s32[4,12,256]{2,0,1:T(4,128)S(1)} %pad_add_fusion), channel_id=1, source_target_pairs={{0,192},{16,208},{32,224},{48,240},{64,128},{80,144},{96,160},{112... | collective-permute-start | bytes 147464 | tf_op jit(solution)/shard_map/ppermute | solution.py:269
  28.6 0.3 collective-permute-start.6
  29.0 0.3 collective-permute-start.7
  29.3 1.1 %collective-permute-done.5 = s32[4,12,256]{2,0,1:T(4,128)S(1)} collective-permute-done((s32[4,12,256]{2,0,1:T(4,128)S(1)}, s32[4,12,256]{2,0,1:T(4,128)S(1)}, u32[]{:S(2)}, u32[]{:S(2)}) %collective-permute-start.5) | collective-permute-done | bytes 49184 | tf_op jit(solution)/shard_map/ppermute | solution.py:269
  30.4 3.0 %collective-permute-done.6 = s32[4,12,256]{2,0,1:T(4,128)S(1)} collective-permute-done((s32[4,12,256]{2,0,1:T(4,128)S(1)}, s32[4,12,256]{2,0,1:T(4,128)S(1)}, u32[]{:S(2)}, u32[]{:S(2)}) %collective-permute-start.6) | collective-permute-done | bytes 49184 | tf_op jit(solution)/shard_map/ppermute | solution.py:269
  33.4 0.1 broadcast_select_fusion.15
  33.6 11.9 %all-to-all-done = bf16[16,2,32,512]{3,2,1,0:T(8,128)(2,1)S(1)} async-done(((bf16[16,2,32,512]{3,2,1,0:T(8,128)(2,1)}), bf16[16,2,32,512]{3,2,1,0:T(8,128)(2,1)S(1)}, u32[]{:S(2)}, u32[]{:S(2)}) %all-to-all-start) | async-done | bytes 1048608 | tf_op jit(solution)/shard_map/all_to_all | solution.py:279
  45.5 1.8 %detect.1 = bf16[512,128]{1,0:T(8,128)(2,1)S(1)} custom-call(bf16[512,512]{1,0:T(8,128)(2,1)S(1)} %fusion.7.matrix_ref, bf16[8,2,2,32,512]{4,3,2,1,0:T(8,128)(2,1)S(1)} %bitcast.6), custom_call_target="tpu_custom_call" | custom-call | tf_op jit(solution)/shard_map/detect/pallas_call | solution.py:124
  47.3 20.7 %all_to_all.15 = bf16[256,2,128]{2,1,0:T(2,128)(2,1)S(1)} all-to-all(bf16[256,2,128]{2,1,0:T(2,128)(2,1)S(1)} %bitcast.8), channel_id=1, replica_groups=mesh['freq'=16,'beam'=16] {'freq','beam'}, dimensions={0} | all-to-all | bytes 262144 | tf_op jit(solution)/shard_map/all_to_all | solution.py:279
  68.0 2.2 %tree.1 = bf16[16,16,256]{2,1,0:T(8,128)(2,1)S(1)} custom-call(bf16[512,128]{1,0:T(8,128)(2,1)S(1)} %bitcast.7, s32[12,16,256]{2,1,0:T(8,128)S(1)} %add_bitcast_fusion.shifts_ref), custom_call_target="tpu_custom_call" | custom-call | tf_op jit(solution)/shard_map/tree/pallas_call | solution.py:209
  70.2 9.8 %all_to_all.16.series_ref = bf16[16,16,256]{2,1,0:T(8,128)(2,1)S(1)} all-to-all(bf16[16,16,256]{2,1,0:T(8,128)(2,1)S(1)} %tree.1), channel_id=1, replica_groups=mesh['freq'=16,'beam'=16] {'freq'}, dimensions={0} | all-to-all | bytes 262144 | tf_op jit(solution)/shard_map/all_to_all | solution.py:279
  80.1 1.8 %peaks.1 = (bf16[16,16,256]{2,1,0:T(8,128)(2,1)}, f32[8,16,256]{2,1,0:T(8,128)}) custom-call(s32[8]{0:T(128)S(1)} %broadcast_maximum_fusion.widths_ref, bf16[16,16,256]{2,1,0:T(8,128)(2,1)S(1)} %all_to_all.16.series_ref), custom_call_target="tpu_custom_call" | custom-call | tf_op jit(solution)/shard_map/peaks/pallas_call | solution.py:245
  (25 shorter events, 0.3 us)
Async XLA Ops:
  0.6 6.0 %collective-permute-start = (bf16[2,16,16,1024]{3,2,1,0:T(8,128)(2,1)}, bf16[2,16,16,1024]{3,2,1,0:T(8,128)(2,1)S(1)}, u32[]{:S(2)}, u32[]{:S(2)}) collective-permute-start(bf16[2,16,16,1024]{3,2,1,0:T(8,128)(2,1)} %volt_hbm.1), channel_id=1, source_target_pairs={{0,1},{1,0},{2,3},{3,2},{4,5},{5,4},{6,7},{7,6},{8,9},{9,8},{10,11... | collective-permute-start | bytes 3145736 | tf_op jit(solution)/shard_map/ppermute | solution.py:286
  4.0 2.7 %collective-permute-start.1 = (f32[2,16,1024]{2,1,0:T(8,128)}, f32[2,16,1024]{2,1,0:T(8,128)S(1)}, u32[]{:S(2)}, u32[]{:S(2)}) collective-permute-start(f32[2,16,1024]{2,1,0:T(8,128)} %gain_hbm.1), channel_id=1, source_target_pairs={{0,1},{1,0},{2,3},{3,2},{4,5},{5,4},{6,7},{7,6},{8,9},{9,8},{10,11... | collective-permute-start | bytes 393224 | tf_op jit(solution)/shard_map/ppermute | solution.py:286
  6.6 1.2 %copy-start = (bf16[16,2,32,512]{3,2,1,0:T(8,128)(2,1)S(1)}, bf16[16,2,32,512]{3,2,1,0:T(8,128)(2,1)}, u32[]{:S(2)}) copy-start(bf16[16,2,32,512]{3,2,1,0:T(8,128)(2,1)} %calibrate.2.rest_0_) | copy-start | bytes 3145732
  8.6 1.0 %copy-start.1 = (bf16[16,2,32,512]{3,2,1,0:T(8,128)(2,1)}, bf16[16,2,32,512]{3,2,1,0:T(8,128)(2,1)S(1)}, u32[]{:S(2)}) copy-start(bf16[16,2,32,512]{3,2,1,0:T(8,128)(2,1)S(1)} %calibrate.3) | copy-start | bytes 3145732
  9.6 6.6 %copy-start.2 = (s32[12,256]{1,0:T(8,128)S(1)}, s32[12,256]{1,0:T(8,128)}, u32[]{:S(2)}) copy-start(s32[12,256]{1,0:T(8,128)} %param.6) | copy-start | bytes 36868
  9.6 35.8 %all-to-all-start = ((bf16[16,2,32,512]{3,2,1,0:T(8,128)(2,1)}), bf16[16,2,32,512]{3,2,1,0:T(8,128)(2,1)S(1)}, u32[]{:S(2)}, u32[]{:S(2)}) async-start(bf16[16,2,32,512]{3,2,1,0:T(8,128)(2,1)} %copy-done.1), calls=%async_computation | async-start | bytes 2097152 | tf_op jit(solution)/shard_map/all_to_all | solution.py:279
  16.3 9.4 %collective-permute-start.2 = (s32[1,12,256]{2,0,1:T(1,128)S(1)}, s32[1,12,256]{2,0,1:T(1,128)S(1)}, u32[]{:S(2)}, u32[]{:S(2)}) collective-permute-start(s32[1,12,256]{2,0,1:T(1,128)S(1)} %broadcast_in_dim.3), channel_id=1, source_target_pairs={{0,48},{16,32},{32,16},{48,0},{64,112},{80,96},{96,80},{112,64},{1... | collective-permute-start | bytes 36872 | tf_op jit(solution)/shard_map/ppermute | solution.py:269
  18.8 6.8 %collective-permute-start.3 = (s32[1,12,256]{2,0,1:T(1,128)S(1)}, s32[1,12,256]{2,0,1:T(1,128)S(1)}, u32[]{:S(2)}, u32[]{:S(2)}) collective-permute-start(s32[1,12,256]{2,0,1:T(1,128)S(1)} %broadcast_in_dim.3), channel_id=1, source_target_pairs={{0,32},{16,48},{32,0},{48,16},{64,96},{80,112},{96,64},{112,80},{1... | collective-permute-start | bytes 36872 | tf_op jit(solution)/shard_map/ppermute | solution.py:269
  19.3 6.3 %collective-permute-start.4 = (s32[1,12,256]{2,0,1:T(1,128)S(1)}, s32[1,12,256]{2,0,1:T(1,128)S(1)}, u32[]{:S(2)}, u32[]{:S(2)}) collective-permute-start(s32[1,12,256]{2,0,1:T(1,128)S(1)} %broadcast_in_dim.3), channel_id=1, source_target_pairs={{0,16},{16,0},{32,48},{48,32},{64,80},{80,64},{96,112},{112,96},{1... | collective-permute-start | bytes 36872 | tf_op jit(solution)/shard_map/ppermute | solution.py:269
  25.7 3.6 %copy-start.3 = (s32[8]{0:T(128)S(1)}, s32[8]{0:T(128)}, u32[]{:S(2)}) copy-start(s32[8]{0:T(128)} %param.7) | copy-start | bytes 100
  25.8 4.6 %collective-permute-start.5 = (s32[4,12,256]{2,0,1:T(4,128)S(1)}, s32[4,12,256]{2,0,1:T(4,128)S(1)}, u32[]{:S(2)}, u32[]{:S(2)}) collective-permute-start(s32[4,12,256]{2,0,1:T(4,128)S(1)} %pad_add_fusion), channel_id=1, source_target_pairs={{0,192},{16,208},{32,224},{48,240},{64,128},{80,144},{96,160},{112... | collective-permute-start | bytes 147464 | tf_op jit(solution)/shard_map/ppermute | solution.py:269
  28.6 4.7 %collective-permute-start.6 = (s32[4,12,256]{2,0,1:T(4,128)S(1)}, s32[4,12,256]{2,0,1:T(4,128)S(1)}, u32[]{:S(2)}, u32[]{:S(2)}) collective-permute-start(s32[4,12,256]{2,0,1:T(4,128)S(1)} %pad_add_fusion), channel_id=1, source_target_pairs={{0,128},{16,144},{32,160},{48,176},{64,192},{80,208},{96,224},{112... | collective-permute-start | bytes 147464 | tf_op jit(solution)/shard_map/ppermute | solution.py:269
  29.0 4.4 %collective-permute-start.7 = (s32[4,12,256]{2,0,1:T(4,128)S(1)}, s32[4,12,256]{2,0,1:T(4,128)S(1)}, u32[]{:S(2)}, u32[]{:S(2)}) collective-permute-start(s32[4,12,256]{2,0,1:T(4,128)S(1)} %pad_add_fusion), channel_id=1, source_target_pairs={{0,64},{16,80},{32,96},{48,112},{64,0},{80,16},{96,32},{112,48},{1... | collective-permute-start | bytes 147464 | tf_op jit(solution)/shard_map/ppermute | solution.py:269

commit v3 on v2

--- a/solution.py
+++ b/solution.py
@@ -13,7 +13,6 @@
 NSUB = 4096
 TIME = 16
 LANES = 128
-CORES = 2
 MIB = 1024 * 1024
 
 
@@ -33,22 +32,18 @@
     return value.astype(jnp.bfloat16)
 
 
-def calibrate_kernel(core_ref, volt_hbm, gain_hbm, *rest, other):
-    out_hbm, volt, gain, wide, done, in_sems, out_sems = rest[-7:]
+def calibrate_kernel(volt_hbm, gain_hbm, out_hbm, volt, gain, wide, done, in_sems, out_sems):
     chunks, _, feeds, samples, _ = volt.shape
-    core = core_ref[0]
-    slot = 1 - core if other else core
 
     def arriving(j):
-        lanes = pl.ds(pl.multiple_of((core * chunks + j) * LANES, LANES), LANES)
+        lanes = pl.ds(j * LANES, LANES)
         return (
             pltpu.make_async_copy(volt_hbm.at[:, :, :, lanes], volt.at[j], in_sems.at[0, j]),
             pltpu.make_async_copy(gain_hbm.at[:, :, lanes], gain.at[j], in_sems.at[1, j]),
         )
 
     def leaving(j):
-        there = out_hbm.at[:, slot, :, pl.ds(j * LANES, LANES)]
-        return pltpu.make_async_copy(done.at[j], there, out_sems.at[j])
+        return pltpu.make_async_copy(done.at[j], out_hbm.at[:, :, pl.ds(j * LANES, LANES)], out_sems.at[j])
 
     for j in range(chunks):
         for copy in arriving(j):
@@ -72,19 +67,14 @@
         leaving(j).wait()
 
 
-def calibrate(core, voltages, gains, begun=None):
+def calibrate(voltages, gains):
     _, feeds, samples, width = voltages.shape
-    chunks = width // CORES // LANES
-    shape = (samples, CORES, 2 * feeds, width // CORES)
-    other = begun is not None
-    operands = (core, voltages, gains) + ((begun,) if other else ())
+    chunks = width // LANES
     return pl.pallas_call(
-        functools.partial(calibrate_kernel, other=other),
-        in_specs=[pl.BlockSpec(memory_space=pltpu.SMEM)]
-        + [pl.BlockSpec(memory_space=pl.ANY if other else pltpu.HBM)] * 2
-        + [pl.BlockSpec(memory_space=pltpu.HBM)] * other,
+        calibrate_kernel,
+        in_specs=[pl.BlockSpec(memory_space=pl.ANY)] * 2,
         out_specs=pl.BlockSpec(memory_space=pltpu.HBM),
-        out_shape=jax.ShapeDtypeStruct(shape, jnp.bfloat16),
+        out_shape=jax.ShapeDtypeStruct((samples, 2 * feeds, width), jnp.bfloat16),
         scratch_shapes=[
             pltpu.VMEM((chunks, 2, feeds, samples, LANES), jnp.bfloat16),
             pltpu.VMEM((chunks, 2, feeds, LANES), jnp.float32),
@@ -93,34 +83,31 @@
             pltpu.SemaphoreType.DMA((2, chunks)),
             pltpu.SemaphoreType.DMA((chunks,)),
         ],
-        input_output_aliases={3: 0} if other else {},
-        compiler_params=pltpu.CompilerParams(vmem_limit_bytes=(8 if other else 60) * MIB),
+        compiler_params=pltpu.CompilerParams(vmem_limit_bytes=60 * MIB),
         name="calibrate",
-    )(*operands)
+    )(voltages, gains)
 
 
 def detect_kernel(matrix_ref, x_ref, out_ref, scratch):
-    _, pair, _, _, width = x_ref.shape
+    width = x_ref.shape[1]
     step = 256
+    total = jnp.zeros((FEEDS, width // CHAN_SUM), jnp.float32)
     channel = lax.broadcasted_iota(jnp.int32, (step, width // CHAN_SUM), 0)
     group = lax.broadcasted_iota(jnp.int32, (step, width // CHAN_SUM), 1)
-    for t in range(pair):
-        total = jnp.zeros((FEEDS, width // CHAN_SUM), jnp.float32)
-        for j in range(width // step):
-            x = x_ref[:, t, :, :, j * step : (j + 1) * step].reshape(2 * FEEDS, step)
-            formed = jnp.dot(matrix_ref[...], x, preferred_element_type=jnp.float32)
-            power = formed[:FEEDS] * formed[:FEEDS] + formed[FEEDS:] * formed[FEEDS:]
-            high = power.astype(jnp.bfloat16)
-            low = (power - high.astype(jnp.float32)).astype(jnp.bfloat16)
-            pooling = ((channel + j * step) // CHAN_SUM == group).astype(jnp.bfloat16)
-            total += jnp.dot(high, pooling, preferred_element_type=jnp.float32)
-            total += jnp.dot(low, pooling, preferred_element_type=jnp.float32)
-        scratch[pl.ds(t, FEEDS, stride=pair), :] = total
+    for j in range(width // step):
+        cols = slice(j * step, (j + 1) * step)
+        formed = jnp.dot(matrix_ref[...], x_ref[:, cols], preferred_element_type=jnp.float32)
+        power = formed[:FEEDS] * formed[:FEEDS] + formed[FEEDS:] * formed[FEEDS:]
+        pooling = ((channel + j * step) // CHAN_SUM == group).astype(jnp.bfloat16)
+        total += jnp.dot(power.astype(jnp.bfloat16), pooling, preferred_element_type=jnp.float32)
+    pieces = width // CHAN_SUM // LANES
+    for h in range(pieces):
+        scratch[pl.ds(h, FEEDS, stride=pieces), :] = total[:, h * LANES : (h + 1) * LANES]
     out_ref[...] = scratch[...].astype(jnp.bfloat16)
 
 
 def detect(received, matrix):
-    shape = (FEEDS * received.shape[1], received.shape[4] // CHAN_SUM)
+    shape = (FEEDS * received.shape[1] // CHAN_SUM // LANES, LANES)
     return pl.pallas_call(
         detect_kernel,
         out_shape=jax.ShapeDtypeStruct(shape, jnp.bfloat16),
@@ -170,7 +157,7 @@
         for piece in range(pieces):
             rows = []
             for t in range(samples):
-                first = (group * 8 * samples + t // 2 * 2 + piece) * pieces + t % 2
+                first = group * 8 * samples * pieces + t * pieces + piece
                 rows.append(wide[pl.ds(first, 8, stride=samples * pieces), :])
             mean = functools.reduce(jnp.add, rows) * (1.0 / samples)
             rows = [row - mean for row in rows]
@@ -219,9 +206,14 @@
     )(detected, shifts)
 
 
-def peaks_kernel(widths_ref, series_ref, same_ref, peaks_ref, wide, sums):
+def width_range(k):
+    return (min(2 ** (k - 1) + 1, TIME), min(2**k, TIME)) if k else (1, 1)
+
+
+def peaks_kernel(widths_ref, series_ref, same_hbm, peaks_hbm, wide, sums, best, same_sem, sems):
     beams, samples, width = series_ref.shape
-    same_ref[...] = series_ref[...]
+    same = pltpu.make_async_copy(series_ref, same_hbm, same_sem)
+    same.start()
     for j in range(width // LANES):
         lanes = slice(j * LANES, (j + 1) * LANES)
         wide[j] = series_ref[:, :, lanes].astype(jnp.float32).reshape(beams * samples, LANES)
@@ -230,28 +222,40 @@
         for t in range(samples):
             total = total + wide[j, pl.ds(t, beams, stride=samples), :]
             sums[t + 1, :, lanes] = total
-    for k in range(peaks_ref.shape[0]):
+    for t in range(samples + 1, sums.shape[0]):
+        sums[t] = jnp.full((beams, width), -1e30, jnp.float32)
+    copies = []
+    for k in range(best.shape[0]):
         reach = widths_ref[k]
-
-        def widen(t, best):
-            return jnp.maximum(best, sums[t + reach] - sums[t])
-
-        best = lax.fori_loop(1, samples + 1 - reach, widen, sums[reach])
-        peaks_ref[k] = best / jnp.sqrt(jnp.full((beams, width), reach).astype(jnp.float32))
+        value = sums[reach]
+        for t in range(1, samples + 1 - width_range(k)[0]):
+            value = jnp.maximum(value, sums[t + reach] - sums[t])
+        best[k] = value / jnp.sqrt(jnp.full((beams, width), reach).astype(jnp.float32))
+        copies.append(pltpu.make_async_copy(best.at[k], peaks_hbm.at[k], sems.at[k]))
+        copies[-1].start()
+    same.wait()
+    for copy in copies:
+        copy.wait()
 
 
 def peaks(widths, series):
     beams, samples, width = series.shape
+    count = widths.shape[0]
+    rows = max(samples + 1 - low + high for low, high in map(width_range, range(count)))
     return pl.pallas_call(
         peaks_kernel,
         in_specs=[pl.BlockSpec(memory_space=pltpu.SMEM), pl.BlockSpec(memory_space=pltpu.VMEM)],
+        out_specs=[pl.BlockSpec(memory_space=pltpu.HBM)] * 2,
         out_shape=[
             jax.ShapeDtypeStruct(series.shape, series.dtype),
-            jax.ShapeDtypeStruct((widths.shape[0], beams, width), jnp.float32),
+            jax.ShapeDtypeStruct((count, beams, width), jnp.float32),
         ],
         scratch_shapes=[
             pltpu.VMEM((width // LANES, beams * samples, LANES), jnp.float32),
-            pltpu.VMEM((samples + 1, beams, width), jnp.float32),
+            pltpu.VMEM((rows, beams, width), jnp.float32),
+            pltpu.VMEM((count, beams, width), jnp.float32),
+            pltpu.SemaphoreType.DMA,
+            pltpu.SemaphoreType.DMA((count,)),
         ],
         compiler_params=pltpu.CompilerParams(vmem_limit_bytes=8 * MIB),
         name="peaks",
@@ -275,24 +279,18 @@
     return whole
 
 
-def exchanged(block, axes, groups=None):
-    return lax.all_to_all(block, axes, split_axis=0, concat_axis=0, axis_index_groups=groups, tiled=True)
+def exchanged(block, axes):
+    return lax.all_to_all(block, axes, split_axis=0, concat_axis=0, tiled=True)
 
 
 def shards(voltages, gains, shifts, widths):
     groups = lax.axis_size("beam")
-    core = (lax.axis_index("beam") & CORES - 1).astype(jnp.int32).reshape(1)
-    swap = [(i, i ^ 1) for i in range(groups)]
-    other = [lax.ppermute(block, "beam", swap) for block in (voltages, gains)]
-    calibrated = calibrate(core, *other, calibrate(core, voltages, gains))
-    calibrated, shifts = lax.optimization_barrier((calibrated, shifts))
-    same_core = [list(range(c, groups, CORES)) for c in range(CORES)]
-    received = exchanged(calibrated, "beam", same_core)
-    received = received.reshape((groups // CORES, CORES) + calibrated.shape[1:])
+    received = exchanged(calibrate(voltages, gains), "beam")
+    matrix, shifts = lax.optimization_barrier((steering(groups), shifts))
     table = jnp.transpose(gathered(shifts, "freq"), (1, 0, 2))
-    early = (steering(groups), table, jnp.maximum(widths, 1))
+    early = (matrix, table, jnp.maximum(widths, 1))
     received, matrix, table, reach = lax.optimization_barrier((received, *early))
-    detected = detect(received, matrix)
+    detected = detect(received.reshape(2 * FEEDS, received.shape[2]), matrix)
     spread = exchanged(detected.reshape(FEEDS, -1, LANES), ("freq", "beam"))
     series = exchanged(tree(spread.reshape(detected.shape), table), "freq")
     return tuple(peaks(reach, series))

time: 82.2 us -> 78.2 us (0.951)
  local copies, waits for them, and re-layouts: 2.24 us -> 0.02 us
  waiting for transfers between devices: 16.4 us -> 14.2 us
  blocking collectives: 30.5 us -> 31.7 us
  Pallas kernels: 8.69 us -> 7.67 us
    all_to_all x1, waiting for transfers between devices: 11.9 us -> 7.09 us  [exchanged(): return lax.all_to_all(block, axes, split_axis=0, concat_axis=0, tiled=True)]
    ppermute x2 -> x0, starting transfers between devices: 3.43 us -> none  [shards(): other = [lax.ppermute(block, 'beam', swap) for block in (voltages, gains)]]
    all_to_all x1, starting transfers between devices: 6.58 us -> 9.99 us  [exchanged(): return lax.all_to_all(block, axes, split_axis=0, concat_axis=0, tiled=True)]
    ppermute x6, waiting for transfers between devices: 4.07 us -> 7.14 us  [gathered(): lax.ppermute(whole, axis, [(i, i ^ k * step) for i in range(count)])]
    unnamed x8 -> x4, local copies, waits for them, and re-layouts: 2.23 us -> 0.01 us
    all_to_all x2, blocking collectives: 30.5 us -> 31.7 us  [exchanged(): return lax.all_to_all(block, axes, split_axis=0, concat_axis=0, tiled=True)]
    pallas_call x2 -> x1, Pallas kernels: 2.84 us -> 2.59 us  [calibrate(): pl.pallas_call(calibrate_kernel, in_specs=[pl.BlockSpec(memory_space=pl.A...]
  transfers between devices with their start and end apart: 9 -> 7, of which waited for: 4 -> 6; matrix products, arithmetic and copies ran while one was open for 8% -> 8% of each run, Pallas kernels for 3% -> 0%
where the time goes in v3:
time: 78.2 us; the launch traced here: 78 us
  blocking collectives  31.7 us (41%)
  starting transfers between devices  17.1 us (22%)
  waiting for transfers between devices  14.2 us (18%)
  Pallas kernels  7.67 us (10%)
  other arithmetic  6.4 us (8%)
    all_to_all x2, blocking collectives, exchanged(): return lax.all_to_all(block, axes, split_axis=0, concat_axis=0, tiled=True)  31.7 us
    all_to_all x1, starting transfers between devices, exchanged(): return lax.all_to_all(block, axes, split_axis=0, concat_axis=0, tiled=True)  9.99 us
    ppermute x6, starting transfers between devices, gathered(): lax.ppermute(whole, axis, [(i, i ^ k * step) for i in range(count)])  7.14 us
    ppermute x6, waiting for transfers between devices, gathered(): lax.ppermute(whole, axis, [(i, i ^ k * step) for i in range(count)])  7.14 us
    all_to_all x1, waiting for transfers between devices, exchanged(): return lax.all_to_all(block, axes, split_axis=0, concat_axis=0, tiled=True)  7.09 us
    convert_element_type x1, other arithmetic, steering(): return value.astype(jnp.bfloat16)  6.08 us
    pallas_call x1, Pallas kernels, calibrate(): pl.pallas_call(calibrate_kernel, in_specs=[pl.BlockSpec(memory_space=pl.A...  2.59 us
    pallas_call x1, Pallas kernels, tree(): pl.pallas_call(tree_kernel, out_shape=jax.ShapeDtypeStruct((blocks, TIME,...  2.22 us
  transfers between devices with their start and end apart: 7, of which 6 were waited for; matrix products, arithmetic and copies ran while one was open for 8% of the time, Pallas kernels for 0%

profile of v3, /device:TPU:1, one launch (start us, length us, event | category | flops | bytes accessed | tf_op | source)
XLA Modules:
  0.0 78.0 jit_solution(10707176760614574246)
XLA Ops:
  0.6 2.6 %calibrate.1 = bf16[16,32,1024]{2,1,0:T(8,128)(2,1)} custom-call(bf16[2,16,16,1024]{3,2,1,0:T(8,128)(2,1)} %volt_hbm.1, f32[2,16,1024]{2,1,0:T(8,128)} %gain_hbm.1), custom_call_target="tpu_custom_call" | custom-call | tf_op jit(solution)/shard_map/calibrate/pallas_call | solution.py:73
  3.2 10.0 %all-to-all-start = ((bf16[16,32,1024]{2,1,0:T(8,128)(2,1)}), bf16[16,32,1024]{2,1,0:T(8,128)(2,1)S(1)}, u32[]{:S(2)}, u32[]{:S(2)}) async-start(bf16[16,32,1024]{2,1,0:T(8,128)(2,1)} %calibrate.1), calls=%async_computation | async-start | bytes 2097152 | tf_op jit(solution)/shard_map/all_to_all | solution.py:283
  13.3 0.0 copy-start
  13.3 6.1 %fusion.7.matrix_ref = bf16[512,512]{1,0:T(8,128)(2,1)S(1)} fusion(s32[512]{0:T(512)S(1)} %get-tuple-element.23, s32[512]{0:T(512)S(1)} %get-tuple-element.27, s32[512]{0:T(512)S(1)} %get-tuple-element.21, s32[512]{0:T(512)S(1)} %get-tuple-element.28, s32[512]{0:T(512)S(1)} %get-tuple-element.25, s32[512]{0:T(512)S(1)} %get-tuple-element.26, ...), kind=kLoop, calls=%fused_computation.25 | loop fusion | flops 15204352 | bytes 547328 | tf_op jit(solution)/shard_map/convert_element_type | solution.py:32
  19.4 2.6 %collective-permute-start = (s32[1,12,256]{2,0,1:T(1,128)S(1)}, s32[1,12,256]{2,0,1:T(1,128)S(1)}, u32[]{:S(2)}, u32[]{:S(2)}) collective-permute-start(s32[1,12,256]{2,0,1:T(1,128)S(1)} %broadcast_in_dim.3), channel_id=1, source_target_pairs={{0,48},{16,32},{32,16},{48,0},{64,112},{80,96},{96,80},{112,64},{1... | collective-permute-start | bytes 36872 | tf_op jit(solution)/shard_map/ppermute | solution.py:273
  22.0 0.5 collective-permute-start.1
  22.5 0.3 collective-permute-start.2
  22.8 0.8 %collective-permute-done = s32[1,12,256]{2,0,1:T(1,128)S(1)} collective-permute-done((s32[1,12,256]{2,0,1:T(1,128)S(1)}, s32[1,12,256]{2,0,1:T(1,128)S(1)}, u32[]{:S(2)}, u32[]{:S(2)}) %collective-permute-start) | collective-permute-done | bytes 12320 | tf_op jit(solution)/shard_map/ppermute | solution.py:273
  23.6 2.8 %collective-permute-done.1 = s32[1,12,256]{2,0,1:T(1,128)S(1)} collective-permute-done((s32[1,12,256]{2,0,1:T(1,128)S(1)}, s32[1,12,256]{2,0,1:T(1,128)S(1)}, u32[]{:S(2)}, u32[]{:S(2)}) %collective-permute-start.1) | collective-permute-done | bytes 12320 | tf_op jit(solution)/shard_map/ppermute | solution.py:273
  26.4 0.0 copy-start.1
  26.4 0.1 pad_add_fusion
  26.5 3.0 %collective-permute-start.4 = (s32[4,12,256]{2,0,1:T(4,128)S(1)}, s32[4,12,256]{2,0,1:T(4,128)S(1)}, u32[]{:S(2)}, u32[]{:S(2)}) collective-permute-start(s32[4,12,256]{2,0,1:T(4,128)S(1)} %pad_add_fusion), channel_id=1, source_target_pairs={{0,128},{16,144},{32,160},{48,176},{64,192},{80,208},{96,224},{112... | collective-permute-start | bytes 147464 | tf_op jit(solution)/shard_map/ppermute | solution.py:273
  29.5 0.8 collective-permute-start.3
  30.3 0.9 %collective-permute-done.4 = s32[4,12,256]{2,0,1:T(4,128)S(1)} collective-permute-done((s32[4,12,256]{2,0,1:T(4,128)S(1)}, s32[4,12,256]{2,0,1:T(4,128)S(1)}, u32[]{:S(2)}, u32[]{:S(2)}) %collective-permute-start.4) | collective-permute-done | bytes 49184 | tf_op jit(solution)/shard_map/ppermute | solution.py:273
  31.2 2.6 %collective-permute-done.3 = s32[4,12,256]{2,0,1:T(4,128)S(1)} collective-permute-done((s32[4,12,256]{2,0,1:T(4,128)S(1)}, s32[4,12,256]{2,0,1:T(4,128)S(1)}, u32[]{:S(2)}, u32[]{:S(2)}) %collective-permute-start.3) | collective-permute-done | bytes 49184 | tf_op jit(solution)/shard_map/ppermute | solution.py:273
  33.8 0.1 collective-permute-done.5
  33.9 0.1 broadcast_select_fusion.12
  33.9 0.1 broadcast_select_fusion.15
  34.1 7.1 %all-to-all-done = bf16[16,32,1024]{2,1,0:T(8,128)(2,1)S(1)} async-done(((bf16[16,32,1024]{2,1,0:T(8,128)(2,1)}), bf16[16,32,1024]{2,1,0:T(8,128)(2,1)S(1)}, u32[]{:S(2)}, u32[]{:S(2)}) %all-to-all-start) | async-done | bytes 1048608 | tf_op jit(solution)/shard_map/all_to_all | solution.py:283
  41.2 1.4 %detect.1 = bf16[512,128]{1,0:T(8,128)(2,1)S(1)} custom-call(bf16[512,512]{1,0:T(8,128)(2,1)S(1)} %fusion.7.matrix_ref, bf16[512,1024]{1,0:T(8,128)(2,1)S(1)} %bitcast.5), custom_call_target="tpu_custom_call" | custom-call | tf_op jit(solution)/shard_map/detect/pallas_call | solution.py:111
  42.6 21.9 %all_to_all.15 = bf16[256,2,128]{2,1,0:T(2,128)(2,1)S(1)} all-to-all(bf16[256,2,128]{2,1,0:T(2,128)(2,1)S(1)} %bitcast.7), channel_id=1, replica_groups=mesh['freq'=16,'beam'=16] {'freq','beam'}, dimensions={0} | all-to-all | bytes 262144 | tf_op jit(solution)/shard_map/all_to_all | solution.py:283
  64.5 2.2 %tree.1 = bf16[16,16,256]{2,1,0:T(8,128)(2,1)S(1)} custom-call(bf16[512,128]{1,0:T(8,128)(2,1)S(1)} %bitcast.6, s32[12,16,256]{2,1,0:T(8,128)S(1)} %add_bitcast_fusion.shifts_ref), custom_call_target="tpu_custom_call" | custom-call | tf_op jit(solution)/shard_map/tree/pallas_call | solution.py:196
  66.7 9.8 %all_to_all.16.series_ref = bf16[16,16,256]{2,1,0:T(8,128)(2,1)S(1)} all-to-all(bf16[16,16,256]{2,1,0:T(8,128)(2,1)S(1)} %tree.1), channel_id=1, replica_groups=mesh['freq'=16,'beam'=16] {'freq'}, dimensions={0} | all-to-all | bytes 262144 | tf_op jit(solution)/shard_map/all_to_all | solution.py:283
  76.5 1.4 %peaks.1 = (bf16[16,16,256]{2,1,0:T(8,128)(2,1)}, f32[8,16,256]{2,1,0:T(8,128)}) custom-call(s32[8]{0:T(128)S(1)} %broadcast_maximum_fusion.widths_ref, bf16[16,16,256]{2,1,0:T(8,128)(2,1)S(1)} %all_to_all.16.series_ref), custom_call_target="tpu_custom_call" | custom-call | tf_op jit(solution)/shard_map/peaks/pallas_call | solution.py:245
  (16 shorter events, 0.2 us)
Async XLA Ops:
  3.2 37.9 %all-to-all-start = ((bf16[16,32,1024]{2,1,0:T(8,128)(2,1)}), bf16[16,32,1024]{2,1,0:T(8,128)(2,1)S(1)}, u32[]{:S(2)}, u32[]{:S(2)}) async-start(bf16[16,32,1024]{2,1,0:T(8,128)(2,1)} %calibrate.1), calls=%async_computation | async-start | bytes 2097152 | tf_op jit(solution)/shard_map/all_to_all | solution.py:283
  13.3 6.1 %copy-start = (s32[12,256]{1,0:T(8,128)S(1)}, s32[12,256]{1,0:T(8,128)}, u32[]{:S(2)}) copy-start(s32[12,256]{1,0:T(8,128)} %param.6) | copy-start | bytes 36868
  19.4 4.2 %collective-permute-start = (s32[1,12,256]{2,0,1:T(1,128)S(1)}, s32[1,12,256]{2,0,1:T(1,128)S(1)}, u32[]{:S(2)}, u32[]{:S(2)}) collective-permute-start(s32[1,12,256]{2,0,1:T(1,128)S(1)} %broadcast_in_dim.3), channel_id=1, source_target_pairs={{0,48},{16,32},{32,16},{48,0},{64,112},{80,96},{96,80},{112,64},{1... | collective-permute-start | bytes 36872 | tf_op jit(solution)/shard_map/ppermute | solution.py:273
  22.0 4.3 %collective-permute-start.1 = (s32[1,12,256]{2,0,1:T(1,128)S(1)}, s32[1,12,256]{2,0,1:T(1,128)S(1)}, u32[]{:S(2)}, u32[]{:S(2)}) collective-permute-start(s32[1,12,256]{2,0,1:T(1,128)S(1)} %broadcast_in_dim.3), channel_id=1, source_target_pairs={{0,32},{16,48},{32,0},{48,16},{64,96},{80,112},{96,64},{112,80},{1... | collective-permute-start | bytes 36872 | tf_op jit(solution)/shard_map/ppermute | solution.py:273
  22.5 3.8 %collective-permute-start.2 = (s32[1,12,256]{2,0,1:T(1,128)S(1)}, s32[1,12,256]{2,0,1:T(1,128)S(1)}, u32[]{:S(2)}, u32[]{:S(2)}) collective-permute-start(s32[1,12,256]{2,0,1:T(1,128)S(1)} %broadcast_in_dim.3), channel_id=1, source_target_pairs={{0,16},{16,0},{32,48},{48,32},{64,80},{80,64},{96,112},{112,96},{1... | collective-permute-start | bytes 36872 | tf_op jit(solution)/shard_map/ppermute | solution.py:273
  26.4 3.9 %copy-start.1 = (s32[8]{0:T(128)S(1)}, s32[8]{0:T(128)}, u32[]{:S(2)}) copy-start(s32[8]{0:T(128)} %param.7) | copy-start | bytes 100
  26.5 4.7 %collective-permute-start.4 = (s32[4,12,256]{2,0,1:T(4,128)S(1)}, s32[4,12,256]{2,0,1:T(4,128)S(1)}, u32[]{:S(2)}, u32[]{:S(2)}) collective-permute-start(s32[4,12,256]{2,0,1:T(4,128)S(1)} %pad_add_fusion), channel_id=1, source_target_pairs={{0,128},{16,144},{32,160},{48,176},{64,192},{80,208},{96,224},{112... | collective-permute-start | bytes 147464 | tf_op jit(solution)/shard_map/ppermute | solution.py:273
  29.5 4.3 %collective-permute-start.3 = (s32[4,12,256]{2,0,1:T(4,128)S(1)}, s32[4,12,256]{2,0,1:T(4,128)S(1)}, u32[]{:S(2)}, u32[]{:S(2)}) collective-permute-start(s32[4,12,256]{2,0,1:T(4,128)S(1)} %pad_add_fusion), channel_id=1, source_target_pairs={{0,192},{16,208},{32,224},{48,240},{64,128},{80,144},{96,160},{112... | collective-permute-start | bytes 147464 | tf_op jit(solution)/shard_map/ppermute | solution.py:273
  30.3 3.6 %collective-permute-start.5 = (s32[4,12,256]{2,0,1:T(4,128)S(1)}, s32[4,12,256]{2,0,1:T(4,128)S(1)}, u32[]{:S(2)}, u32[]{:S(2)}) collective-permute-start(s32[4,12,256]{2,0,1:T(4,128)S(1)} %pad_add_fusion), channel_id=1, source_target_pairs={{0,64},{16,80},{32,96},{48,112},{64,0},{80,16},{96,32},{112,48},{1... | collective-permute-start | bytes 147464 | tf_op jit(solution)/shard_map/ppermute | solution.py:273

commit v4 on v3

--- a/solution.py
+++ b/solution.py
@@ -13,6 +13,7 @@
 NSUB = 4096
 TIME = 16
 LANES = 128
+PITCH = 24
 MIB = 1024 * 1024
 
 
@@ -52,12 +53,14 @@
         for copy in arriving(j):
             copy.wait()
         for part in range(2):
-            wide[j, part] = volt[j, part].astype(jnp.float32).reshape(feeds * samples, LANES)
+            block = volt[j, part].astype(jnp.float32)
+            for f in range(feeds):
+                wide[j, part, f * PITCH : f * PITCH + samples] = block[f]
         gain_re = gain[j, 0]
         gain_im = gain[j, 1]
         for t in range(samples):
-            volt_re = wide[j, 0, pl.ds(t, feeds, stride=samples), :]
-            volt_im = wide[j, 1, pl.ds(t, feeds, stride=samples), :]
+            volt_re = wide[j, 0, pl.ds(t, feeds, stride=PITCH), :]
+            volt_im = wide[j, 1, pl.ds(t, feeds, stride=PITCH), :]
             real = gain_re * volt_re - gain_im * volt_im
             imag = gain_re * volt_im + gain_im * volt_re
             done[j, t, :feeds] = real.astype(jnp.bfloat16)
@@ -78,7 +81,7 @@
         scratch_shapes=[
             pltpu.VMEM((chunks, 2, feeds, samples, LANES), jnp.bfloat16),
             pltpu.VMEM((chunks, 2, feeds, LANES), jnp.float32),
-            pltpu.VMEM((chunks, 2, feeds * samples, LANES), jnp.float32),
+            pltpu.VMEM((chunks, 2, feeds * PITCH, LANES), jnp.float32),
             pltpu.VMEM((chunks, samples, 2 * feeds, LANES), jnp.bfloat16),
             pltpu.SemaphoreType.DMA((2, chunks)),
             pltpu.SemaphoreType.DMA((chunks,)),
@@ -98,8 +101,14 @@
         cols = slice(j * step, (j + 1) * step)
         formed = jnp.dot(matrix_ref[...], x_ref[:, cols], preferred_element_type=jnp.float32)
         power = formed[:FEEDS] * formed[:FEEDS] + formed[FEEDS:] * formed[FEEDS:]
-        pooling = ((channel + j * step) // CHAN_SUM == group).astype(jnp.bfloat16)
-        total += jnp.dot(power.astype(jnp.bfloat16), pooling, preferred_element_type=jnp.float32)
+        sums = []
+        for lane in range(0, step, LANES):
+            part = power[:, lane : lane + LANES]
+            part = part + pltpu.roll(part, LANES - 1, 1)
+            sums.append(part + pltpu.roll(part, LANES - 2, 1))
+        picking = (channel + j * step == group * CHAN_SUM).astype(jnp.bfloat16)
+        summed = jnp.concatenate(sums, axis=1).astype(jnp.bfloat16)
+        total += jnp.dot(summed, picking, preferred_element_type=jnp.float32)
     pieces = width // CHAN_SUM // LANES
     for h in range(pieces):
         scratch[pl.ds(h, FEEDS, stride=pieces), :] = total[:, h * LANES : (h + 1) * LANES]
@@ -135,10 +144,11 @@
 
 
 def folded(rows, axis, half, bits):
-    size = rows[0].shape[axis]
-    upper = (lax.broadcasted_iota(jnp.int32, rows[0].shape, axis) & half) != 0
-    lower_rows = [jnp.where(upper, pltpu.roll(x, half, axis), x) for x in rows]
-    higher_rows = [jnp.where(upper, x, pltpu.roll(x, size - half, axis)) for x in rows]
+    place = lax.broadcasted_iota(jnp.int32, rows[0].shape, axis)
+    upper = (place & half) != 0
+    facing = [jnp.take_along_axis(x, place ^ half, axis=axis) for x in rows]
+    lower_rows = [jnp.where(upper, y, x) for x, y in zip(rows, facing)]
+    higher_rows = [jnp.where(upper, x, y) for x, y in zip(rows, facing)]
     return merged(lower_rows, higher_rows, bits)
 
 

time: 78.2 us -> 77.5 us (level)
  no operation moved by 1% of the time
where the time goes in v4:
time: 77.5 us; the launch traced here: 77.3 us
  blocking collectives  31.7 us (41%)
  starting transfers between devices  17.1 us (22%)
  waiting for transfers between devices  14.2 us (18%)
  Pallas kernels  7 us (9%)
  other arithmetic  6.4 us (8%)
    all_to_all x2, blocking collectives, exchanged(): return lax.all_to_all(block, axes, split_axis=0, concat_axis=0, tiled=True)  31.7 us
    all_to_all x1, starting transfers between devices, exchanged(): return lax.all_to_all(block, axes, split_axis=0, concat_axis=0, tiled=True)  9.99 us
    ppermute x6, starting transfers between devices, gathered(): lax.ppermute(whole, axis, [(i, i ^ k * step) for i in range(count)])  7.14 us
    ppermute x6, waiting for transfers between devices, gathered(): lax.ppermute(whole, axis, [(i, i ^ k * step) for i in range(count)])  7.14 us
    all_to_all x1, waiting for transfers between devices, exchanged(): return lax.all_to_all(block, axes, split_axis=0, concat_axis=0, tiled=True)  7.09 us
    convert_element_type x1, other arithmetic, steering(): return value.astype(jnp.bfloat16)  6.08 us
    pallas_call x1, Pallas kernels, calibrate(): pl.pallas_call(calibrate_kernel, in_specs=[pl.BlockSpec(memory_space=pl.A...  2.42 us
    pallas_call x1, Pallas kernels, detect(): pl.pallas_call(detect_kernel, out_shape=jax.ShapeDtypeStruct(shape, jnp.b...  1.71 us
  transfers between devices with their start and end apart: 7, of which 6 were waited for; matrix products, arithmetic and copies ran while one was open for 8% of the time, Pallas kernels for 0%

profile of v4, /device:TPU:1, one launch (start us, length us, event | category | flops | bytes accessed | tf_op | source)
XLA Modules:
  0.0 77.3 jit_solution(8794132408623481559)
XLA Ops:
  0.6 2.4 %calibrate.1 = bf16[16,32,1024]{2,1,0:T(8,128)(2,1)} custom-call(bf16[2,16,16,1024]{3,2,1,0:T(8,128)(2,1)} %volt_hbm.1, f32[2,16,1024]{2,1,0:T(8,128)} %gain_hbm.1), custom_call_target="tpu_custom_call" | custom-call | tf_op jit(solution)/shard_map/calibrate/pallas_call | solution.py:76
  3.1 10.0 %all-to-all-start = ((bf16[16,32,1024]{2,1,0:T(8,128)(2,1)}), bf16[16,32,1024]{2,1,0:T(8,128)(2,1)S(1)}, u32[]{:S(2)}, u32[]{:S(2)}) async-start(bf16[16,32,1024]{2,1,0:T(8,128)(2,1)} %calibrate.1), calls=%async_computation | async-start | bytes 2097152 | tf_op jit(solution)/shard_map/all_to_all | solution.py:293
  13.1 0.0 copy-start
  13.2 6.1 %fusion.7.matrix_ref = bf16[512,512]{1,0:T(8,128)(2,1)S(1)} fusion(s32[512]{0:T(512)S(1)} %get-tuple-element.23, s32[512]{0:T(512)S(1)} %get-tuple-element.27, s32[512]{0:T(512)S(1)} %get-tuple-element.21, s32[512]{0:T(512)S(1)} %get-tuple-element.28, s32[512]{0:T(512)S(1)} %get-tuple-element.25, s32[512]{0:T(512)S(1)} %get-tuple-element.26, ...), kind=kLoop, calls=%fused_computation.25 | loop fusion | flops 15204352 | bytes 547328 | tf_op jit(solution)/shard_map/convert_element_type | solution.py:33
  19.3 2.6 %collective-permute-start = (s32[1,12,256]{2,0,1:T(1,128)S(1)}, s32[1,12,256]{2,0,1:T(1,128)S(1)}, u32[]{:S(2)}, u32[]{:S(2)}) collective-permute-start(s32[1,12,256]{2,0,1:T(1,128)S(1)} %broadcast_in_dim.3), channel_id=1, source_target_pairs={{0,48},{16,32},{32,16},{48,0},{64,112},{80,96},{96,80},{112,64},{1... | collective-permute-start | bytes 36872 | tf_op jit(solution)/shard_map/ppermute | solution.py:283
  21.9 0.5 collective-permute-start.1
  22.4 0.3 collective-permute-start.2
  22.6 0.8 %collective-permute-done = s32[1,12,256]{2,0,1:T(1,128)S(1)} collective-permute-done((s32[1,12,256]{2,0,1:T(1,128)S(1)}, s32[1,12,256]{2,0,1:T(1,128)S(1)}, u32[]{:S(2)}, u32[]{:S(2)}) %collective-permute-start) | collective-permute-done | bytes 12320 | tf_op jit(solution)/shard_map/ppermute | solution.py:283
  23.4 2.8 %collective-permute-done.1 = s32[1,12,256]{2,0,1:T(1,128)S(1)} collective-permute-done((s32[1,12,256]{2,0,1:T(1,128)S(1)}, s32[1,12,256]{2,0,1:T(1,128)S(1)}, u32[]{:S(2)}, u32[]{:S(2)}) %collective-permute-start.1) | collective-permute-done | bytes 12320 | tf_op jit(solution)/shard_map/ppermute | solution.py:283
  26.3 0.0 copy-start.1
  26.3 0.1 pad_add_fusion
  26.3 3.0 %collective-permute-start.4 = (s32[4,12,256]{2,0,1:T(4,128)S(1)}, s32[4,12,256]{2,0,1:T(4,128)S(1)}, u32[]{:S(2)}, u32[]{:S(2)}) collective-permute-start(s32[4,12,256]{2,0,1:T(4,128)S(1)} %pad_add_fusion), channel_id=1, source_target_pairs={{0,128},{16,144},{32,160},{48,176},{64,192},{80,208},{96,224},{112... | collective-permute-start | bytes 147464 | tf_op jit(solution)/shard_map/ppermute | solution.py:283
  29.3 0.8 %collective-permute-start.3 = (s32[4,12,256]{2,0,1:T(4,128)S(1)}, s32[4,12,256]{2,0,1:T(4,128)S(1)}, u32[]{:S(2)}, u32[]{:S(2)}) collective-permute-start(s32[4,12,256]{2,0,1:T(4,128)S(1)} %pad_add_fusion), channel_id=1, source_target_pairs={{0,192},{16,208},{32,224},{48,240},{64,128},{80,144},{96,160},{112... | collective-permute-start | bytes 147464 | tf_op jit(solution)/shard_map/ppermute | solution.py:283
  30.1 0.9 %collective-permute-done.4 = s32[4,12,256]{2,0,1:T(4,128)S(1)} collective-permute-done((s32[4,12,256]{2,0,1:T(4,128)S(1)}, s32[4,12,256]{2,0,1:T(4,128)S(1)}, u32[]{:S(2)}, u32[]{:S(2)}) %collective-permute-start.4) | collective-permute-done | bytes 49184 | tf_op jit(solution)/shard_map/ppermute | solution.py:283
  31.0 2.6 %collective-permute-done.3 = s32[4,12,256]{2,0,1:T(4,128)S(1)} collective-permute-done((s32[4,12,256]{2,0,1:T(4,128)S(1)}, s32[4,12,256]{2,0,1:T(4,128)S(1)}, u32[]{:S(2)}, u32[]{:S(2)}) %collective-permute-start.3) | collective-permute-done | bytes 49184 | tf_op jit(solution)/shard_map/ppermute | solution.py:283
  33.6 0.1 collective-permute-done.5
  33.7 0.1 broadcast_select_fusion.12
  33.8 0.1 broadcast_select_fusion.15
  33.9 7.1 %all-to-all-done = bf16[16,32,1024]{2,1,0:T(8,128)(2,1)S(1)} async-done(((bf16[16,32,1024]{2,1,0:T(8,128)(2,1)}), bf16[16,32,1024]{2,1,0:T(8,128)(2,1)S(1)}, u32[]{:S(2)}, u32[]{:S(2)}) %all-to-all-start) | async-done | bytes 1048608 | tf_op jit(solution)/shard_map/all_to_all | solution.py:293
  41.0 1.7 %detect.1 = bf16[512,128]{1,0:T(8,128)(2,1)S(1)} custom-call(bf16[512,512]{1,0:T(8,128)(2,1)S(1)} %fusion.7.matrix_ref, bf16[512,1024]{1,0:T(8,128)(2,1)S(1)} %bitcast.5), custom_call_target="tpu_custom_call" | custom-call | tf_op jit(solution)/shard_map/detect/pallas_call | solution.py:120
  42.7 21.9 %all_to_all.15 = bf16[256,2,128]{2,1,0:T(2,128)(2,1)S(1)} all-to-all(bf16[256,2,128]{2,1,0:T(2,128)(2,1)S(1)} %bitcast.7), channel_id=1, replica_groups=mesh['freq'=16,'beam'=16] {'freq','beam'}, dimensions={0} | all-to-all | bytes 262144 | tf_op jit(solution)/shard_map/all_to_all | solution.py:293
  64.6 1.4 %tree.1 = bf16[16,16,256]{2,1,0:T(8,128)(2,1)S(1)} custom-call(bf16[512,128]{1,0:T(8,128)(2,1)S(1)} %bitcast.6, s32[12,16,256]{2,1,0:T(8,128)S(1)} %add_bitcast_fusion.shifts_ref), custom_call_target="tpu_custom_call" | custom-call | tf_op jit(solution)/shard_map/tree/pallas_call | solution.py:206
  66.0 9.8 %all_to_all.16.series_ref = bf16[16,16,256]{2,1,0:T(8,128)(2,1)S(1)} all-to-all(bf16[16,16,256]{2,1,0:T(8,128)(2,1)S(1)} %tree.1), channel_id=1, replica_groups=mesh['freq'=16,'beam'=16] {'freq'}, dimensions={0} | all-to-all | bytes 262144 | tf_op jit(solution)/shard_map/all_to_all | solution.py:293
  75.8 1.4 %peaks.1 = (bf16[16,16,256]{2,1,0:T(8,128)(2,1)}, f32[8,16,256]{2,1,0:T(8,128)}) custom-call(s32[8]{0:T(128)S(1)} %broadcast_maximum_fusion.widths_ref, bf16[16,16,256]{2,1,0:T(8,128)(2,1)S(1)} %all_to_all.16.series_ref), custom_call_target="tpu_custom_call" | custom-call | tf_op jit(solution)/shard_map/peaks/pallas_call | solution.py:255
  (16 shorter events, 0.2 us)
Async XLA Ops:
  3.1 37.9 %all-to-all-start = ((bf16[16,32,1024]{2,1,0:T(8,128)(2,1)}), bf16[16,32,1024]{2,1,0:T(8,128)(2,1)S(1)}, u32[]{:S(2)}, u32[]{:S(2)}) async-start(bf16[16,32,1024]{2,1,0:T(8,128)(2,1)} %calibrate.1), calls=%async_computation | async-start | bytes 2097152 | tf_op jit(solution)/shard_map/all_to_all | solution.py:293
  13.1 6.1 %copy-start = (s32[12,256]{1,0:T(8,128)S(1)}, s32[12,256]{1,0:T(8,128)}, u32[]{:S(2)}) copy-start(s32[12,256]{1,0:T(8,128)} %param.6) | copy-start | bytes 36868
  19.3 4.2 %collective-permute-start = (s32[1,12,256]{2,0,1:T(1,128)S(1)}, s32[1,12,256]{2,0,1:T(1,128)S(1)}, u32[]{:S(2)}, u32[]{:S(2)}) collective-permute-start(s32[1,12,256]{2,0,1:T(1,128)S(1)} %broadcast_in_dim.3), channel_id=1, source_target_pairs={{0,48},{16,32},{32,16},{48,0},{64,112},{80,96},{96,80},{112,64},{1... | collective-permute-start | bytes 36872 | tf_op jit(solution)/shard_map/ppermute | solution.py:283
  21.9 4.3 %collective-permute-start.1 = (s32[1,12,256]{2,0,1:T(1,128)S(1)}, s32[1,12,256]{2,0,1:T(1,128)S(1)}, u32[]{:S(2)}, u32[]{:S(2)}) collective-permute-start(s32[1,12,256]{2,0,1:T(1,128)S(1)} %broadcast_in_dim.3), channel_id=1, source_target_pairs={{0,32},{16,48},{32,0},{48,16},{64,96},{80,112},{96,64},{112,80},{1... | collective-permute-start | bytes 36872 | tf_op jit(solution)/shard_map/ppermute | solution.py:283
  22.4 3.8 %collective-permute-start.2 = (s32[1,12,256]{2,0,1:T(1,128)S(1)}, s32[1,12,256]{2,0,1:T(1,128)S(1)}, u32[]{:S(2)}, u32[]{:S(2)}) collective-permute-start(s32[1,12,256]{2,0,1:T(1,128)S(1)} %broadcast_in_dim.3), channel_id=1, source_target_pairs={{0,16},{16,0},{32,48},{48,32},{64,80},{80,64},{96,112},{112,96},{1... | collective-permute-start | bytes 36872 | tf_op jit(solution)/shard_map/ppermute | solution.py:283
  26.3 3.9 %copy-start.1 = (s32[8]{0:T(128)S(1)}, s32[8]{0:T(128)}, u32[]{:S(2)}) copy-start(s32[8]{0:T(128)} %param.7) | copy-start | bytes 100
  26.3 4.7 %collective-permute-start.4 = (s32[4,12,256]{2,0,1:T(4,128)S(1)}, s32[4,12,256]{2,0,1:T(4,128)S(1)}, u32[]{:S(2)}, u32[]{:S(2)}) collective-permute-start(s32[4,12,256]{2,0,1:T(4,128)S(1)} %pad_add_fusion), channel_id=1, source_target_pairs={{0,128},{16,144},{32,160},{48,176},{64,192},{80,208},{96,224},{112... | collective-permute-start | bytes 147464 | tf_op jit(solution)/shard_map/ppermute | solution.py:283
  29.3 4.3 %collective-permute-start.3 = (s32[4,12,256]{2,0,1:T(4,128)S(1)}, s32[4,12,256]{2,0,1:T(4,128)S(1)}, u32[]{:S(2)}, u32[]{:S(2)}) collective-permute-start(s32[4,12,256]{2,0,1:T(4,128)S(1)} %pad_add_fusion), channel_id=1, source_target_pairs={{0,192},{16,208},{32,224},{48,240},{64,128},{80,144},{96,160},{112... | collective-permute-start | bytes 147464 | tf_op jit(solution)/shard_map/ppermute | solution.py:283
  30.1 3.6 %collective-permute-start.5 = (s32[4,12,256]{2,0,1:T(4,128)S(1)}, s32[4,12,256]{2,0,1:T(4,128)S(1)}, u32[]{:S(2)}, u32[]{:S(2)}) collective-permute-start(s32[4,12,256]{2,0,1:T(4,128)S(1)} %pad_add_fusion), channel_id=1, source_target_pairs={{0,64},{16,80},{32,96},{48,112},{64,0},{80,16},{96,32},{112,48},{1... | collective-permute-start | bytes 147464 | tf_op jit(solution)/shard_map/ppermute | solution.py:283

commit v5 on v4

--- a/solution.py
+++ b/solution.py
@@ -13,43 +13,65 @@
 NSUB = 4096
 TIME = 16
 LANES = 128
+CORES = 2
 PITCH = 24
 MIB = 1024 * 1024
 
 
-def steering(groups):
+def steering(groups, chip):
     size = FEEDS // groups
-    row = lax.broadcasted_iota(jnp.int32, (2 * FEEDS, 2 * FEEDS), 0)
-    col = lax.broadcasted_iota(jnp.int32, (2 * FEEDS, 2 * FEEDS), 1)
+    chips = groups // CORES
+    span = FEEDS // chips
+    row = lax.broadcasted_iota(jnp.int32, (2 * FEEDS, LANES), 0)
+    col = lax.broadcasted_iota(jnp.int32, (2 * FEEDS, LANES), 1)
     out_part = row // FEEDS
     beam = row % groups * size + row % FEEDS // groups
-    feed = col // (2 * size) * size + col % size
-    in_part = col // size % 2
-    angles = (beam * feed % FEEDS).astype(jnp.float32) * (2.0 * math.pi / FEEDS)
+    rest = col // (2 * size) % CORES * size + col % size
+    quarters = out_part - col // size % 2
+    angles = (beam * rest + quarters * (FEEDS // 4) & FEEDS - 1).astype(jnp.float32) * (2.0 * math.pi / FEEDS)
     factor = 1.0 / math.sqrt(FEEDS)
     cosine = jnp.cos(angles) * factor
     sine = jnp.sin(angles) * factor
-    value = jnp.where(in_part == out_part, cosine, jnp.where(out_part == 0, sine, -sine))
-    return value.astype(jnp.bfloat16)
-
-
-def calibrate_kernel(volt_hbm, gain_hbm, out_hbm, volt, gain, wide, done, in_sems, out_sems):
+    blocks = []
+    for first in range(0, chips, LANES // (2 * span)):
+        source = chip - (first + col // (2 * span)) & chips - 1
+        turn = beam * source & chips - 1
+        whole_cosine = eighth_cosine(turn)
+        whole_sine = eighth_cosine(turn - chips // 4 & chips - 1)
+        blocks.append((whole_cosine * cosine - whole_sine * sine).astype(jnp.bfloat16))
+    return jnp.concatenate(blocks, axis=1)
+
+
+def eighth_cosine(turn):
+    size = jnp.where(turn % 2 == 1, math.sqrt(0.5), jnp.where(turn % 4 == 2, 0.0, 1.0))
+    return jnp.where((turn > 2) & (turn < 6), -size, size)
+
+
+def calibrate_kernel(where_ref, volt_hbm, gain_hbm, *rest, own):
+    if own:
+        outs, rest = rest[:1], rest[1:]
+    else:
+        begun_ref, outs, rest = rest[0], rest[1:9], rest[9:]
+    volt, gain, wide, in_sems = rest
     chunks, _, feeds, samples, _ = volt.shape
+    chip, core = where_ref[0], where_ref[1]
 
     def arriving(j):
-        lanes = pl.ds(j * LANES, LANES)
+        lanes = pl.ds(pl.multiple_of((core * chunks + j) * LANES, LANES), LANES)
         return (
             pltpu.make_async_copy(volt_hbm.at[:, :, :, lanes], volt.at[j], in_sems.at[0, j]),
             pltpu.make_async_copy(gain_hbm.at[:, :, lanes], gain.at[j], in_sems.at[1, j]),
         )
 
-    def leaving(j):
-        return pltpu.make_async_copy(done.at[j], out_hbm.at[:, :, pl.ds(j * LANES, LANES)], out_sems.at[j])
-
     for j in range(chunks):
         for copy in arriving(j):
             copy.start()
+    if not own:
+        for k, out in enumerate(outs):
+            for t in range(2):
+                out[t, core] = begun_ref[2 * (chip + k & len(outs) - 1) + t]
     for j in range(chunks):
+        lanes = slice(j * LANES, (j + 1) * LANES)
         for copy in arriving(j):
             copy.wait()
         for part in range(2):
@@ -58,72 +80,82 @@
                 wide[j, part, f * PITCH : f * PITCH + samples] = block[f]
         gain_re = gain[j, 0]
         gain_im = gain[j, 1]
-        for t in range(samples):
-            volt_re = wide[j, 0, pl.ds(t, feeds, stride=PITCH), :]
-            volt_im = wide[j, 1, pl.ds(t, feeds, stride=PITCH), :]
-            real = gain_re * volt_re - gain_im * volt_im
-            imag = gain_re * volt_im + gain_im * volt_re
-            done[j, t, :feeds] = real.astype(jnp.bfloat16)
-            done[j, t, feeds:] = imag.astype(jnp.bfloat16)
-        leaving(j).start()
-    for j in range(chunks):
-        leaving(j).wait()
-
-
-def calibrate(voltages, gains):
+        for k in range(samples // 2):
+            for t in range(2):
+                sample = 2 * k + t if own else 2 * (chip + k & samples // 2 - 1) + t
+                volt_re = wide[j, 0, pl.ds(sample, feeds, stride=PITCH), :]
+                volt_im = wide[j, 1, pl.ds(sample, feeds, stride=PITCH), :]
+                real = (gain_re * volt_re - gain_im * volt_im).astype(jnp.bfloat16)
+                imag = (gain_re * volt_im + gain_im * volt_re).astype(jnp.bfloat16)
+                if own:
+                    outs[0][sample, :feeds, lanes] = real
+                    outs[0][sample, feeds:, lanes] = imag
+                else:
+                    outs[k][t, 1 - core, :feeds, lanes] = real
+                    outs[k][t, 1 - core, feeds:, lanes] = imag
+
+
+def calibrate(where, voltages, gains, begun=None):
     _, feeds, samples, width = voltages.shape
-    chunks = width // LANES
+    chunks = width // CORES // LANES
+    own = begun is None
+    shape = (samples, 2 * feeds, width // CORES)
+    if own:
+        out_shape = jax.ShapeDtypeStruct(shape, jnp.bfloat16)
+    else:
+        out_shape = [jax.ShapeDtypeStruct((2, CORES) + shape[1:], jnp.bfloat16)] * (samples // 2)
+    operands = (where, voltages, gains) + (() if own else (begun,))
     return pl.pallas_call(
-        calibrate_kernel,
-        in_specs=[pl.BlockSpec(memory_space=pl.ANY)] * 2,
-        out_specs=pl.BlockSpec(memory_space=pltpu.HBM),
-        out_shape=jax.ShapeDtypeStruct((samples, 2 * feeds, width), jnp.bfloat16),
+        functools.partial(calibrate_kernel, own=own),
+        in_specs=[pl.BlockSpec(memory_space=pltpu.SMEM)]
+        + [pl.BlockSpec(memory_space=pl.ANY)] * 2
+        + [pl.BlockSpec(memory_space=pltpu.VMEM)] * (not own),
+        out_shape=out_shape,
         scratch_shapes=[
             pltpu.VMEM((chunks, 2, feeds, samples, LANES), jnp.bfloat16),
             pltpu.VMEM((chunks, 2, feeds, LANES), jnp.float32),
             pltpu.VMEM((chunks, 2, feeds * PITCH, LANES), jnp.float32),
-            pltpu.VMEM((chunks, samples, 2 * feeds, LANES), jnp.bfloat16),
             pltpu.SemaphoreType.DMA((2, chunks)),
-            pltpu.SemaphoreType.DMA((chunks,)),
         ],
-        compiler_params=pltpu.CompilerParams(vmem_limit_bytes=60 * MIB),
+        compiler_params=pltpu.CompilerParams(vmem_limit_bytes=(58 if own else 16) * MIB),
         name="calibrate",
-    )(voltages, gains)
-
-
-def detect_kernel(matrix_ref, x_ref, out_ref, scratch):
-    width = x_ref.shape[1]
+    )(*operands)
+
+
+def detect_kernel(matrix_ref, *rest):
+    parts, (out_ref, scratch) = rest[:-2], rest[-2:]
+    pair, _, _, width = parts[0].shape
     step = 256
-    total = jnp.zeros((FEEDS, width // CHAN_SUM), jnp.float32)
     channel = lax.broadcasted_iota(jnp.int32, (step, width // CHAN_SUM), 0)
     group = lax.broadcasted_iota(jnp.int32, (step, width // CHAN_SUM), 1)
-    for j in range(width // step):
-        cols = slice(j * step, (j + 1) * step)
-        formed = jnp.dot(matrix_ref[...], x_ref[:, cols], preferred_element_type=jnp.float32)
-        power = formed[:FEEDS] * formed[:FEEDS] + formed[FEEDS:] * formed[FEEDS:]
-        sums = []
-        for lane in range(0, step, LANES):
-            part = power[:, lane : lane + LANES]
-            part = part + pltpu.roll(part, LANES - 1, 1)
-            sums.append(part + pltpu.roll(part, LANES - 2, 1))
-        picking = (channel + j * step == group * CHAN_SUM).astype(jnp.bfloat16)
-        summed = jnp.concatenate(sums, axis=1).astype(jnp.bfloat16)
-        total += jnp.dot(summed, picking, preferred_element_type=jnp.float32)
-    pieces = width // CHAN_SUM // LANES
-    for h in range(pieces):
-        scratch[pl.ds(h, FEEDS, stride=pieces), :] = total[:, h * LANES : (h + 1) * LANES]
+    for t in range(pair):
+        total = jnp.zeros((FEEDS, width // CHAN_SUM), jnp.float32)
+        for j in range(width // step):
+            cols = slice(j * step, (j + 1) * step)
+            x = jnp.concatenate([part[t, core, :, cols] for part in parts for core in range(CORES)], axis=0)
+            formed = jnp.dot(matrix_ref[...], x, preferred_element_type=jnp.float32)
+            power = formed[:FEEDS] * formed[:FEEDS] + formed[FEEDS:] * formed[FEEDS:]
+            sums = []
+            for lane in range(0, step, LANES):
+                part = power[:, lane : lane + LANES]
+                part = part + pltpu.roll(part, LANES - 1, 1)
+                sums.append(part + pltpu.roll(part, LANES - 2, 1))
+            picking = (channel + j * step == group * CHAN_SUM).astype(jnp.bfloat16)
+            summed = jnp.concatenate(sums, axis=1).astype(jnp.bfloat16)
+            total += jnp.dot(summed, picking, preferred_element_type=jnp.float32)
+        scratch[pl.ds(t, FEEDS, stride=pair), :] = total
     out_ref[...] = scratch[...].astype(jnp.bfloat16)
 
 
-def detect(received, matrix):
-    shape = (FEEDS * received.shape[1] // CHAN_SUM // LANES, LANES)
+def detect(parts, matrix):
+    shape = (FEEDS * parts[0].shape[0], parts[0].shape[3] // CHAN_SUM)
     return pl.pallas_call(
         detect_kernel,
         out_shape=jax.ShapeDtypeStruct(shape, jnp.bfloat16),
         scratch_shapes=[pltpu.VMEM(shape, jnp.float32)],
         compiler_params=pltpu.CompilerParams(vmem_limit_bytes=16 * MIB),
         name="detect",
-    )(matrix, received)
+    )(matrix, *parts)
 
 
 def shifted(rows, bits):
@@ -167,7 +199,7 @@
         for piece in range(pieces):
             rows = []
             for t in range(samples):
-                first = group * 8 * samples * pieces + t * pieces + piece
+                first = (group * 8 * samples + t // 2 * 2 + piece) * pieces + t % 2
                 rows.append(wide[pl.ds(first, 8, stride=samples * pieces), :])
             mean = functools.reduce(jnp.add, rows) * (1.0 / samples)
             rows = [row - mean for row in rows]
@@ -272,37 +304,41 @@
     )(widths, series)
 
 
-def gathered(block, axis):
-    count = lax.axis_size(axis)
-    position = lax.axis_index(axis)
-    whole = block[None]
-    step = 1
-    while step < count:
-        parts = [whole]
-        for k in range(1, 4):
-            parts.append(lax.ppermute(whole, axis, [(i, i ^ k * step) for i in range(count)]))
-        for bit in (1, 2):
-            odd = position & bit * step != 0
-            parts = [jnp.where(odd, parts[k ^ bit], parts[k]) for k in range(4)]
-        whole = jnp.concatenate(parts)
-        step *= 4
-    return whole
-
-
 def exchanged(block, axes):
     return lax.all_to_all(block, axes, split_axis=0, concat_axis=0, tiled=True)
 
 
+def travelled(messages):
+    groups = lax.axis_size("beam")
+    chips = len(messages)
+
+    def sent(block, distance):
+        return lax.ppermute(block, "beam", [(i, (i + distance * CORES) % groups) for i in range(groups)])
+
+    got = list(messages)
+    for k in [2, chips - 2] + list(range(3, chips - 2)):
+        got[k] = sent(messages[k], k)
+    near = lax.optimization_barrier((messages[1], messages[-1], got[2], got[-2]))
+    got[1], got[-1], got[2], got[-2] = sent(near[0], 1), sent(near[1], chips - 1), near[2], near[3]
+    return got
+
+
 def shards(voltages, gains, shifts, widths):
     groups = lax.axis_size("beam")
-    received = exchanged(calibrate(voltages, gains), "beam")
-    matrix, shifts = lax.optimization_barrier((steering(groups), shifts))
-    table = jnp.transpose(gathered(shifts, "freq"), (1, 0, 2))
-    early = (matrix, table, jnp.maximum(widths, 1))
-    received, matrix, table, reach = lax.optimization_barrier((received, *early))
-    detected = detect(received.reshape(2 * FEEDS, received.shape[2]), matrix)
+    place = lax.axis_index("beam").astype(jnp.int32)
+    chip, core = place >> 1, place & 1
+    where = jnp.stack([chip, core])
+    padded = jnp.concatenate([shifts, jnp.zeros((64 - shifts.shape[0], shifts.shape[1]), jnp.int32)])
+    table = lax.all_gather(padded, "freq")[:, : shifts.shape[0]]
+    swap = [(i, i ^ 1) for i in range(groups)]
+    other = [lax.ppermute(block, "beam", swap) for block in (voltages, gains)]
+    messages = calibrate(where, *other, calibrate(where, voltages, gains))
+    received = travelled(messages)
+    early = (steering(groups, chip), jnp.maximum(widths, 1))
+    received, matrix, reach = lax.optimization_barrier((received, *early))
+    detected = detect(received, matrix)
     spread = exchanged(detected.reshape(FEEDS, -1, LANES), ("freq", "beam"))
-    series = exchanged(tree(spread.reshape(detected.shape), table), "freq")
+    series = exchanged(tree(spread.reshape(detected.shape), jnp.transpose(table, (1, 0, 2))), "freq")
     return tuple(peaks(reach, series))
 
 

time: 77.5 us -> 101 us (1.30)
  blocking collectives: 31.7 us -> 9.81 us
  starting transfers between devices: 17.1 us -> 31.8 us
  between operations: 0.77 us -> 14.3 us
  waiting for transfers between devices: 14.2 us -> 23.3 us
  local copies, waits for them, and re-layouts: 0.02 us -> 3.49 us
  other arithmetic: 6.4 us -> 9.24 us
  Pallas kernels: 7 us -> 9.08 us
    all_to_all x2 -> x1, blocking collectives: 31.7 us -> 9.81 us  [exchanged(): return lax.all_to_all(block, axes, split_axis=0, concat_axis=0, tiled=True)]
    ppermute x6 -> x9, starting transfers between devices: 7.14 us -> 19.6 us  [the longest x7 16.1 us: sent(): lax.ppermute(block, 'beam', [(i, (i + distance * CORES) % groups) for i i...]
    all_to_all x1, waiting for transfers between devices: 7.09 us -> 11.7 us  [exchanged(): return lax.all_to_all(block, axes, split_axis=0, concat_axis=0, tiled=True)]
    ppermute x6 -> x9, waiting for transfers between devices: 7.14 us -> 11.6 us  [the longest x7 11.6 us: sent(): lax.ppermute(block, 'beam', [(i, (i + distance * CORES) % groups) for i i...]
    convert_element_type x1 -> x4, other arithmetic: 6.08 us -> 8.48 us  [steering(): (whole_cosine * cosine - whole_sine * sine).astype(jnp.bfloat16)]
    all_to_all x1, starting transfers between devices: 9.99 us -> 12.2 us  [exchanged(): return lax.all_to_all(block, axes, split_axis=0, concat_axis=0, tiled=True)]
    pallas_call x1 -> x2, Pallas kernels: 2.42 us -> 4.03 us  [calibrate(): pl.pallas_call(functools.partial(calibrate_kernel, own=own), in_specs=[pl...]
    concatenate x0 -> x1, local copies, waits for them, and re-layouts: none -> 1.35 us  [shards(): jnp.concatenate([shifts, jnp.zeros((64 - shifts.shape[0], shifts.shape[1]...]
  transfers between devices with their start and end apart: 7 -> 11, of which waited for: 6 -> 6; matrix products, arithmetic and copies ran while one was open for 8% -> 12% of each run, Pallas kernels for 0% -> 6%
where the time goes in v5:
time: 101 us
  starting transfers between devices  31.8 us (31%)
  waiting for transfers between devices  23.3 us (23%)
  between operations  14.3 us (14%)
  blocking collectives  9.81 us (10%)
  other arithmetic  9.24 us (9%)
  Pallas kernels  9.08 us (9%)
  local copies, waits for them, and re-layouts  3.49 us (3%)
    ppermute x7, starting transfers between devices, sent(): lax.ppermute(block, 'beam', [(i, (i + distance * CORES) % groups) for i i...  16.1 us
    all_to_all x1, starting transfers between devices, exchanged(): return lax.all_to_all(block, axes, split_axis=0, concat_axis=0, tiled=True)  12.2 us
    all_to_all x1, waiting for transfers between devices, exchanged(): return lax.all_to_all(block, axes, split_axis=0, concat_axis=0, tiled=True)  11.7 us
    ppermute x7, waiting for transfers between devices, sent(): lax.ppermute(block, 'beam', [(i, (i + distance * CORES) % groups) for i i...  11.6 us
    all_to_all x1, blocking collectives, exchanged(): return lax.all_to_all(block, axes, split_axis=0, concat_axis=0, tiled=True)  9.81 us
    convert_element_type x4, other arithmetic, steering(): (whole_cosine * cosine - whole_sine * sine).astype(jnp.bfloat16)  8.48 us
    pallas_call x2, Pallas kernels, calibrate(): pl.pallas_call(functools.partial(calibrate_kernel, own=own), in_specs=[pl...  4.03 us
    ppermute x2, starting transfers between devices, shards(): other = [lax.ppermute(block, 'beam', swap) for block in (voltages, gains)]  3.43 us
  transfers between devices with their start and end apart: 11, of which 6 were waited for; matrix products, arithmetic and copies ran while one was open for 12% of the time, Pallas kernels for 6%

profile of v5, /device:TPU:1, one launch (start us, length us, event | category | flops | bytes accessed | tf_op | source)
XLA Modules:
  0.0 101.0 jit_solution(14318787897594019889)
XLA Ops:
  7.2 3.3 %collective-permute-start = (bf16[2,16,16,1024]{3,2,1,0:T(8,128)(2,1)}, bf16[2,16,16,1024]{3,2,1,0:T(8,128)(2,1)S(1)}, u32[]{:S(2)}, u32[]{:S(2)}) collective-permute-start(bf16[2,16,16,1024]{3,2,1,0:T(8,128)(2,1)} %volt_hbm.1), channel_id=1, source_target_pairs={{0,1},{1,0},{2,3},{3,2},{4,5},{5,4},{6,7},{7,6},{8,9},{9,8},{10,11... | collective-permute-start | bytes 3145736 | tf_op jit(solution)/shard_map/ppermute | solution.py:334
  10.6 1.4 %concatenate.7 = s32[64,256]{1,0:T(8,128)} pad(s32[12,256]{1,0:T(8,128)} %param.6, s32[]{:T(128)} %constant.212.clone.1), padding=0_52x0_0 | pad | bytes 77828 | tf_op jit(solution)/shard_map/concatenate | solution.py:331
  12.2 2.1 %fusion.39 = bf16[512,128]{1,0:T(8,128)(2,1)S(1)} fusion(s32[128]{0:T(128)S(1)} %get-tuple-element.61, s32[128]{0:T(128)S(1)} %get-tuple-element.65, s32[]{:T(128)} %shift_right_arithmetic.3, s32[512]{0:T(512)S(1)} %get-tuple-element.47, s32[512]{0:T(512)S(1)} %get-tuple-element.50, pred[512]{0:T(512)(128)(4,1)S(1)} %get-tuple-element.53, ...), kind=kLoop, calls=%fused_computation.109 | loop fusion | flops 8126464 | bytes 149508 | tf_op jit(solution)/shard_map/convert_element_type | solution.py:41
  14.3 2.1 %fusion.31 = bf16[512,128]{1,0:T(8,128)(2,1)S(1)} fusion(s32[128]{0:T(128)S(1)} %get-tuple-element.61, s32[128]{0:T(128)S(1)} %get-tuple-element.65, s32[]{:T(128)} %shift_right_arithmetic.3, s32[512]{0:T(512)S(1)} %get-tuple-element.47, s32[512]{0:T(512)S(1)} %get-tuple-element.50, pred[512]{0:T(512)(128)(4,1)S(1)} %get-tuple-element.53, ...), kind=kLoop, calls=%fused_computation.101 | loop fusion | flops 8126464 | bytes 149508 | tf_op jit(solution)/shard_map/convert_element_type | solution.py:41
  16.4 2.1 %fusion.23 = bf16[512,128]{1,0:T(8,128)(2,1)S(1)} fusion(s32[128]{0:T(128)S(1)} %get-tuple-element.61, s32[128]{0:T(128)S(1)} %get-tuple-element.65, s32[]{:T(128)} %shift_right_arithmetic.3, s32[512]{0:T(512)S(1)} %get-tuple-element.47, s32[512]{0:T(512)S(1)} %get-tuple-element.50, pred[512]{0:T(512)(128)(4,1)S(1)} %get-tuple-element.53, ...), kind=kLoop, calls=%fused_computation.93 | loop fusion | flops 8126464 | bytes 149508 | tf_op jit(solution)/shard_map/convert_element_type | solution.py:41
  19.2 2.9 %calibrate.2.rest_0_ = bf16[16,32,512]{2,1,0:T(8,128)(2,1)} custom-call(s32[2]{0:T(128)} %pad_add_fusion.where_ref, bf16[2,16,16,1024]{3,2,1,0:T(8,128)(2,1)} %volt_hbm.1, f32[2,16,1024]{2,1,0:T(8,128)} %gain_hbm.1), custom_call_target="tpu_custom_call" | custom-call | tf_op jit(solution)/shard_map/calibrate/pallas_call | solution.py:108
  23.2 1.1 %calibrate.3 = (bf16[2,2,32,512]{3,2,1,0:T(8,128)(2,1)S(1)}, bf16[2,2,32,512]{3,2,1,0:T(8,128)(2,1)S(1)}, bf16[2,2,32,512]{3,2,1,0:T(8,128)(2,1)S(1)}, bf16[2,2,...) custom-call(s32[2]{0:T(128)S(1)} %copy-done.1, ...), custom_call_target="tpu_custom_call" | custom-call | tf_op jit(solution)/shard_map/calibrate/pallas_call | solution.py:108
  24.3 1.3 %collective-permute-start.2 = (bf16[2,2,32,512]{3,2,1,0:T(8,128)(2,1)S(1)}, bf16[2,2,32,512]{3,2,1,0:T(8,128)(2,1)S(1)}, u32[]{:S(2)}, u32[]{:S(2)}) collective-permute-start(bf16[2,2,32,512]{3,2,1,0:T(8,128)(2,1)S(1)} %get-tuple-element.27), channel_id=1, source_target_pairs={{0,4},{1,5},{2,6},{3,7},{4,8},{5,9},{6,10},{7,11},{8,12},{9,13},{1... | collective-permute-start | bytes 393224 | tf_op jit(solution)/shard_map/ppermute | solution.py:316
  25.7 3.1 %collective-permute-start.3 = (bf16[2,2,32,512]{3,2,1,0:T(8,128)(2,1)S(1)}, bf16[2,2,32,512]{3,2,1,0:T(8,128)(2,1)S(1)}, u32[]{:S(2)}, u32[]{:S(2)}) collective-permute-start(bf16[2,2,32,512]{3,2,1,0:T(8,128)(2,1)S(1)} %get-tuple-element.28), channel_id=1, source_target_pairs={{0,12},{1,13},{2,14},{3,15},{4,0},{5,1},{6,2},{7,3},{8,4},{9,5},{1... | collective-permute-start | bytes 393224 | tf_op jit(solution)/shard_map/ppermute | solution.py:316
  28.8 2.1 %fusion.6 = bf16[512,128]{1,0:T(8,128)(2,1)S(1)} fusion(s32[128]{0:T(128)S(1)} %get-tuple-element.61, s32[128]{0:T(128)S(1)} %get-tuple-element.65, s32[]{:T(128)} %shift_right_arithmetic.3, s32[512]{0:T(512)S(1)} %get-tuple-element.47, s32[512]{0:T(512)S(1)} %get-tuple-element.50, pred[512]{0:T(512)(128)(4,1)S(1)} %get-tuple-element.53, ...), kind=kLoop, calls=%fused_computation.76 | loop fusion | flops 8060928 | bytes 149508 | tf_op jit(solution)/shard_map/convert_element_type | solution.py:41
  30.9 1.6 %collective-permute-start.5 = (bf16[2,2,32,512]{3,2,1,0:T(8,128)(2,1)S(1)}, bf16[2,2,32,512]{3,2,1,0:T(8,128)(2,1)S(1)}, u32[]{:S(2)}, u32[]{:S(2)}) collective-permute-start(bf16[2,2,32,512]{3,2,1,0:T(8,128)(2,1)S(1)} %get-tuple-element.31), channel_id=1, source_target_pairs={{0,6},{1,7},{2,8},{3,9},{4,10},{5,11},{6,12},{7,13},{8,14},{9,15},... | collective-permute-start | bytes 393224 | tf_op jit(solution)/shard_map/ppermute | solution.py:316
  32.5 3.3 %collective-permute-start.6 = (bf16[2,2,32,512]{3,2,1,0:T(8,128)(2,1)S(1)}, bf16[2,2,32,512]{3,2,1,0:T(8,128)(2,1)S(1)}, u32[]{:S(2)}, u32[]{:S(2)}) collective-permute-start(bf16[2,2,32,512]{3,2,1,0:T(8,128)(2,1)S(1)} %get-tuple-element.32), channel_id=1, source_target_pairs={{0,8},{1,9},{2,10},{3,11},{4,12},{5,13},{6,14},{7,15},{8,0},{9,1},... | collective-permute-start | bytes 393224 | tf_op jit(solution)/shard_map/ppermute | solution.py:316
  35.8 4.0 %collective-permute-start.7 = (bf16[2,2,32,512]{3,2,1,0:T(8,128)(2,1)S(1)}, bf16[2,2,32,512]{3,2,1,0:T(8,128)(2,1)S(1)}, u32[]{:S(2)}, u32[]{:S(2)}) collective-permute-start(bf16[2,2,32,512]{3,2,1,0:T(8,128)(2,1)S(1)} %get-tuple-element.33), channel_id=1, source_target_pairs={{0,10},{1,11},{2,12},{3,13},{4,14},{5,15},{6,0},{7,1},{8,2},{9,3},... | collective-permute-start | bytes 393224 | tf_op jit(solution)/shard_map/ppermute | solution.py:316
  40.6 1.9 %collective-permute-start.8 = (bf16[2,2,32,512]{3,2,1,0:T(8,128)(2,1)S(1)}, bf16[2,2,32,512]{3,2,1,0:T(8,128)(2,1)S(1)}, u32[]{:S(2)}, u32[]{:S(2)}) collective-permute-start(bf16[2,2,32,512]{3,2,1,0:T(8,128)(2,1)S(1)} %get-tuple-element.35), channel_id=1, source_target_pairs={{0,14},{1,15},{2,0},{3,1},{4,2},{5,3},{6,4},{7,5},{8,6},{9,7},{10,... | collective-permute-start | bytes 393224 | tf_op jit(solution)/shard_map/ppermute | solution.py:316
  43.2 5.0 %collective-permute-done.6.rest_4_ = bf16[2,2,32,512]{3,2,1,0:T(8,128)(2,1)S(1)} collective-permute-done((bf16[2,2,32,512]{3,2,1,0:T(8,128)(2,1)S(1)}, bf16[2,2,32,512]{3,2,1,0:T(8,128)(2,1)S(1)}, u32[]{:S(2)}, u32[]{:S(2)}) %collective-permute-start.6) | collective-permute-done | bytes 131104 | tf_op jit(solution)/shard_map/ppermute | solution.py:316
  48.2 1.3 %collective-permute-done.7.rest_5_ = bf16[2,2,32,512]{3,2,1,0:T(8,128)(2,1)S(1)} collective-permute-done((bf16[2,2,32,512]{3,2,1,0:T(8,128)(2,1)S(1)}, bf16[2,2,32,512]{3,2,1,0:T(8,128)(2,1)S(1)}, u32[]{:S(2)}, u32[]{:S(2)}) %collective-permute-start.7) | collective-permute-done | bytes 131104 | tf_op jit(solution)/shard_map/ppermute | solution.py:316
  49.5 2.9 %collective-permute-done.4.rest_1_ = bf16[2,2,32,512]{3,2,1,0:T(8,128)(2,1)S(1)} collective-permute-done((bf16[2,2,32,512]{3,2,1,0:T(8,128)(2,1)S(1)}, bf16[2,2,32,512]{3,2,1,0:T(8,128)(2,1)S(1)}, u32[]{:S(2)}, u32[]{:S(2)}) %collective-permute-start.4) | collective-permute-done | bytes 131104 | tf_op jit(solution)/shard_map/ppermute | solution.py:316
  52.4 1.8 %collective-permute-done.8.rest_7_ = bf16[2,2,32,512]{3,2,1,0:T(8,128)(2,1)S(1)} collective-permute-done((bf16[2,2,32,512]{3,2,1,0:T(8,128)(2,1)S(1)}, bf16[2,2,32,512]{3,2,1,0:T(8,128)(2,1)S(1)}, u32[]{:S(2)}, u32[]{:S(2)}) %collective-permute-start.8) | collective-permute-done | bytes 131104 | tf_op jit(solution)/shard_map/ppermute | solution.py:316
  54.2 2.2 %detect.1 = bf16[512,128]{1,0:T(8,128)(2,1)} custom-call(bf16[512,512]{1,0:T(8,128)(2,1)S(1)} %pad_maximum_fusion.matrix_ref, bf16[2,2,32,512]{3,2,1,0:T(8,128)(2,1)S(1)} %get-tuple-element.38.rest_0_, bf16[2,2,32,512]{3,2,1,0:T(8,128)(2,1)S(1)} %collective-permute-done.4.rest_1_, bf16[2,2,32,512]{3,2,1,0:T(8,128)(2,1)S(1)} %collective-permute-done.2.rest_2_, ...), custom_call_target="tpu_custom_call" | custom-call | tf_op jit(solution)/shard_map/detect/pallas_call | solution.py:152
  56.4 12.2 %all-to-all-start = ((bf16[256,2,128]{2,1,0:T(2,128)(2,1)}), bf16[256,2,128]{2,1,0:T(2,128)(2,1)S(1)}, u32[]{:S(2)}, u32[]{:S(2)}) async-start(bf16[256,2,128]{2,1,0:T(2,128)(2,1)} %bitcast.2), calls=%async_computation | async-start | bytes 262144 | tf_op jit(solution)/shard_map/all_to_all | solution.py:308
  69.8 11.7 %all-to-all-done = bf16[256,2,128]{2,1,0:T(2,128)(2,1)S(1)} async-done(((bf16[256,2,128]{2,1,0:T(2,128)(2,1)}), bf16[256,2,128]{2,1,0:T(2,128)(2,1)S(1)}, u32[]{:S(2)}, u32[]{:S(2)}) %all-to-all-start) | async-done | bytes 131104 | tf_op jit(solution)/shard_map/all_to_all | solution.py:308
  81.5 1.4 %tree.1 = bf16[16,16,256]{2,1,0:T(8,128)(2,1)S(1)} custom-call(bf16[512,128]{1,0:T(8,128)(2,1)S(1)} %bitcast.9, s32[12,16,256]{2,1,0:T(8,128)S(1)} %bitcast.8), custom_call_target="tpu_custom_call" | custom-call | tf_op jit(solution)/shard_map/tree/pallas_call | solution.py:238
  82.9 9.8 %all_to_all.10.series_ref = bf16[16,16,256]{2,1,0:T(8,128)(2,1)S(1)} all-to-all(bf16[16,16,256]{2,1,0:T(8,128)(2,1)S(1)} %tree.1), channel_id=1, replica_groups=mesh['freq'=16,'beam'=16] {'freq'}, dimensions={0} | all-to-all | bytes 262144 | tf_op jit(solution)/shard_map/all_to_all | solution.py:308
  92.7 1.4 %peaks.1 = (bf16[16,16,256]{2,1,0:T(8,128)(2,1)}, f32[8,16,256]{2,1,0:T(8,128)}) custom-call(s32[8]{0:T(128)S(1)} %broadcast_maximum_fusion.widths_ref, bf16[16,16,256]{2,1,0:T(8,128)(2,1)S(1)} %all_to_all.10.series_ref), custom_call_target="tpu_custom_call" | custom-call | tf_op jit(solution)/shard_map/peaks/pallas_call | solution.py:287
  (32 shorter events, 4.5 us)
Async XLA Ops:
  7.2 61.5 %all-gather.3.cloned.1.call-start = ((), (), s32[]{:S(2)}) async-start(), calls=%async_computation.2 | async-start | bytes 1114112 | tf_op jit(solution)/shard_map/all_gather | solution.py:332
  7.2 14.9 %collective-permute-start = (bf16[2,16,16,1024]{3,2,1,0:T(8,128)(2,1)}, bf16[2,16,16,1024]{3,2,1,0:T(8,128)(2,1)S(1)}, u32[]{:S(2)}, u32[]{:S(2)}) collective-permute-start(bf16[2,16,16,1024]{3,2,1,0:T(8,128)(2,1)} %volt_hbm.1), channel_id=1, source_target_pairs={{0,1},{1,0},{2,3},{3,2},{4,5},{5,4},{6,7},{7,6},{8,9},{9,8},{10,11... | collective-permute-start | bytes 3145736 | tf_op jit(solution)/shard_map/ppermute | solution.py:334
  10.5 11.6 %collective-permute-start.1 = (f32[2,16,1024]{2,1,0:T(8,128)}, f32[2,16,1024]{2,1,0:T(8,128)S(1)}, u32[]{:S(2)}, u32[]{:S(2)}) collective-permute-start(f32[2,16,1024]{2,1,0:T(8,128)} %gain_hbm.1), channel_id=1, source_target_pairs={{0,1},{1,0},{2,3},{3,2},{4,5},{5,4},{6,7},{7,6},{8,9},{9,8},{10,11... | collective-permute-start | bytes 393224 | tf_op jit(solution)/shard_map/ppermute | solution.py:334
  19.2 2.9 %copy-start.1 = (s32[2]{0:T(128)S(1)}, s32[2]{0:T(128)}, u32[]{:S(2)}) copy-start(s32[2]{0:T(128)} %pad_add_fusion.where_ref) | copy-start | bytes 28
  22.2 1.0 %copy-start = (bf16[16,32,512]{2,1,0:T(8,128)(2,1)S(1)}, bf16[16,32,512]{2,1,0:T(8,128)(2,1)}, u32[]{:S(2)}) copy-start(bf16[16,32,512]{2,1,0:T(8,128)(2,1)} %calibrate.2.rest_0_) | copy-start | bytes 1572868
  24.3 15.5 %collective-permute-start.2 = (bf16[2,2,32,512]{3,2,1,0:T(8,128)(2,1)S(1)}, bf16[2,2,32,512]{3,2,1,0:T(8,128)(2,1)S(1)}, u32[]{:S(2)}, u32[]{:S(2)}) collective-permute-start(bf16[2,2,32,512]{3,2,1,0:T(8,128)(2,1)S(1)} %get-tuple-element.27), channel_id=1, source_target_pairs={{0,4},{1,5},{2,6},{3,7},{4,8},{5,9},{6,10},{7,11},{8,12},{9,13},{1... | collective-permute-start | bytes 393224 | tf_op jit(solution)/shard_map/ppermute | solution.py:316
  25.7 14.1 %collective-permute-start.3 = (bf16[2,2,32,512]{3,2,1,0:T(8,128)(2,1)S(1)}, bf16[2,2,32,512]{3,2,1,0:T(8,128)(2,1)S(1)}, u32[]{:S(2)}, u32[]{:S(2)}) collective-permute-start(bf16[2,2,32,512]{3,2,1,0:T(8,128)(2,1)S(1)} %get-tuple-element.28), channel_id=1, source_target_pairs={{0,12},{1,13},{2,14},{3,15},{4,0},{5,1},{6,2},{7,3},{8,4},{9,5},{1... | collective-permute-start | bytes 393224 | tf_op jit(solution)/shard_map/ppermute | solution.py:316
  30.9 12.3 %collective-permute-start.5 = (bf16[2,2,32,512]{3,2,1,0:T(8,128)(2,1)S(1)}, bf16[2,2,32,512]{3,2,1,0:T(8,128)(2,1)S(1)}, u32[]{:S(2)}, u32[]{:S(2)}) collective-permute-start(bf16[2,2,32,512]{3,2,1,0:T(8,128)(2,1)S(1)} %get-tuple-element.31), channel_id=1, source_target_pairs={{0,6},{1,7},{2,8},{3,9},{4,10},{5,11},{6,12},{7,13},{8,14},{9,15},... | collective-permute-start | bytes 393224 | tf_op jit(solution)/shard_map/ppermute | solution.py:316
  32.5 15.7 %collective-permute-start.6 = (bf16[2,2,32,512]{3,2,1,0:T(8,128)(2,1)S(1)}, bf16[2,2,32,512]{3,2,1,0:T(8,128)(2,1)S(1)}, u32[]{:S(2)}, u32[]{:S(2)}) collective-permute-start(bf16[2,2,32,512]{3,2,1,0:T(8,128)(2,1)S(1)} %get-tuple-element.32), channel_id=1, source_target_pairs={{0,8},{1,9},{2,10},{3,11},{4,12},{5,13},{6,14},{7,15},{8,0},{9,1},... | collective-permute-start | bytes 393224 | tf_op jit(solution)/shard_map/ppermute | solution.py:316
  35.8 13.7 %collective-permute-start.7 = (bf16[2,2,32,512]{3,2,1,0:T(8,128)(2,1)S(1)}, bf16[2,2,32,512]{3,2,1,0:T(8,128)(2,1)S(1)}, u32[]{:S(2)}, u32[]{:S(2)}) collective-permute-start(bf16[2,2,32,512]{3,2,1,0:T(8,128)(2,1)S(1)} %get-tuple-element.33), channel_id=1, source_target_pairs={{0,10},{1,11},{2,12},{3,13},{4,14},{5,15},{6,0},{7,1},{8,2},{9,3},... | collective-permute-start | bytes 393224 | tf_op jit(solution)/shard_map/ppermute | solution.py:316
  39.8 2.8 %copy-start.2 = (s32[8]{0:T(128)S(1)}, s32[8]{0:T(128)}, u32[]{:S(2)}) copy-start(s32[8]{0:T(128)} %param.7) | copy-start | bytes 100
  39.8 12.6 %collective-permute-start.4 = (bf16[2,2,32,512]{3,2,1,0:T(8,128)(2,1)S(1)}, bf16[2,2,32,512]{3,2,1,0:T(8,128)(2,1)S(1)}, u32[]{:S(2)}, u32[]{:S(2)}) collective-permute-start(bf16[2,2,32,512]{3,2,1,0:T(8,128)(2,1)S(1)} %get-tuple-element.29), channel_id=1, source_target_pairs={{0,2},{1,3},{2,4},{3,5},{4,6},{5,7},{6,8},{7,9},{8,10},{9,11},{10,... | collective-permute-start | bytes 393224 | tf_op jit(solution)/shard_map/ppermute | solution.py:316
  40.6 13.6 %collective-permute-start.8 = (bf16[2,2,32,512]{3,2,1,0:T(8,128)(2,1)S(1)}, bf16[2,2,32,512]{3,2,1,0:T(8,128)(2,1)S(1)}, u32[]{:S(2)}, u32[]{:S(2)}) collective-permute-start(bf16[2,2,32,512]{3,2,1,0:T(8,128)(2,1)S(1)} %get-tuple-element.35), channel_id=1, source_target_pairs={{0,14},{1,15},{2,0},{3,1},{4,2},{5,3},{6,4},{7,5},{8,6},{9,7},{10,... | collective-permute-start | bytes 393224 | tf_op jit(solution)/shard_map/ppermute | solution.py:316
  56.4 25.0 %all-to-all-start = ((bf16[256,2,128]{2,1,0:T(2,128)(2,1)}), bf16[256,2,128]{2,1,0:T(2,128)(2,1)S(1)}, u32[]{:S(2)}, u32[]{:S(2)}) async-start(bf16[256,2,128]{2,1,0:T(2,128)(2,1)} %bitcast.2), calls=%async_computation | async-start | bytes 262144 | tf_op jit(solution)/shard_map/all_to_all | solution.py:308
Sparse Core Ops, SparseCore 0:
  12.1 48.9 all-gather.2

commit v6 on v5

--- a/solution.py
+++ b/solution.py
@@ -28,10 +28,10 @@
     beam = row % groups * size + row % FEEDS // groups
     rest = col // (2 * size) % CORES * size + col % size
     quarters = out_part - col // size % 2
-    angles = (beam * rest + quarters * (FEEDS // 4) & FEEDS - 1).astype(jnp.float32) * (2.0 * math.pi / FEEDS)
+    phase = beam * rest + quarters * (FEEDS // 4) + chip * FEEDS & FEEDS - 1
+    angles = phase.astype(jnp.float32) * (2.0 * math.pi / FEEDS)
     factor = 1.0 / math.sqrt(FEEDS)
-    cosine = jnp.cos(angles) * factor
-    sine = jnp.sin(angles) * factor
+    cosine, sine = lax.optimization_barrier((jnp.cos(angles) * factor, jnp.sin(angles) * factor))
     blocks = []
     for first in range(0, chips, LANES // (2 * span)):
         source = chip - (first + col // (2 * span)) & chips - 1
@@ -48,13 +48,13 @@
 
 
 def calibrate_kernel(where_ref, volt_hbm, gain_hbm, *rest, own):
-    if own:
-        outs, rest = rest[:1], rest[1:]
-    else:
-        begun_ref, outs, rest = rest[0], rest[1:9], rest[9:]
-    volt, gain, wide, in_sems = rest
+    volt, gain, wide, in_sems, sems = rest[-5:]
     chunks, _, feeds, samples, _ = volt.shape
     chip, core = where_ref[0], where_ref[1]
+    if own:
+        out_hbm, done = rest[:2]
+    else:
+        begun_hbm, outs = rest[0], rest[1 : 1 + samples // 2]
 
     def arriving(j):
         lanes = pl.ds(pl.multiple_of((core * chunks + j) * LANES, LANES), LANES)
@@ -63,13 +63,19 @@
             pltpu.make_async_copy(gain_hbm.at[:, :, lanes], gain.at[j], in_sems.at[1, j]),
         )
 
+    def leaving(j):
+        return pltpu.make_async_copy(done.at[j], out_hbm.at[:, :, pl.ds(j * LANES, LANES)], sems.at[j])
+
+    def joining(k):
+        pair = begun_hbm.at[pl.ds(2 * (chip + k & samples // 2 - 1), 2)]
+        return pltpu.make_async_copy(pair, outs[k].at[:, core], sems.at[k])
+
     for j in range(chunks):
         for copy in arriving(j):
             copy.start()
     if not own:
-        for k, out in enumerate(outs):
-            for t in range(2):
-                out[t, core] = begun_ref[2 * (chip + k & len(outs) - 1) + t]
+        for k in range(len(outs)):
+            joining(k).start()
     for j in range(chunks):
         lanes = slice(j * LANES, (j + 1) * LANES)
         for copy in arriving(j):
@@ -88,11 +94,19 @@
                 real = (gain_re * volt_re - gain_im * volt_im).astype(jnp.bfloat16)
                 imag = (gain_re * volt_im + gain_im * volt_re).astype(jnp.bfloat16)
                 if own:
-                    outs[0][sample, :feeds, lanes] = real
-                    outs[0][sample, feeds:, lanes] = imag
+                    done[j, sample, :feeds] = real
+                    done[j, sample, feeds:] = imag
                 else:
                     outs[k][t, 1 - core, :feeds, lanes] = real
                     outs[k][t, 1 - core, feeds:, lanes] = imag
+        if own:
+            leaving(j).start()
+    if own:
+        for j in range(chunks):
+            leaving(j).wait()
+    else:
+        for k in range(len(outs)):
+            joining(k).wait()
 
 
 def calibrate(where, voltages, gains, begun=None):
@@ -102,22 +116,25 @@
     shape = (samples, 2 * feeds, width // CORES)
     if own:
         out_shape = jax.ShapeDtypeStruct(shape, jnp.bfloat16)
+        out_specs = pl.BlockSpec(memory_space=pltpu.HBM)
     else:
         out_shape = [jax.ShapeDtypeStruct((2, CORES) + shape[1:], jnp.bfloat16)] * (samples // 2)
+        out_specs = [pl.BlockSpec(memory_space=pltpu.VMEM)] * (samples // 2)
     operands = (where, voltages, gains) + (() if own else (begun,))
     return pl.pallas_call(
         functools.partial(calibrate_kernel, own=own),
-        in_specs=[pl.BlockSpec(memory_space=pltpu.SMEM)]
-        + [pl.BlockSpec(memory_space=pl.ANY)] * 2
-        + [pl.BlockSpec(memory_space=pltpu.VMEM)] * (not own),
+        in_specs=[pl.BlockSpec(memory_space=pltpu.SMEM)] + [pl.BlockSpec(memory_space=pl.ANY)] * (len(operands) - 1),
+        out_specs=out_specs,
         out_shape=out_shape,
-        scratch_shapes=[
+        scratch_shapes=[pltpu.VMEM((chunks, samples, 2 * feeds, LANES), jnp.bfloat16)] * own
+        + [
             pltpu.VMEM((chunks, 2, feeds, samples, LANES), jnp.bfloat16),
             pltpu.VMEM((chunks, 2, feeds, LANES), jnp.float32),
             pltpu.VMEM((chunks, 2, feeds * PITCH, LANES), jnp.float32),
             pltpu.SemaphoreType.DMA((2, chunks)),
+            pltpu.SemaphoreType.DMA((chunks if own else samples // 2,)),
         ],
-        compiler_params=pltpu.CompilerParams(vmem_limit_bytes=(58 if own else 16) * MIB),
+        compiler_params=pltpu.CompilerParams(vmem_limit_bytes=(58 if own else 8) * MIB),
         name="calibrate",
     )(*operands)
 
@@ -126,24 +143,23 @@
     parts, (out_ref, scratch) = rest[:-2], rest[-2:]
     pair, _, _, width = parts[0].shape
     step = 256
-    channel = lax.broadcasted_iota(jnp.int32, (step, width // CHAN_SUM), 0)
-    group = lax.broadcasted_iota(jnp.int32, (step, width // CHAN_SUM), 1)
+    groups = width // CHAN_SUM
+    channel = lax.broadcasted_iota(jnp.int32, (width, groups), 0)
+    picking = channel == lax.broadcasted_iota(jnp.int32, (width, groups), 1) * CHAN_SUM
+    picking = picking.astype(jnp.bfloat16)
     for t in range(pair):
-        total = jnp.zeros((FEEDS, width // CHAN_SUM), jnp.float32)
-        for j in range(width // step):
-            cols = slice(j * step, (j + 1) * step)
+        sums = []
+        for first in range(0, width, step):
+            cols = slice(first, first + step)
             x = jnp.concatenate([part[t, core, :, cols] for part in parts for core in range(CORES)], axis=0)
             formed = jnp.dot(matrix_ref[...], x, preferred_element_type=jnp.float32)
             power = formed[:FEEDS] * formed[:FEEDS] + formed[FEEDS:] * formed[FEEDS:]
-            sums = []
             for lane in range(0, step, LANES):
                 part = power[:, lane : lane + LANES]
                 part = part + pltpu.roll(part, LANES - 1, 1)
-                sums.append(part + pltpu.roll(part, LANES - 2, 1))
-            picking = (channel + j * step == group * CHAN_SUM).astype(jnp.bfloat16)
-            summed = jnp.concatenate(sums, axis=1).astype(jnp.bfloat16)
-            total += jnp.dot(summed, picking, preferred_element_type=jnp.float32)
-        scratch[pl.ds(t, FEEDS, stride=pair), :] = total
+                sums.append((part + pltpu.roll(part, LANES - 2, 1)).astype(jnp.bfloat16))
+        summed = jnp.concatenate(sums, axis=1)
+        scratch[pl.ds(t, FEEDS, stride=pair), :] = jnp.dot(summed, picking, preferred_element_type=jnp.float32)
     out_ref[...] = scratch[...].astype(jnp.bfloat16)
 
 
@@ -188,7 +204,10 @@
     blocks, samples, width = out_ref.shape
     pieces = width // LANES
     scale = 1.0 / (8.0 * math.sqrt(NSUB))
-    wide[...] = detected_ref[...].astype(jnp.float32)
+    length = samples * pieces
+    pitch = length + 8
+    for q in range(blocks):
+        wide[q * pitch : q * pitch + length] = detected_ref[q * length : (q + 1) * length].astype(jnp.float32)
 
     def bits_of(section, group, piece):
         offsets = shifts_ref[section, group * 8 : (group + 1) * 8, piece * LANES : (piece + 1) * LANES]
@@ -199,8 +218,8 @@
         for piece in range(pieces):
             rows = []
             for t in range(samples):
-                first = (group * 8 * samples + t // 2 * 2 + piece) * pieces + t % 2
-                rows.append(wide[pl.ds(first, 8, stride=samples * pieces), :])
+                first = group * 8 * pitch + t // 2 * 4 + piece * 2 + t % 2
+                rows.append(wide[pl.ds(first, 8, stride=pitch), :])
             mean = functools.reduce(jnp.add, rows) * (1.0 / samples)
             rows = [row - mean for row in rows]
             for section in range(lane_bits):
@@ -226,9 +245,10 @@
         for group in range(2):
             rows = merged(parts[0], parts[1], bits_of(lane_bits + 4, group, piece))
             for t in range(samples):
-                turned[piece, pl.ds(group * 8 * samples + t, 8, stride=samples), :] = rows[t] * scale
-        block = turned[piece].reshape(blocks, samples, LANES)
-        out_ref[:, :, piece * LANES : (piece + 1) * LANES] = block.astype(jnp.bfloat16)
+                turned[piece, pl.ds(group * 8 * PITCH + t, 8, stride=PITCH), :] = rows[t] * scale
+        for q in range(blocks):
+            block = turned[piece, q * PITCH : q * PITCH + samples, :]
+            out_ref[q, :, piece * LANES : (piece + 1) * LANES] = block.astype(jnp.bfloat16)
 
 
 def tree(detected, shifts):
@@ -239,9 +259,9 @@
         tree_kernel,
         out_shape=jax.ShapeDtypeStruct((blocks, TIME, width), jnp.bfloat16),
         scratch_shapes=[
-            pltpu.VMEM((rows, LANES), jnp.float32),
+            pltpu.VMEM((rows + 8 * blocks, LANES), jnp.float32),
             pltpu.VMEM((pieces, blocks // 8, TIME, 8, LANES), jnp.float32),
-            pltpu.VMEM((pieces, blocks * TIME, LANES), jnp.float32),
+            pltpu.VMEM((pieces, blocks * PITCH, LANES), jnp.float32),
         ],
         compiler_params=pltpu.CompilerParams(vmem_limit_bytes=8 * MIB),
         name="tree",
@@ -308,37 +328,32 @@
     return lax.all_to_all(block, axes, split_axis=0, concat_axis=0, tiled=True)
 
 
-def travelled(messages):
-    groups = lax.axis_size("beam")
-    chips = len(messages)
-
-    def sent(block, distance):
-        return lax.ppermute(block, "beam", [(i, (i + distance * CORES) % groups) for i in range(groups)])
-
-    got = list(messages)
-    for k in [2, chips - 2] + list(range(3, chips - 2)):
-        got[k] = sent(messages[k], k)
-    near = lax.optimization_barrier((messages[1], messages[-1], got[2], got[-2]))
-    got[1], got[-1], got[2], got[-2] = sent(near[0], 1), sent(near[1], chips - 1), near[2], near[3]
-    return got
-
-
 def shards(voltages, gains, shifts, widths):
     groups = lax.axis_size("beam")
     place = lax.axis_index("beam").astype(jnp.int32)
     chip, core = place >> 1, place & 1
     where = jnp.stack([chip, core])
-    padded = jnp.concatenate([shifts, jnp.zeros((64 - shifts.shape[0], shifts.shape[1]), jnp.int32)])
-    table = lax.all_gather(padded, "freq")[:, : shifts.shape[0]]
     swap = [(i, i ^ 1) for i in range(groups)]
     other = [lax.ppermute(block, "beam", swap) for block in (voltages, gains)]
     messages = calibrate(where, *other, calibrate(where, voltages, gains))
-    received = travelled(messages)
-    early = (steering(groups, chip), jnp.maximum(widths, 1))
-    received, matrix, reach = lax.optimization_barrier((received, *early))
+
+    def sent(block, distance):
+        return lax.ppermute(block, "beam", [(i, (i + distance * CORES) % groups) for i in range(groups)])
+
+    got = list(messages)
+    for k in (2, 6, 3, 4, 5):
+        got[k] = sent(messages[k], k)
+    late = (messages[1], messages[7], got[2], got[6], chip, shifts)
+    near, far, got[2], got[6], chip, shifts = lax.optimization_barrier(late)
+    got[1], got[7] = sent(near, 1), sent(far, 7)
+    short = jnp.concatenate([shifts.astype(jnp.bfloat16), jnp.zeros((16 - shifts.shape[0], shifts.shape[1]), jnp.bfloat16)])
+    table = exchanged(jnp.broadcast_to(short[None], (lax.axis_size("freq"),) + short.shape), "freq")
+    table = jnp.transpose(table[:, : shifts.shape[0]].astype(jnp.int32), (1, 0, 2))
+    early = (steering(groups, chip), jnp.maximum(widths, 1), table)
+    received, matrix, reach, table = lax.optimization_barrier((got, *early))
     detected = detect(received, matrix)
     spread = exchanged(detected.reshape(FEEDS, -1, LANES), ("freq", "beam"))
-    series = exchanged(tree(spread.reshape(detected.shape), jnp.transpose(table, (1, 0, 2))), "freq")
+    series = exchanged(tree(spread.reshape(detected.shape), table), "freq")
     return tuple(peaks(reach, series))
 
 

time: 101 us -> 83.1 us (0.82)
  blocking collectives: 9.81 us -> 37.6 us
  waiting for transfers between devices: 23.3 us -> 1.22 us
  between operations: 14.3 us -> 1.01 us
  starting transfers between devices: 31.8 us -> 26.3 us
  other arithmetic: 9.24 us -> 5.17 us
    all_to_all x1 -> x2, blocking collectives: 9.81 us -> 37.6 us  [exchanged(): return lax.all_to_all(block, axes, split_axis=0, concat_axis=0, tiled=True)]
    ppermute x7, waiting for transfers between devices: 11.6 us -> 0.02 us  [sent(): lax.ppermute(block, 'beam', [(i, (i + distance * CORES) % groups) for i i...]
    all_to_all x1, waiting for transfers between devices: 11.7 us -> 1.2 us  [exchanged(): return lax.all_to_all(block, axes, split_axis=0, concat_axis=0, tiled=True)]
    convert_element_type x4 -> x1, other arithmetic: 8.48 us -> 2.81 us  [steering(): (whole_cosine * cosine - whole_sine * sine).astype(jnp.bfloat16)]
    all_to_all x1, starting transfers between devices: 12.2 us -> 6.75 us  [exchanged(): return lax.all_to_all(block, axes, split_axis=0, concat_axis=0, tiled=True)]
    mul x0 -> x1, other arithmetic: none -> 1.57 us  [steering(): jnp.sin(angles) * factor]
    concatenate x1, local copies, waits for them, and re-layouts: 1.35 us -> 0.01 us  [shards(): jnp.concatenate([shifts.astype(jnp.bfloat16), jnp.zeros((16 - shifts.shap...]
    unnamed x7 -> x8, local copies, waits for them, and re-layouts: 1.16 us -> 2.28 us
  transfers between devices with their start and end apart: 11 -> 10, of which waited for: 6 -> 1; matrix products, arithmetic and copies ran while one was open for 12% -> 7% of each run, Pallas kernels for 6% -> 3%
where the time goes in v6:
time: 83.1 us; the launch traced here: 82.8 us
  blocking collectives  37.6 us (45%)
  starting transfers between devices  26.3 us (32%)
  Pallas kernels  8.5 us (10%)
  other arithmetic  5.17 us (6%)
  local copies, waits for them, and re-layouts  2.95 us (4%)
  waiting for transfers between devices  1.22 us (1%)
  between operations  1.01 us (1%)
    all_to_all x2, blocking collectives, exchanged(): return lax.all_to_all(block, axes, split_axis=0, concat_axis=0, tiled=True)  37.6 us
    ppermute x7, starting transfers between devices, sent(): lax.ppermute(block, 'beam', [(i, (i + distance * CORES) % groups) for i i...  16.1 us
    all_to_all x1, starting transfers between devices, exchanged(): return lax.all_to_all(block, axes, split_axis=0, concat_axis=0, tiled=True)  6.75 us
    pallas_call x2, Pallas kernels, calibrate(): pl.pallas_call(functools.partial(calibrate_kernel, own=own), in_specs=[pl...  4.17 us
    ppermute x2, starting transfers between devices, shards(): other = [lax.ppermute(block, 'beam', swap) for block in (voltages, gains)]  3.43 us
    convert_element_type x1, other arithmetic, steering(): (whole_cosine * cosine - whole_sine * sine).astype(jnp.bfloat16)  2.81 us
    unnamed x8, local copies, waits for them, and re-layouts  2.28 us
  transfers between devices with their start and end apart: 10, of which 1 were waited for; matrix products, arithmetic and copies ran while one was open for 7% of the time, Pallas kernels for 3%

profile of v6, /device:TPU:1, one launch (start us, length us, event | category | flops | bytes accessed | tf_op | source)
XLA Modules:
  0.0 82.8 jit_solution(17294244263385516316)
XLA Ops:
  0.6 3.3 %collective-permute-start = (bf16[2,16,16,1024]{3,2,1,0:T(8,128)(2,1)}, bf16[2,16,16,1024]{3,2,1,0:T(8,128)(2,1)S(1)}, u32[]{:S(2)}, u32[]{:S(2)}) collective-permute-start(bf16[2,16,16,1024]{3,2,1,0:T(8,128)(2,1)} %volt_hbm.1), channel_id=1, source_target_pairs={{0,1},{1,0},{2,3},{3,2},{4,5},{5,4},{6,7},{7,6},{8,9},{9,8},{10,11... | collective-permute-start | bytes 3145736 | tf_op jit(solution)/shard_map/ppermute | solution.py:337
  4.2 0.6 copy-done.3
  4.8 0.6 pad_add_fusion.where_ref
  5.4 2.6 %calibrate.2.rest_0_ = bf16[16,32,512]{2,1,0:T(8,128)(2,1)} custom-call(s32[2]{0:T(128)} %pad_add_fusion.where_ref, bf16[2,16,16,1024]{3,2,1,0:T(8,128)(2,1)} %volt_hbm.1, f32[2,16,1024]{2,1,0:T(8,128)} %gain_hbm.1), custom_call_target="tpu_custom_call" | custom-call | tf_op jit(solution)/shard_map/calibrate/pallas_call | solution.py:124
  8.1 0.6 copy-done.1
  8.7 1.0 %copy-done = bf16[16,32,512]{2,1,0:T(8,128)(2,1)S(1)} copy-done((bf16[16,32,512]{2,1,0:T(8,128)(2,1)S(1)}, bf16[16,32,512]{2,1,0:T(8,128)(2,1)}, u32[]{:S(2)}) %copy-start) | copy-done | bytes 524312
  9.8 1.5 %calibrate.3 = (bf16[2,2,32,512]{3,2,1,0:T(8,128)(2,1)S(1)}, bf16[2,2,32,512]{3,2,1,0:T(8,128)(2,1)S(1)}, bf16[2,2,32,512]{3,2,1,0:T(8,128)(2,1)S(1)}, bf16[2,2,...) custom-call(s32[2]{0:T(128)S(1)} %copy-done.1, ...), custom_call_target="tpu_custom_call" | custom-call | tf_op jit(solution)/shard_map/calibrate/pallas_call | solution.py:124
  11.3 1.3 %collective-permute-start.2 = (bf16[2,2,32,512]{3,2,1,0:T(8,128)(2,1)S(1)}, bf16[2,2,32,512]{3,2,1,0:T(8,128)(2,1)S(1)}, u32[]{:S(2)}, u32[]{:S(2)}) collective-permute-start(bf16[2,2,32,512]{3,2,1,0:T(8,128)(2,1)S(1)} %get-tuple-element.32), channel_id=1, source_target_pairs={{0,4},{1,5},{2,6},{3,7},{4,8},{5,9},{6,10},{7,11},{8,12},{9,13},{1... | collective-permute-start | bytes 393224 | tf_op jit(solution)/shard_map/ppermute | solution.py:341
  12.6 3.1 %collective-permute-start.3 = (bf16[2,2,32,512]{3,2,1,0:T(8,128)(2,1)S(1)}, bf16[2,2,32,512]{3,2,1,0:T(8,128)(2,1)S(1)}, u32[]{:S(2)}, u32[]{:S(2)}) collective-permute-start(bf16[2,2,32,512]{3,2,1,0:T(8,128)(2,1)S(1)} %get-tuple-element.33), channel_id=1, source_target_pairs={{0,12},{1,13},{2,14},{3,15},{4,0},{5,1},{6,2},{7,3},{8,4},{9,5},{1... | collective-permute-start | bytes 393224 | tf_op jit(solution)/shard_map/ppermute | solution.py:341
  15.7 1.6 %collective-permute-start.5 = (bf16[2,2,32,512]{3,2,1,0:T(8,128)(2,1)S(1)}, bf16[2,2,32,512]{3,2,1,0:T(8,128)(2,1)S(1)}, u32[]{:S(2)}, u32[]{:S(2)}) collective-permute-start(bf16[2,2,32,512]{3,2,1,0:T(8,128)(2,1)S(1)} %get-tuple-element.36), channel_id=1, source_target_pairs={{0,6},{1,7},{2,8},{3,9},{4,10},{5,11},{6,12},{7,13},{8,14},{9,15},... | collective-permute-start | bytes 393224 | tf_op jit(solution)/shard_map/ppermute | solution.py:341
  17.4 3.3 %collective-permute-start.6 = (bf16[2,2,32,512]{3,2,1,0:T(8,128)(2,1)S(1)}, bf16[2,2,32,512]{3,2,1,0:T(8,128)(2,1)S(1)}, u32[]{:S(2)}, u32[]{:S(2)}) collective-permute-start(bf16[2,2,32,512]{3,2,1,0:T(8,128)(2,1)S(1)} %get-tuple-element.37), channel_id=1, source_target_pairs={{0,8},{1,9},{2,10},{3,11},{4,12},{5,13},{6,14},{7,15},{8,0},{9,1},... | collective-permute-start | bytes 393224 | tf_op jit(solution)/shard_map/ppermute | solution.py:341
  20.6 4.0 %collective-permute-start.7 = (bf16[2,2,32,512]{3,2,1,0:T(8,128)(2,1)S(1)}, bf16[2,2,32,512]{3,2,1,0:T(8,128)(2,1)S(1)}, u32[]{:S(2)}, u32[]{:S(2)}) collective-permute-start(bf16[2,2,32,512]{3,2,1,0:T(8,128)(2,1)S(1)} %get-tuple-element.38), channel_id=1, source_target_pairs={{0,10},{1,11},{2,12},{3,13},{4,14},{5,15},{6,0},{7,1},{8,2},{9,3},... | collective-permute-start | bytes 393224 | tf_op jit(solution)/shard_map/ppermute | solution.py:341
  24.7 1.6 %sine_multiply_fusion = (f32[512,128]{1,0:T(8,128)S(1)}, f32[512,128]{1,0:T(8,128)S(1)}) fusion(s32[]{:T(128)S(6)} %mul.77, s32[128]{0:T(128)S(1)} %get-tuple-element.72, s32[128]{0:T(128)S(1)} %get-tuple-element.76, pred[128]{0:T(512)(128)(4,1)S(1)} %compare_and_fusion.3, s32[512]{0:T(512)S(1)} %get-tuple-element.62, s32[512]{0:T(512)S(1)} %get-tuple-element.67, ...), kind=kLoop, calls=%fused_computation.138 | loop fusion | flops 3735552 | bytes 541572 | tf_op jit(solution)/shard_map/mul | solution.py:34
  26.3 0.7 broadcast_in_dim.43
  27.0 6.8 %all-to-all-start = ((bf16[16,16,256]{2,1,0:T(8,128)(2,1)}), bf16[16,16,256]{2,1,0:T(8,128)(2,1)S(1)}, u32[]{:S(2)}, u32[]{:S(2)}) async-start(bf16[16,16,256]{2,1,0:T(8,128)(2,1)} %broadcast_in_dim.43), calls=%async_computation | async-start | bytes 262144 | tf_op jit(solution)/shard_map/all_to_all | solution.py:328
  33.7 0.8 collective-permute-start.4
  34.5 1.9 %collective-permute-start.8 = (bf16[2,2,32,512]{3,2,1,0:T(8,128)(2,1)S(1)}, bf16[2,2,32,512]{3,2,1,0:T(8,128)(2,1)S(1)}, u32[]{:S(2)}, u32[]{:S(2)}) collective-permute-start(bf16[2,2,32,512]{3,2,1,0:T(8,128)(2,1)S(1)} %get-tuple-element.40), channel_id=1, source_target_pairs={{0,14},{1,15},{2,0},{3,1},{4,2},{5,3},{6,4},{7,5},{8,6},{9,7},{10,... | collective-permute-start | bytes 393224 | tf_op jit(solution)/shard_map/ppermute | solution.py:341
  36.5 2.8 %fusion.6 = (bf16[512,128]{1,0:T(8,128)(2,1)S(1)}, bf16[512,128]{1,0:T(8,128)(2,1)S(1)}, bf16[512,128]{1,0:T(8,128)(2,1)S(1)}, bf16[512,128]{1,0:T(8,128)(2,1)S(1)}) fusion(f32[512,128]{1,0:T(8,128)S(1)} %get-tuple-element.42, f32[512,128]{1,0:T(8,128)S(1)} %get-tuple-element.43, s32[128]{0:T(128)S(1)} %get-tuple-element.78, s32[128]{0:T(128)S(1)} %get-tuple-element.79, ...), kind=kLoop, calls=%fused_computation.76 | loop fusion | flops 18808832 | bytes 1058948 | tf_op jit(solution)/shard_map/convert_element_type | solution.py:41
  39.4 1.2 %all-to-all-done = bf16[16,16,256]{2,1,0:T(8,128)(2,1)S(1)} async-done(((bf16[16,16,256]{2,1,0:T(8,128)(2,1)}), bf16[16,16,256]{2,1,0:T(8,128)(2,1)S(1)}, u32[]{:S(2)}, u32[]{:S(2)}) %all-to-all-start) | async-done | bytes 131104 | tf_op jit(solution)/shard_map/all_to_all | solution.py:328
  40.7 1.5 %detect.1 = bf16[512,128]{1,0:T(8,128)(2,1)S(1)} custom-call(bf16[512,512]{1,0:T(8,128)(2,1)S(1)} %pad_maximum_fusion.matrix_ref, bf16[2,2,32,512]{3,2,1,0:T(8,128)(2,1)S(1)} %get-tuple-element.47.rest_0_, bf16[2,2,32,512]{3,2,1,0:T(8,128)(2,1)S(1)} %collective-permute-done.4.rest_1_, bf16[2,2,32,512]{3,2,1,0:T(8,128)(2,1)S(1)} %collective-permute-done.2.rest_2_, ...), custom_call_target="tpu_custom_call" | custom-call | tf_op jit(solution)/shard_map/detect/pallas_call | solution.py:168
  42.2 27.8 %all_to_all.15 = bf16[256,2,128]{2,1,0:T(2,128)(2,1)S(1)} all-to-all(bf16[256,2,128]{2,1,0:T(2,128)(2,1)S(1)} %bitcast.8), channel_id=1, replica_groups=mesh['freq'=16,'beam'=16] {'freq','beam'}, dimensions={0} | all-to-all | bytes 262144 | tf_op jit(solution)/shard_map/all_to_all | solution.py:328
  70.0 1.4 %tree.1 = bf16[16,16,256]{2,1,0:T(8,128)(2,1)S(1)} custom-call(bf16[512,128]{1,0:T(8,128)(2,1)S(1)} %bitcast.7, s32[12,16,256]{2,1,0:T(8,128)S(1)} %convert_bitcast_fusion.shifts_ref), custom_call_target="tpu_custom_call" | custom-call | tf_op jit(solution)/shard_map/tree/pallas_call | solution.py:258
  71.4 9.8 %all_to_all.16.series_ref = bf16[16,16,256]{2,1,0:T(8,128)(2,1)S(1)} all-to-all(bf16[16,16,256]{2,1,0:T(8,128)(2,1)S(1)} %tree.1), channel_id=1, replica_groups=mesh['freq'=16,'beam'=16] {'freq'}, dimensions={0} | all-to-all | bytes 262144 | tf_op jit(solution)/shard_map/all_to_all | solution.py:328
  81.2 1.4 %peaks.1 = (bf16[16,16,256]{2,1,0:T(8,128)(2,1)}, f32[8,16,256]{2,1,0:T(8,128)}) custom-call(s32[8]{0:T(128)S(1)} %broadcast_maximum_fusion.widths_ref, bf16[16,16,256]{2,1,0:T(8,128)(2,1)S(1)} %all_to_all.16.series_ref), custom_call_target="tpu_custom_call" | custom-call | tf_op jit(solution)/shard_map/peaks/pallas_call | solution.py:307
  (32 shorter events, 0.3 us)
Async XLA Ops:
  0.6 7.5 %collective-permute-start = (bf16[2,16,16,1024]{3,2,1,0:T(8,128)(2,1)}, bf16[2,16,16,1024]{3,2,1,0:T(8,128)(2,1)S(1)}, u32[]{:S(2)}, u32[]{:S(2)}) collective-permute-start(bf16[2,16,16,1024]{3,2,1,0:T(8,128)(2,1)} %volt_hbm.1), channel_id=1, source_target_pairs={{0,1},{1,0},{2,3},{3,2},{4,5},{5,4},{6,7},{7,6},{8,9},{9,8},{10,11... | collective-permute-start | bytes 3145736 | tf_op jit(solution)/shard_map/ppermute | solution.py:337
  4.0 4.1 %collective-permute-start.1 = (f32[2,16,1024]{2,1,0:T(8,128)}, f32[2,16,1024]{2,1,0:T(8,128)S(1)}, u32[]{:S(2)}, u32[]{:S(2)}) collective-permute-start(f32[2,16,1024]{2,1,0:T(8,128)} %gain_hbm.1), channel_id=1, source_target_pairs={{0,1},{1,0},{2,3},{3,2},{4,5},{5,4},{6,7},{7,6},{8,9},{9,8},{10,11... | collective-permute-start | bytes 393224 | tf_op jit(solution)/shard_map/ppermute | solution.py:337
  4.1 0.7 copy-start.3
  8.1 0.6 copy-start.1
  8.7 1.0 %copy-start = (bf16[16,32,512]{2,1,0:T(8,128)(2,1)S(1)}, bf16[16,32,512]{2,1,0:T(8,128)(2,1)}, u32[]{:S(2)}) copy-start(bf16[16,32,512]{2,1,0:T(8,128)(2,1)} %calibrate.2.rest_0_) | copy-start | bytes 1572868
  11.3 13.4 %collective-permute-start.2 = (bf16[2,2,32,512]{3,2,1,0:T(8,128)(2,1)S(1)}, bf16[2,2,32,512]{3,2,1,0:T(8,128)(2,1)S(1)}, u32[]{:S(2)}, u32[]{:S(2)}) collective-permute-start(bf16[2,2,32,512]{3,2,1,0:T(8,128)(2,1)S(1)} %get-tuple-element.32), channel_id=1, source_target_pairs={{0,4},{1,5},{2,6},{3,7},{4,8},{5,9},{6,10},{7,11},{8,12},{9,13},{1... | collective-permute-start | bytes 393224 | tf_op jit(solution)/shard_map/ppermute | solution.py:341
  12.6 12.1 %collective-permute-start.3 = (bf16[2,2,32,512]{3,2,1,0:T(8,128)(2,1)S(1)}, bf16[2,2,32,512]{3,2,1,0:T(8,128)(2,1)S(1)}, u32[]{:S(2)}, u32[]{:S(2)}) collective-permute-start(bf16[2,2,32,512]{3,2,1,0:T(8,128)(2,1)S(1)} %get-tuple-element.33), channel_id=1, source_target_pairs={{0,12},{1,13},{2,14},{3,15},{4,0},{5,1},{6,2},{7,3},{8,4},{9,5},{1... | collective-permute-start | bytes 393224 | tf_op jit(solution)/shard_map/ppermute | solution.py:341
  15.7 24.9 %collective-permute-start.5 = (bf16[2,2,32,512]{3,2,1,0:T(8,128)(2,1)S(1)}, bf16[2,2,32,512]{3,2,1,0:T(8,128)(2,1)S(1)}, u32[]{:S(2)}, u32[]{:S(2)}) collective-permute-start(bf16[2,2,32,512]{3,2,1,0:T(8,128)(2,1)S(1)} %get-tuple-element.36), channel_id=1, source_target_pairs={{0,6},{1,7},{2,8},{3,9},{4,10},{5,11},{6,12},{7,13},{8,14},{9,15},... | collective-permute-start | bytes 393224 | tf_op jit(solution)/shard_map/ppermute | solution.py:341
  17.4 23.3 %collective-permute-start.6 = (bf16[2,2,32,512]{3,2,1,0:T(8,128)(2,1)S(1)}, bf16[2,2,32,512]{3,2,1,0:T(8,128)(2,1)S(1)}, u32[]{:S(2)}, u32[]{:S(2)}) collective-permute-start(bf16[2,2,32,512]{3,2,1,0:T(8,128)(2,1)S(1)} %get-tuple-element.37), channel_id=1, source_target_pairs={{0,8},{1,9},{2,10},{3,11},{4,12},{5,13},{6,14},{7,15},{8,0},{9,1},... | collective-permute-start | bytes 393224 | tf_op jit(solution)/shard_map/ppermute | solution.py:341
  20.6 20.0 %collective-permute-start.7 = (bf16[2,2,32,512]{3,2,1,0:T(8,128)(2,1)S(1)}, bf16[2,2,32,512]{3,2,1,0:T(8,128)(2,1)S(1)}, u32[]{:S(2)}, u32[]{:S(2)}) collective-permute-start(bf16[2,2,32,512]{3,2,1,0:T(8,128)(2,1)S(1)} %get-tuple-element.38), channel_id=1, source_target_pairs={{0,10},{1,11},{2,12},{3,13},{4,14},{5,15},{6,0},{7,1},{8,2},{9,3},... | collective-permute-start | bytes 393224 | tf_op jit(solution)/shard_map/ppermute | solution.py:341
  24.7 1.6 %copy-start.2 = (s32[12,256]{1,0:T(8,128)S(1)}, s32[12,256]{1,0:T(8,128)}, u32[]{:S(2)}) copy-start(s32[12,256]{1,0:T(8,128)} %param.6) | copy-start | bytes 36868
  27.0 13.6 %all-to-all-start = ((bf16[16,16,256]{2,1,0:T(8,128)(2,1)}), bf16[16,16,256]{2,1,0:T(8,128)(2,1)S(1)}, u32[]{:S(2)}, u32[]{:S(2)}) async-start(bf16[16,16,256]{2,1,0:T(8,128)(2,1)} %broadcast_in_dim.43), calls=%async_computation | async-start | bytes 262144 | tf_op jit(solution)/shard_map/all_to_all | solution.py:328
  33.7 6.9 %collective-permute-start.4 = (bf16[2,2,32,512]{3,2,1,0:T(8,128)(2,1)S(1)}, bf16[2,2,32,512]{3,2,1,0:T(8,128)(2,1)S(1)}, u32[]{:S(2)}, u32[]{:S(2)}) collective-permute-start(bf16[2,2,32,512]{3,2,1,0:T(8,128)(2,1)S(1)} %get-tuple-element.34), channel_id=1, source_target_pairs={{0,2},{1,3},{2,4},{3,5},{4,6},{5,7},{6,8},{7,9},{8,10},{9,11},{10,... | collective-permute-start | bytes 393224 | tf_op jit(solution)/shard_map/ppermute | solution.py:341
  34.5 6.1 %collective-permute-start.8 = (bf16[2,2,32,512]{3,2,1,0:T(8,128)(2,1)S(1)}, bf16[2,2,32,512]{3,2,1,0:T(8,128)(2,1)S(1)}, u32[]{:S(2)}, u32[]{:S(2)}) collective-permute-start(bf16[2,2,32,512]{3,2,1,0:T(8,128)(2,1)S(1)} %get-tuple-element.40), channel_id=1, source_target_pairs={{0,14},{1,15},{2,0},{3,1},{4,2},{5,3},{6,4},{7,5},{8,6},{9,7},{10,... | collective-permute-start | bytes 393224 | tf_op jit(solution)/shard_map/ppermute | solution.py:341

commit v7 on v6

--- a/solution.py
+++ b/solution.py
@@ -47,10 +47,10 @@
     return jnp.where((turn > 2) & (turn < 6), -size, size)
 
 
-def calibrate_kernel(where_ref, volt_hbm, gain_hbm, *rest, own):
+def calibrate_kernel(chip_ref, core_ref, volt_hbm, gain_hbm, *rest, own):
     volt, gain, wide, in_sems, sems = rest[-5:]
     chunks, _, feeds, samples, _ = volt.shape
-    chip, core = where_ref[0], where_ref[1]
+    chip, core = chip_ref[0], core_ref[0]
     if own:
         out_hbm, done = rest[:2]
     else:
@@ -109,7 +109,7 @@
             joining(k).wait()
 
 
-def calibrate(where, voltages, gains, begun=None):
+def calibrate(chip, core, voltages, gains, begun=None):
     _, feeds, samples, width = voltages.shape
     chunks = width // CORES // LANES
     own = begun is None
@@ -120,10 +120,10 @@
     else:
         out_shape = [jax.ShapeDtypeStruct((2, CORES) + shape[1:], jnp.bfloat16)] * (samples // 2)
         out_specs = [pl.BlockSpec(memory_space=pltpu.VMEM)] * (samples // 2)
-    operands = (where, voltages, gains) + (() if own else (begun,))
+    operands = (chip.reshape(1), core.reshape(1), voltages, gains) + (() if own else (begun,))
     return pl.pallas_call(
         functools.partial(calibrate_kernel, own=own),
-        in_specs=[pl.BlockSpec(memory_space=pltpu.SMEM)] + [pl.BlockSpec(memory_space=pl.ANY)] * (len(operands) - 1),
+        in_specs=[pl.BlockSpec(memory_space=pltpu.SMEM)] * 2 + [pl.BlockSpec(memory_space=pl.ANY)] * (len(operands) - 2),
         out_specs=out_specs,
         out_shape=out_shape,
         scratch_shapes=[pltpu.VMEM((chunks, samples, 2 * feeds, LANES), jnp.bfloat16)] * own
@@ -332,20 +332,19 @@
     groups = lax.axis_size("beam")
     place = lax.axis_index("beam").astype(jnp.int32)
     chip, core = place >> 1, place & 1
-    where = jnp.stack([chip, core])
     swap = [(i, i ^ 1) for i in range(groups)]
     other = [lax.ppermute(block, "beam", swap) for block in (voltages, gains)]
-    messages = calibrate(where, *other, calibrate(where, voltages, gains))
+    messages = calibrate(chip, core, *other, calibrate(chip, core, voltages, gains))
 
     def sent(block, distance):
         return lax.ppermute(block, "beam", [(i, (i + distance * CORES) % groups) for i in range(groups)])
 
     got = list(messages)
-    for k in (2, 6, 3, 4, 5):
+    for k in (1, 7, 2, 6, 4):
         got[k] = sent(messages[k], k)
-    late = (messages[1], messages[7], got[2], got[6], chip, shifts)
-    near, far, got[2], got[6], chip, shifts = lax.optimization_barrier(late)
-    got[1], got[7] = sent(near, 1), sent(far, 7)
+    third, fifth, got[1], got[7] = lax.optimization_barrier((messages[3], messages[5], got[1], got[7]))
+    got[3], got[5] = sent(third, 3), sent(fifth, 5)
+    got[2], got[6], chip, shifts, widths = lax.optimization_barrier((got[2], got[6], chip, shifts, widths))
     short = jnp.concatenate([shifts.astype(jnp.bfloat16), jnp.zeros((16 - shifts.shape[0], shifts.shape[1]), jnp.bfloat16)])
     table = exchanged(jnp.broadcast_to(short[None], (lax.axis_size("freq"),) + short.shape), "freq")
     table = jnp.transpose(table[:, : shifts.shape[0]].astype(jnp.int32), (1, 0, 2))

time: 83.1 us -> 83.7 us (level)
  waiting for transfers between devices: 1.22 us -> 5.8 us
  local copies, waits for them, and re-layouts: 2.95 us -> 1.73 us
  Pallas kernels: 8.5 us -> 7.29 us
  blocking collectives: 37.6 us -> 36.6 us
    all_to_all x1, waiting for transfers between devices: 1.2 us -> 3.89 us  [exchanged(): return lax.all_to_all(block, axes, split_axis=0, concat_axis=0, tiled=True)]
    ppermute x7, waiting for transfers between devices: 0.02 us -> 1.43 us  [sent(): lax.ppermute(block, 'beam', [(i, (i + distance * CORES) % groups) for i i...]
    unnamed x8 -> x6, local copies, waits for them, and re-layouts: 2.28 us -> 1.05 us
    pallas_call x2, Pallas kernels: 4.17 us -> 2.96 us  [calibrate(): pl.pallas_call(functools.partial(calibrate_kernel, own=own), in_specs=[pl...]
    all_to_all x2, blocking collectives: 37.6 us -> 36.6 us  [exchanged(): return lax.all_to_all(block, axes, split_axis=0, concat_axis=0, tiled=True)]
  transfers between devices with their start and end apart: 10 -> 10, of which waited for: 1 -> 4; matrix products, arithmetic and copies ran while one was open for 7% -> 6% of each run, Pallas kernels for 3% -> 2%
where the time goes in v7:
time: 83.7 us; the launch traced here: 83.4 us
  blocking collectives  36.6 us (44%)
  starting transfers between devices  26.4 us (32%)
  Pallas kernels  7.29 us (9%)
  waiting for transfers between devices  5.8 us (7%)
  other arithmetic  4.6 us (5%)
  local copies, waits for them, and re-layouts  1.73 us (2%)
  between operations  0.96 us (1%)
    all_to_all x2, blocking collectives, exchanged(): return lax.all_to_all(block, axes, split_axis=0, concat_axis=0, tiled=True)  36.6 us
    ppermute x7, starting transfers between devices, sent(): lax.ppermute(block, 'beam', [(i, (i + distance * CORES) % groups) for i i...  16.1 us
    all_to_all x1, starting transfers between devices, exchanged(): return lax.all_to_all(block, axes, split_axis=0, concat_axis=0, tiled=True)  6.89 us
    all_to_all x1, waiting for transfers between devices, exchanged(): return lax.all_to_all(block, axes, split_axis=0, concat_axis=0, tiled=True)  3.89 us
    ppermute x2, starting transfers between devices, shards(): other = [lax.ppermute(block, 'beam', swap) for block in (voltages, gains)]  3.43 us
    pallas_call x2, Pallas kernels, calibrate(): pl.pallas_call(functools.partial(calibrate_kernel, own=own), in_specs=[pl...  2.96 us
    convert_element_type x1, other arithmetic, steering(): (whole_cosine * cosine - whole_sine * sine).astype(jnp.bfloat16)  2.85 us
  transfers between devices with their start and end apart: 10, of which 4 were waited for; matrix products, arithmetic and copies ran while one was open for 6% of the time, Pallas kernels for 2%

profile of v7, /device:TPU:1, one launch (start us, length us, event | category | flops | bytes accessed | tf_op | source)
XLA Modules:
  0.0 83.4 jit_solution(4324468621279852451)
XLA Ops:
  0.6 3.3 %collective-permute-start = (bf16[2,16,16,1024]{3,2,1,0:T(8,128)(2,1)}, bf16[2,16,16,1024]{3,2,1,0:T(8,128)(2,1)S(1)}, u32[]{:S(2)}, u32[]{:S(2)}) collective-permute-start(bf16[2,16,16,1024]{3,2,1,0:T(8,128)(2,1)} %volt_hbm.1), channel_id=1, source_target_pairs={{0,1},{1,0},{2,3},{3,2},{4,5},{5,4},{6,7},{7,6},{8,9},{9,8},{10,11... | collective-permute-start | bytes 3145736 | tf_op jit(solution)/shard_map/ppermute | solution.py:336
  4.2 2.0 %calibrate.2.rest_0_ = bf16[16,32,512]{2,1,0:T(8,128)(2,1)} custom-call(s32[1]{0:T(128)} %bitcast.chip_ref, s32[1]{0:T(128)} %bitcast.1.core_ref, bf16[2,16,16,1024]{3,2,1,0:T(8,128)(2,1)} %volt_hbm.1, f32[2,16,1024]{2,1,0:T(8,128)} %gain_hbm.1), custom_call_target="tpu_custom_call" | custom-call | tf_op jit(solution)/shard_map/calibrate/pallas_call | solution.py:124
  6.2 0.5 collective-permute-done.1.gain_hbm
  6.6 1.0 %copy-done = bf16[16,32,512]{2,1,0:T(8,128)(2,1)S(1)} copy-done((bf16[16,32,512]{2,1,0:T(8,128)(2,1)S(1)}, bf16[16,32,512]{2,1,0:T(8,128)(2,1)}, u32[]{:S(2)}) %copy-start) | copy-done | bytes 524312
  7.7 1.0 %calibrate.3 = (bf16[2,2,32,512]{3,2,1,0:T(8,128)(2,1)S(1)}, bf16[2,2,32,512]{3,2,1,0:T(8,128)(2,1)S(1)}, bf16[2,2,32,512]{3,2,1,0:T(8,128)(2,1)S(1)}, bf16[2,2,...) custom-call(s32[1]{0:T(128)} %bitcast.chip_ref, ...), custom_call_target="tpu_custom_call" | custom-call | tf_op jit(solution)/shard_map/calibrate/pallas_call | solution.py:124
  8.7 1.3 %collective-permute-start.4 = (bf16[2,2,32,512]{3,2,1,0:T(8,128)(2,1)S(1)}, bf16[2,2,32,512]{3,2,1,0:T(8,128)(2,1)S(1)}, u32[]{:S(2)}, u32[]{:S(2)}) collective-permute-start(bf16[2,2,32,512]{3,2,1,0:T(8,128)(2,1)S(1)} %get-tuple-element.38), channel_id=1, source_target_pairs={{0,4},{1,5},{2,6},{3,7},{4,8},{5,9},{6,10},{7,11},{8,12},{9,13},{1... | collective-permute-start | bytes 393224 | tf_op jit(solution)/shard_map/ppermute | solution.py:340
  10.0 3.1 %collective-permute-start.5 = (bf16[2,2,32,512]{3,2,1,0:T(8,128)(2,1)S(1)}, bf16[2,2,32,512]{3,2,1,0:T(8,128)(2,1)S(1)}, u32[]{:S(2)}, u32[]{:S(2)}) collective-permute-start(bf16[2,2,32,512]{3,2,1,0:T(8,128)(2,1)S(1)} %get-tuple-element.39), channel_id=1, source_target_pairs={{0,12},{1,13},{2,14},{3,15},{4,0},{5,1},{6,2},{7,3},{8,4},{9,5},{1... | collective-permute-start | bytes 393224 | tf_op jit(solution)/shard_map/ppermute | solution.py:340
  13.1 0.8 collective-permute-start.2
  14.0 1.9 %collective-permute-start.3 = (bf16[2,2,32,512]{3,2,1,0:T(8,128)(2,1)S(1)}, bf16[2,2,32,512]{3,2,1,0:T(8,128)(2,1)S(1)}, u32[]{:S(2)}, u32[]{:S(2)}) collective-permute-start(bf16[2,2,32,512]{3,2,1,0:T(8,128)(2,1)S(1)} %get-tuple-element.36), channel_id=1, source_target_pairs={{0,14},{1,15},{2,0},{3,1},{4,2},{5,3},{6,4},{7,5},{8,6},{9,7},{10,... | collective-permute-start | bytes 393224 | tf_op jit(solution)/shard_map/ppermute | solution.py:340
  15.9 4.4 %collective-permute-start.7 = (bf16[2,2,32,512]{3,2,1,0:T(8,128)(2,1)S(1)}, bf16[2,2,32,512]{3,2,1,0:T(8,128)(2,1)S(1)}, u32[]{:S(2)}, u32[]{:S(2)}) collective-permute-start(bf16[2,2,32,512]{3,2,1,0:T(8,128)(2,1)S(1)} %get-tuple-element.42), channel_id=1, source_target_pairs={{0,8},{1,9},{2,10},{3,11},{4,12},{5,13},{6,14},{7,15},{8,0},{9,1},... | collective-permute-start | bytes 393224 | tf_op jit(solution)/shard_map/ppermute | solution.py:340
  20.3 0.3 collective-permute-done.5.rest_6_
  20.6 1.6 %sine_multiply_fusion = (f32[512,128]{1,0:T(8,128)S(1)}, f32[512,128]{1,0:T(8,128)S(1)}) fusion(s32[]{:T(128)S(6)} %mul.77, s32[128]{0:T(128)S(1)} %get-tuple-element.78, s32[128]{0:T(128)S(1)} %get-tuple-element.82, pred[128]{0:T(512)(128)(4,1)S(1)} %compare_and_fusion.3, s32[512]{0:T(512)S(1)} %get-tuple-element.68, s32[512]{0:T(512)S(1)} %get-tuple-element.73, ...), kind=kLoop, calls=%fused_computation.138 | loop fusion | flops 3735552 | bytes 541572 | tf_op jit(solution)/shard_map/mul | solution.py:34
  22.2 1.1 %collective-permute-done.3.rest_7_ = bf16[2,2,32,512]{3,2,1,0:T(8,128)(2,1)S(1)} collective-permute-done((bf16[2,2,32,512]{3,2,1,0:T(8,128)(2,1)S(1)}, bf16[2,2,32,512]{3,2,1,0:T(8,128)(2,1)S(1)}, u32[]{:S(2)}, u32[]{:S(2)}) %collective-permute-start.3) | collective-permute-done | bytes 131104 | tf_op jit(solution)/shard_map/ppermute | solution.py:340
  23.3 3.7 %collective-permute-start.6 = (bf16[2,2,32,512]{3,2,1,0:T(8,128)(2,1)S(1)}, bf16[2,2,32,512]{3,2,1,0:T(8,128)(2,1)S(1)}, u32[]{:S(2)}, u32[]{:S(2)}) collective-permute-start(bf16[2,2,32,512]{3,2,1,0:T(8,128)(2,1)S(1)} %get-tuple-element.41), channel_id=1, source_target_pairs={{0,6},{1,7},{2,8},{3,9},{4,10},{5,11},{6,12},{7,13},{8,14},{9,15},... | collective-permute-start | bytes 393224 | tf_op jit(solution)/shard_map/ppermute | solution.py:340
  27.0 0.8 collective-permute-start.8
  27.8 0.7 broadcast_in_dim.43
  28.4 6.9 %all-to-all-start = ((bf16[16,16,256]{2,1,0:T(8,128)(2,1)}), bf16[16,16,256]{2,1,0:T(8,128)(2,1)S(1)}, u32[]{:S(2)}, u32[]{:S(2)}) async-start(bf16[16,16,256]{2,1,0:T(8,128)(2,1)} %broadcast_in_dim.43), calls=%async_computation | async-start | bytes 262144 | tf_op jit(solution)/shard_map/all_to_all | solution.py:328
  35.3 2.9 %fusion.6 = (bf16[512,128]{1,0:T(8,128)(2,1)S(1)}, bf16[512,128]{1,0:T(8,128)(2,1)S(1)}, bf16[512,128]{1,0:T(8,128)(2,1)S(1)}, bf16[512,128]{1,0:T(8,128)(2,1)S(1)}) fusion(f32[512,128]{1,0:T(8,128)S(1)} %get-tuple-element.47, f32[512,128]{1,0:T(8,128)S(1)} %get-tuple-element.48, s32[128]{0:T(128)S(1)} %get-tuple-element.84, s32[128]{0:T(128)S(1)} %get-tuple-element.85, ...), kind=kLoop, calls=%fused_computation.76 | loop fusion | flops 18808832 | bytes 1058948 | tf_op jit(solution)/shard_map/convert_element_type | solution.py:41
  38.3 3.9 %all-to-all-done = bf16[16,16,256]{2,1,0:T(8,128)(2,1)S(1)} async-done(((bf16[16,16,256]{2,1,0:T(8,128)(2,1)}), bf16[16,16,256]{2,1,0:T(8,128)(2,1)S(1)}, u32[]{:S(2)}, u32[]{:S(2)}) %all-to-all-start) | async-done | bytes 131104 | tf_op jit(solution)/shard_map/all_to_all | solution.py:328
  42.2 1.5 %detect.1 = bf16[512,128]{1,0:T(8,128)(2,1)S(1)} custom-call(bf16[512,512]{1,0:T(8,128)(2,1)S(1)} %pad_maximum_fusion.matrix_ref, bf16[2,2,32,512]{3,2,1,0:T(8,128)(2,1)S(1)} %get-tuple-element.53.rest_0_, bf16[2,2,32,512]{3,2,1,0:T(8,128)(2,1)S(1)} %collective-permute-done.2.rest_1_, bf16[2,2,32,512]{3,2,1,0:T(8,128)(2,1)S(1)} %collective-permute-done.4.rest_2_, ...), custom_call_target="tpu_custom_call" | custom-call | tf_op jit(solution)/shard_map/detect/pallas_call | solution.py:168
  43.8 26.8 %all_to_all.15 = bf16[256,2,128]{2,1,0:T(2,128)(2,1)S(1)} all-to-all(bf16[256,2,128]{2,1,0:T(2,128)(2,1)S(1)} %bitcast.8), channel_id=1, replica_groups=mesh['freq'=16,'beam'=16] {'freq','beam'}, dimensions={0} | all-to-all | bytes 262144 | tf_op jit(solution)/shard_map/all_to_all | solution.py:328
  70.6 1.4 %tree.1 = bf16[16,16,256]{2,1,0:T(8,128)(2,1)S(1)} custom-call(bf16[512,128]{1,0:T(8,128)(2,1)S(1)} %bitcast.7, s32[12,16,256]{2,1,0:T(8,128)S(1)} %convert_bitcast_fusion.shifts_ref), custom_call_target="tpu_custom_call" | custom-call | tf_op jit(solution)/shard_map/tree/pallas_call | solution.py:258
  72.0 9.8 %all_to_all.16.series_ref = bf16[16,16,256]{2,1,0:T(8,128)(2,1)S(1)} all-to-all(bf16[16,16,256]{2,1,0:T(8,128)(2,1)S(1)} %tree.1), channel_id=1, replica_groups=mesh['freq'=16,'beam'=16] {'freq'}, dimensions={0} | all-to-all | bytes 262144 | tf_op jit(solution)/shard_map/all_to_all | solution.py:328
  81.8 1.4 %peaks.1 = (bf16[16,16,256]{2,1,0:T(8,128)(2,1)}, f32[8,16,256]{2,1,0:T(8,128)}) custom-call(s32[8]{0:T(128)S(1)} %broadcast_maximum_fusion.widths_ref, bf16[16,16,256]{2,1,0:T(8,128)(2,1)S(1)} %all_to_all.16.series_ref), custom_call_target="tpu_custom_call" | custom-call | tf_op jit(solution)/shard_map/peaks/pallas_call | solution.py:307
  (29 shorter events, 0.3 us)
Async XLA Ops:
  0.6 6.0 %collective-permute-start = (bf16[2,16,16,1024]{3,2,1,0:T(8,128)(2,1)}, bf16[2,16,16,1024]{3,2,1,0:T(8,128)(2,1)S(1)}, u32[]{:S(2)}, u32[]{:S(2)}) collective-permute-start(bf16[2,16,16,1024]{3,2,1,0:T(8,128)(2,1)} %volt_hbm.1), channel_id=1, source_target_pairs={{0,1},{1,0},{2,3},{3,2},{4,5},{5,4},{6,7},{7,6},{8,9},{9,8},{10,11... | collective-permute-start | bytes 3145736 | tf_op jit(solution)/shard_map/ppermute | solution.py:336
  4.0 2.7 %collective-permute-start.1 = (f32[2,16,1024]{2,1,0:T(8,128)}, f32[2,16,1024]{2,1,0:T(8,128)S(1)}, u32[]{:S(2)}, u32[]{:S(2)}) collective-permute-start(f32[2,16,1024]{2,1,0:T(8,128)} %gain_hbm.1), channel_id=1, source_target_pairs={{0,1},{1,0},{2,3},{3,2},{4,5},{5,4},{6,7},{7,6},{8,9},{9,8},{10,11... | collective-permute-start | bytes 393224 | tf_op jit(solution)/shard_map/ppermute | solution.py:336
  6.6 1.0 %copy-start = (bf16[16,32,512]{2,1,0:T(8,128)(2,1)S(1)}, bf16[16,32,512]{2,1,0:T(8,128)(2,1)}, u32[]{:S(2)}) copy-start(bf16[16,32,512]{2,1,0:T(8,128)(2,1)} %calibrate.2.rest_0_) | copy-start | bytes 1572868
  8.7 11.6 %collective-permute-start.4 = (bf16[2,2,32,512]{3,2,1,0:T(8,128)(2,1)S(1)}, bf16[2,2,32,512]{3,2,1,0:T(8,128)(2,1)S(1)}, u32[]{:S(2)}, u32[]{:S(2)}) collective-permute-start(bf16[2,2,32,512]{3,2,1,0:T(8,128)(2,1)S(1)} %get-tuple-element.38), channel_id=1, source_target_pairs={{0,4},{1,5},{2,6},{3,7},{4,8},{5,9},{6,10},{7,11},{8,12},{9,13},{1... | collective-permute-start | bytes 393224 | tf_op jit(solution)/shard_map/ppermute | solution.py:340
  10.0 10.6 %collective-permute-start.5 = (bf16[2,2,32,512]{3,2,1,0:T(8,128)(2,1)S(1)}, bf16[2,2,32,512]{3,2,1,0:T(8,128)(2,1)S(1)}, u32[]{:S(2)}, u32[]{:S(2)}) collective-permute-start(bf16[2,2,32,512]{3,2,1,0:T(8,128)(2,1)S(1)} %get-tuple-element.39), channel_id=1, source_target_pairs={{0,12},{1,13},{2,14},{3,15},{4,0},{5,1},{6,2},{7,3},{8,4},{9,5},{1... | collective-permute-start | bytes 393224 | tf_op jit(solution)/shard_map/ppermute | solution.py:340
  13.1 9.0 %collective-permute-start.2 = (bf16[2,2,32,512]{3,2,1,0:T(8,128)(2,1)S(1)}, bf16[2,2,32,512]{3,2,1,0:T(8,128)(2,1)S(1)}, u32[]{:S(2)}, u32[]{:S(2)}) collective-permute-start(bf16[2,2,32,512]{3,2,1,0:T(8,128)(2,1)S(1)} %get-tuple-element.35), channel_id=1, source_target_pairs={{0,2},{1,3},{2,4},{3,5},{4,6},{5,7},{6,8},{7,9},{8,10},{9,11},{10,... | collective-permute-start | bytes 393224 | tf_op jit(solution)/shard_map/ppermute | solution.py:340
  14.0 9.3 %collective-permute-start.3 = (bf16[2,2,32,512]{3,2,1,0:T(8,128)(2,1)S(1)}, bf16[2,2,32,512]{3,2,1,0:T(8,128)(2,1)S(1)}, u32[]{:S(2)}, u32[]{:S(2)}) collective-permute-start(bf16[2,2,32,512]{3,2,1,0:T(8,128)(2,1)S(1)} %get-tuple-element.36), channel_id=1, source_target_pairs={{0,14},{1,15},{2,0},{3,1},{4,2},{5,3},{6,4},{7,5},{8,6},{9,7},{10,... | collective-permute-start | bytes 393224 | tf_op jit(solution)/shard_map/ppermute | solution.py:340
  15.9 26.3 %collective-permute-start.7 = (bf16[2,2,32,512]{3,2,1,0:T(8,128)(2,1)S(1)}, bf16[2,2,32,512]{3,2,1,0:T(8,128)(2,1)S(1)}, u32[]{:S(2)}, u32[]{:S(2)}) collective-permute-start(bf16[2,2,32,512]{3,2,1,0:T(8,128)(2,1)S(1)} %get-tuple-element.42), channel_id=1, source_target_pairs={{0,8},{1,9},{2,10},{3,11},{4,12},{5,13},{6,14},{7,15},{8,0},{9,1},... | collective-permute-start | bytes 393224 | tf_op jit(solution)/shard_map/ppermute | solution.py:340
  20.6 7.2 %copy-start.1 = (s32[12,256]{1,0:T(8,128)S(1)}, s32[12,256]{1,0:T(8,128)}, u32[]{:S(2)}) copy-start(s32[12,256]{1,0:T(8,128)} %param.6) | copy-start | bytes 36868
  23.3 19.0 %collective-permute-start.6 = (bf16[2,2,32,512]{3,2,1,0:T(8,128)(2,1)S(1)}, bf16[2,2,32,512]{3,2,1,0:T(8,128)(2,1)S(1)}, u32[]{:S(2)}, u32[]{:S(2)}) collective-permute-start(bf16[2,2,32,512]{3,2,1,0:T(8,128)(2,1)S(1)} %get-tuple-element.41), channel_id=1, source_target_pairs={{0,6},{1,7},{2,8},{3,9},{4,10},{5,11},{6,12},{7,13},{8,14},{9,15},... | collective-permute-start | bytes 393224 | tf_op jit(solution)/shard_map/ppermute | solution.py:340
  27.0 15.3 %collective-permute-start.8 = (bf16[2,2,32,512]{3,2,1,0:T(8,128)(2,1)S(1)}, bf16[2,2,32,512]{3,2,1,0:T(8,128)(2,1)S(1)}, u32[]{:S(2)}, u32[]{:S(2)}) collective-permute-start(bf16[2,2,32,512]{3,2,1,0:T(8,128)(2,1)S(1)} %get-tuple-element.43), channel_id=1, source_target_pairs={{0,10},{1,11},{2,12},{3,13},{4,14},{5,15},{6,0},{7,1},{8,2},{9,3},... | collective-permute-start | bytes 393224 | tf_op jit(solution)/shard_map/ppermute | solution.py:340
  28.4 6.9 %copy-start.2 = (s32[8]{0:T(128)S(1)}, s32[8]{0:T(128)}, u32[]{:S(2)}) copy-start(s32[8]{0:T(128)} %param.7) | copy-start | bytes 100
  28.4 13.7 %all-to-all-start = ((bf16[16,16,256]{2,1,0:T(8,128)(2,1)}), bf16[16,16,256]{2,1,0:T(8,128)(2,1)S(1)}, u32[]{:S(2)}, u32[]{:S(2)}) async-start(bf16[16,16,256]{2,1,0:T(8,128)(2,1)} %broadcast_in_dim.43), calls=%async_computation | async-start | bytes 262144 | tf_op jit(solution)/shard_map/all_to_all | solution.py:328

commit v8 on v4

--- a/solution.py
+++ b/solution.py
@@ -94,24 +94,21 @@
 def detect_kernel(matrix_ref, x_ref, out_ref, scratch):
     width = x_ref.shape[1]
     step = 256
-    total = jnp.zeros((FEEDS, width // CHAN_SUM), jnp.float32)
-    channel = lax.broadcasted_iota(jnp.int32, (step, width // CHAN_SUM), 0)
-    group = lax.broadcasted_iota(jnp.int32, (step, width // CHAN_SUM), 1)
-    for j in range(width // step):
-        cols = slice(j * step, (j + 1) * step)
-        formed = jnp.dot(matrix_ref[...], x_ref[:, cols], preferred_element_type=jnp.float32)
-        power = formed[:FEEDS] * formed[:FEEDS] + formed[FEEDS:] * formed[FEEDS:]
+    pieces = width // CHAN_SUM // LANES
+    deep = CHAN_SUM * LANES
+    picking = lax.broadcasted_iota(jnp.int32, (deep, LANES), 0) == lax.broadcasted_iota(jnp.int32, (deep, LANES), 1) * CHAN_SUM
+    picking = picking.astype(jnp.bfloat16)
+    for h in range(pieces):
         sums = []
-        for lane in range(0, step, LANES):
-            part = power[:, lane : lane + LANES]
-            part = part + pltpu.roll(part, LANES - 1, 1)
-            sums.append(part + pltpu.roll(part, LANES - 2, 1))
-        picking = (channel + j * step == group * CHAN_SUM).astype(jnp.bfloat16)
-        summed = jnp.concatenate(sums, axis=1).astype(jnp.bfloat16)
-        total += jnp.dot(summed, picking, preferred_element_type=jnp.float32)
-    pieces = width // CHAN_SUM // LANES
-    for h in range(pieces):
-        scratch[pl.ds(h, FEEDS, stride=pieces), :] = total[:, h * LANES : (h + 1) * LANES]
+        for first in range(h * deep, (h + 1) * deep, step):
+            formed = jnp.dot(matrix_ref[...], x_ref[:, first : first + step], preferred_element_type=jnp.float32)
+            power = formed[:FEEDS] * formed[:FEEDS] + formed[FEEDS:] * formed[FEEDS:]
+            for lane in range(0, step, LANES):
+                part = power[:, lane : lane + LANES]
+                part = part + pltpu.roll(part, LANES - 1, 1)
+                sums.append((part + pltpu.roll(part, LANES - 2, 1)).astype(jnp.bfloat16))
+        summed = jnp.concatenate(sums, axis=1)
+        scratch[pl.ds(h, FEEDS, stride=pieces), :] = jnp.dot(summed, picking, preferred_element_type=jnp.float32)
     out_ref[...] = scratch[...].astype(jnp.bfloat16)
 
 
@@ -156,7 +153,10 @@
     blocks, samples, width = out_ref.shape
     pieces = width // LANES
     scale = 1.0 / (8.0 * math.sqrt(NSUB))
-    wide[...] = detected_ref[...].astype(jnp.float32)
+    length = samples * pieces
+    pitch = length + 8
+    for q in range(blocks):
+        wide[q * pitch : q * pitch + length] = detected_ref[q * length : (q + 1) * length].astype(jnp.float32)
 
     def bits_of(section, group, piece):
         offsets = shifts_ref[section, group * 8 : (group + 1) * 8, piece * LANES : (piece + 1) * LANES]
@@ -167,8 +167,8 @@
         for piece in range(pieces):
             rows = []
             for t in range(samples):
-                first = group * 8 * samples * pieces + t * pieces + piece
-                rows.append(wide[pl.ds(first, 8, stride=samples * pieces), :])
+                first = group * 8 * pitch + t * pieces + piece
+                rows.append(wide[pl.ds(first, 8, stride=pitch), :])
             mean = functools.reduce(jnp.add, rows) * (1.0 / samples)
             rows = [row - mean for row in rows]
             for section in range(lane_bits):
@@ -194,9 +194,10 @@
         for group in range(2):
             rows = merged(parts[0], parts[1], bits_of(lane_bits + 4, group, piece))
             for t in range(samples):
-                turned[piece, pl.ds(group * 8 * samples + t, 8, stride=samples), :] = rows[t] * scale
-        block = turned[piece].reshape(blocks, samples, LANES)
-        out_ref[:, :, piece * LANES : (piece + 1) * LANES] = block.astype(jnp.bfloat16)
+                turned[piece, pl.ds(group * 8 * PITCH + t, 8, stride=PITCH), :] = rows[t] * scale
+        for q in range(blocks):
+            block = turned[piece, q * PITCH : q * PITCH + samples, :]
+            out_ref[q, :, piece * LANES : (piece + 1) * LANES] = block.astype(jnp.bfloat16)
 
 
 def tree(detected, shifts):
@@ -207,9 +208,9 @@
         tree_kernel,
         out_shape=jax.ShapeDtypeStruct((blocks, TIME, width), jnp.bfloat16),
         scratch_shapes=[
-            pltpu.VMEM((rows, LANES), jnp.float32),
+            pltpu.VMEM((rows + 8 * blocks, LANES), jnp.float32),
             pltpu.VMEM((pieces, blocks // 8, TIME, 8, LANES), jnp.float32),
-            pltpu.VMEM((pieces, blocks * TIME, LANES), jnp.float32),
+            pltpu.VMEM((pieces, blocks * PITCH, LANES), jnp.float32),
         ],
         compiler_params=pltpu.CompilerParams(vmem_limit_bytes=8 * MIB),
         name="tree",
@@ -226,11 +227,13 @@
     same.start()
     for j in range(width // LANES):
         lanes = slice(j * LANES, (j + 1) * LANES)
-        wide[j] = series_ref[:, :, lanes].astype(jnp.float32).reshape(beams * samples, LANES)
+        block = series_ref[:, :, lanes].astype(jnp.float32)
+        for b in range(beams):
+            wide[j, b * PITCH : b * PITCH + samples] = block[b]
         total = jnp.zeros((beams, LANES), jnp.float32)
         sums[0, :, lanes] = total
         for t in range(samples):
-            total = total + wide[j, pl.ds(t, beams, stride=samples), :]
+            total = total + wide[j, pl.ds(t, beams, stride=PITCH), :]
             sums[t + 1, :, lanes] = total
     for t in range(samples + 1, sums.shape[0]):
         sums[t] = jnp.full((beams, width), -1e30, jnp.float32)
@@ -261,7 +264,7 @@
             jax.ShapeDtypeStruct((count, beams, width), jnp.float32),
         ],
         scratch_shapes=[
-            pltpu.VMEM((width // LANES, beams * samples, LANES), jnp.float32),
+            pltpu.VMEM((width // LANES, beams * PITCH, LANES), jnp.float32),
             pltpu.VMEM((rows, beams, width), jnp.float32),
             pltpu.VMEM((count, beams, width), jnp.float32),
             pltpu.SemaphoreType.DMA,

time: 77.5 us -> 77.3 us (level)
  no operation moved by 1% of the time
where the time goes in v8:
time: 77.3 us; the launch traced here: 77 us
  blocking collectives  31.7 us (41%)
  starting transfers between devices  17.1 us (22%)
  waiting for transfers between devices  14.2 us (18%)
  Pallas kernels  6.72 us (9%)
  other arithmetic  6.4 us (8%)
    all_to_all x2, blocking collectives, exchanged(): return lax.all_to_all(block, axes, split_axis=0, concat_axis=0, tiled=True)  31.7 us
    all_to_all x1, starting transfers between devices, exchanged(): return lax.all_to_all(block, axes, split_axis=0, concat_axis=0, tiled=True)  9.99 us
    ppermute x6, starting transfers between devices, gathered(): lax.ppermute(whole, axis, [(i, i ^ k * step) for i in range(count)])  7.14 us
    ppermute x6, waiting for transfers between devices, gathered(): lax.ppermute(whole, axis, [(i, i ^ k * step) for i in range(count)])  7.14 us
    all_to_all x1, waiting for transfers between devices, exchanged(): return lax.all_to_all(block, axes, split_axis=0, concat_axis=0, tiled=True)  7.09 us
    convert_element_type x1, other arithmetic, steering(): return value.astype(jnp.bfloat16)  6.08 us
    pallas_call x1, Pallas kernels, calibrate(): pl.pallas_call(calibrate_kernel, in_specs=[pl.BlockSpec(memory_space=pl.A...  2.42 us
  transfers between devices with their start and end apart: 7, of which 6 were waited for; matrix products, arithmetic and copies ran while one was open for 8% of the time, Pallas kernels for 0%

profile of v8, /device:TPU:1, one launch (start us, length us, event | category | flops | bytes accessed | tf_op | source)
XLA Modules:
  0.0 77.0 jit_solution(13760603203742806578)
XLA Ops:
  0.6 2.4 %calibrate.1 = bf16[16,32,1024]{2,1,0:T(8,128)(2,1)} custom-call(bf16[2,16,16,1024]{3,2,1,0:T(8,128)(2,1)} %volt_hbm.1, f32[2,16,1024]{2,1,0:T(8,128)} %gain_hbm.1), custom_call_target="tpu_custom_call" | custom-call | tf_op jit(solution)/shard_map/calibrate/pallas_call | solution.py:76
  3.1 10.0 %all-to-all-start = ((bf16[16,32,1024]{2,1,0:T(8,128)(2,1)}), bf16[16,32,1024]{2,1,0:T(8,128)(2,1)S(1)}, u32[]{:S(2)}, u32[]{:S(2)}) async-start(bf16[16,32,1024]{2,1,0:T(8,128)(2,1)} %calibrate.1), calls=%async_computation | async-start | bytes 2097152 | tf_op jit(solution)/shard_map/all_to_all | solution.py:296
  13.1 0.0 copy-start
  13.2 6.1 %fusion.7.matrix_ref = bf16[512,512]{1,0:T(8,128)(2,1)S(1)} fusion(s32[512]{0:T(512)S(1)} %get-tuple-element.23, s32[512]{0:T(512)S(1)} %get-tuple-element.27, s32[512]{0:T(512)S(1)} %get-tuple-element.21, s32[512]{0:T(512)S(1)} %get-tuple-element.28, s32[512]{0:T(512)S(1)} %get-tuple-element.25, s32[512]{0:T(512)S(1)} %get-tuple-element.26, ...), kind=kLoop, calls=%fused_computation.25 | loop fusion | flops 15204352 | bytes 547328 | tf_op jit(solution)/shard_map/convert_element_type | solution.py:33
  19.3 2.6 %collective-permute-start = (s32[1,12,256]{2,0,1:T(1,128)S(1)}, s32[1,12,256]{2,0,1:T(1,128)S(1)}, u32[]{:S(2)}, u32[]{:S(2)}) collective-permute-start(s32[1,12,256]{2,0,1:T(1,128)S(1)} %broadcast_in_dim.3), channel_id=1, source_target_pairs={{0,48},{16,32},{32,16},{48,0},{64,112},{80,96},{96,80},{112,64},{1... | collective-permute-start | bytes 36872 | tf_op jit(solution)/shard_map/ppermute | solution.py:286
  21.9 0.5 collective-permute-start.1
  22.4 0.3 collective-permute-start.2
  22.6 0.8 %collective-permute-done = s32[1,12,256]{2,0,1:T(1,128)S(1)} collective-permute-done((s32[1,12,256]{2,0,1:T(1,128)S(1)}, s32[1,12,256]{2,0,1:T(1,128)S(1)}, u32[]{:S(2)}, u32[]{:S(2)}) %collective-permute-start) | collective-permute-done | bytes 12320 | tf_op jit(solution)/shard_map/ppermute | solution.py:286
  23.4 2.8 %collective-permute-done.1 = s32[1,12,256]{2,0,1:T(1,128)S(1)} collective-permute-done((s32[1,12,256]{2,0,1:T(1,128)S(1)}, s32[1,12,256]{2,0,1:T(1,128)S(1)}, u32[]{:S(2)}, u32[]{:S(2)}) %collective-permute-start.1) | collective-permute-done | bytes 12320 | tf_op jit(solution)/shard_map/ppermute | solution.py:286
  26.3 0.0 copy-start.1
  26.3 0.1 pad_add_fusion
  26.3 3.0 %collective-permute-start.4 = (s32[4,12,256]{2,0,1:T(4,128)S(1)}, s32[4,12,256]{2,0,1:T(4,128)S(1)}, u32[]{:S(2)}, u32[]{:S(2)}) collective-permute-start(s32[4,12,256]{2,0,1:T(4,128)S(1)} %pad_add_fusion), channel_id=1, source_target_pairs={{0,128},{16,144},{32,160},{48,176},{64,192},{80,208},{96,224},{112... | collective-permute-start | bytes 147464 | tf_op jit(solution)/shard_map/ppermute | solution.py:286
  29.3 0.8 %collective-permute-start.3 = (s32[4,12,256]{2,0,1:T(4,128)S(1)}, s32[4,12,256]{2,0,1:T(4,128)S(1)}, u32[]{:S(2)}, u32[]{:S(2)}) collective-permute-start(s32[4,12,256]{2,0,1:T(4,128)S(1)} %pad_add_fusion), channel_id=1, source_target_pairs={{0,192},{16,208},{32,224},{48,240},{64,128},{80,144},{96,160},{112... | collective-permute-start | bytes 147464 | tf_op jit(solution)/shard_map/ppermute | solution.py:286
  30.1 0.9 %collective-permute-done.4 = s32[4,12,256]{2,0,1:T(4,128)S(1)} collective-permute-done((s32[4,12,256]{2,0,1:T(4,128)S(1)}, s32[4,12,256]{2,0,1:T(4,128)S(1)}, u32[]{:S(2)}, u32[]{:S(2)}) %collective-permute-start.4) | collective-permute-done | bytes 49184 | tf_op jit(solution)/shard_map/ppermute | solution.py:286
  31.0 2.6 %collective-permute-done.3 = s32[4,12,256]{2,0,1:T(4,128)S(1)} collective-permute-done((s32[4,12,256]{2,0,1:T(4,128)S(1)}, s32[4,12,256]{2,0,1:T(4,128)S(1)}, u32[]{:S(2)}, u32[]{:S(2)}) %collective-permute-start.3) | collective-permute-done | bytes 49184 | tf_op jit(solution)/shard_map/ppermute | solution.py:286
  33.6 0.1 collective-permute-done.5
  33.7 0.1 broadcast_select_fusion.12
  33.8 0.1 broadcast_select_fusion.15
  33.9 7.1 %all-to-all-done = bf16[16,32,1024]{2,1,0:T(8,128)(2,1)S(1)} async-done(((bf16[16,32,1024]{2,1,0:T(8,128)(2,1)}), bf16[16,32,1024]{2,1,0:T(8,128)(2,1)S(1)}, u32[]{:S(2)}, u32[]{:S(2)}) %all-to-all-start) | async-done | bytes 1048608 | tf_op jit(solution)/shard_map/all_to_all | solution.py:296
  41.0 1.5 %detect.1 = bf16[512,128]{1,0:T(8,128)(2,1)S(1)} custom-call(bf16[512,512]{1,0:T(8,128)(2,1)S(1)} %fusion.7.matrix_ref, bf16[512,1024]{1,0:T(8,128)(2,1)S(1)} %bitcast.5), custom_call_target="tpu_custom_call" | custom-call | tf_op jit(solution)/shard_map/detect/pallas_call | solution.py:117
  42.5 21.9 %all_to_all.15 = bf16[256,2,128]{2,1,0:T(2,128)(2,1)S(1)} all-to-all(bf16[256,2,128]{2,1,0:T(2,128)(2,1)S(1)} %bitcast.7), channel_id=1, replica_groups=mesh['freq'=16,'beam'=16] {'freq','beam'}, dimensions={0} | all-to-all | bytes 262144 | tf_op jit(solution)/shard_map/all_to_all | solution.py:296
  64.4 1.4 %tree.1 = bf16[16,16,256]{2,1,0:T(8,128)(2,1)S(1)} custom-call(bf16[512,128]{1,0:T(8,128)(2,1)S(1)} %bitcast.6, s32[12,16,256]{2,1,0:T(8,128)S(1)} %add_bitcast_fusion.shifts_ref), custom_call_target="tpu_custom_call" | custom-call | tf_op jit(solution)/shard_map/tree/pallas_call | solution.py:207
  65.8 9.8 %all_to_all.16.series_ref = bf16[16,16,256]{2,1,0:T(8,128)(2,1)S(1)} all-to-all(bf16[16,16,256]{2,1,0:T(8,128)(2,1)S(1)} %tree.1), channel_id=1, replica_groups=mesh['freq'=16,'beam'=16] {'freq'}, dimensions={0} | all-to-all | bytes 262144 | tf_op jit(solution)/shard_map/all_to_all | solution.py:296
  75.6 1.4 %peaks.1 = (bf16[16,16,256]{2,1,0:T(8,128)(2,1)}, f32[8,16,256]{2,1,0:T(8,128)}) custom-call(s32[8]{0:T(128)S(1)} %broadcast_maximum_fusion.widths_ref, bf16[16,16,256]{2,1,0:T(8,128)(2,1)S(1)} %all_to_all.16.series_ref), custom_call_target="tpu_custom_call" | custom-call | tf_op jit(solution)/shard_map/peaks/pallas_call | solution.py:258
  (16 shorter events, 0.2 us)
Async XLA Ops:
  3.1 37.9 %all-to-all-start = ((bf16[16,32,1024]{2,1,0:T(8,128)(2,1)}), bf16[16,32,1024]{2,1,0:T(8,128)(2,1)S(1)}, u32[]{:S(2)}, u32[]{:S(2)}) async-start(bf16[16,32,1024]{2,1,0:T(8,128)(2,1)} %calibrate.1), calls=%async_computation | async-start | bytes 2097152 | tf_op jit(solution)/shard_map/all_to_all | solution.py:296
  13.1 6.1 %copy-start = (s32[12,256]{1,0:T(8,128)S(1)}, s32[12,256]{1,0:T(8,128)}, u32[]{:S(2)}) copy-start(s32[12,256]{1,0:T(8,128)} %param.6) | copy-start | bytes 36868
  19.3 4.2 %collective-permute-start = (s32[1,12,256]{2,0,1:T(1,128)S(1)}, s32[1,12,256]{2,0,1:T(1,128)S(1)}, u32[]{:S(2)}, u32[]{:S(2)}) collective-permute-start(s32[1,12,256]{2,0,1:T(1,128)S(1)} %broadcast_in_dim.3), channel_id=1, source_target_pairs={{0,48},{16,32},{32,16},{48,0},{64,112},{80,96},{96,80},{112,64},{1... | collective-permute-start | bytes 36872 | tf_op jit(solution)/shard_map/ppermute | solution.py:286
  21.9 4.3 %collective-permute-start.1 = (s32[1,12,256]{2,0,1:T(1,128)S(1)}, s32[1,12,256]{2,0,1:T(1,128)S(1)}, u32[]{:S(2)}, u32[]{:S(2)}) collective-permute-start(s32[1,12,256]{2,0,1:T(1,128)S(1)} %broadcast_in_dim.3), channel_id=1, source_target_pairs={{0,32},{16,48},{32,0},{48,16},{64,96},{80,112},{96,64},{112,80},{1... | collective-permute-start | bytes 36872 | tf_op jit(solution)/shard_map/ppermute | solution.py:286
  22.4 3.8 %collective-permute-start.2 = (s32[1,12,256]{2,0,1:T(1,128)S(1)}, s32[1,12,256]{2,0,1:T(1,128)S(1)}, u32[]{:S(2)}, u32[]{:S(2)}) collective-permute-start(s32[1,12,256]{2,0,1:T(1,128)S(1)} %broadcast_in_dim.3), channel_id=1, source_target_pairs={{0,16},{16,0},{32,48},{48,32},{64,80},{80,64},{96,112},{112,96},{1... | collective-permute-start | bytes 36872 | tf_op jit(solution)/shard_map/ppermute | solution.py:286
  26.3 3.9 %copy-start.1 = (s32[8]{0:T(128)S(1)}, s32[8]{0:T(128)}, u32[]{:S(2)}) copy-start(s32[8]{0:T(128)} %param.7) | copy-start | bytes 100
  26.3 4.7 %collective-permute-start.4 = (s32[4,12,256]{2,0,1:T(4,128)S(1)}, s32[4,12,256]{2,0,1:T(4,128)S(1)}, u32[]{:S(2)}, u32[]{:S(2)}) collective-permute-start(s32[4,12,256]{2,0,1:T(4,128)S(1)} %pad_add_fusion), channel_id=1, source_target_pairs={{0,128},{16,144},{32,160},{48,176},{64,192},{80,208},{96,224},{112... | collective-permute-start | bytes 147464 | tf_op jit(solution)/shard_map/ppermute | solution.py:286
  29.3 4.3 %collective-permute-start.3 = (s32[4,12,256]{2,0,1:T(4,128)S(1)}, s32[4,12,256]{2,0,1:T(4,128)S(1)}, u32[]{:S(2)}, u32[]{:S(2)}) collective-permute-start(s32[4,12,256]{2,0,1:T(4,128)S(1)} %pad_add_fusion), channel_id=1, source_target_pairs={{0,192},{16,208},{32,224},{48,240},{64,128},{80,144},{96,160},{112... | collective-permute-start | bytes 147464 | tf_op jit(solution)/shard_map/ppermute | solution.py:286
  30.1 3.6 %collective-permute-start.5 = (s32[4,12,256]{2,0,1:T(4,128)S(1)}, s32[4,12,256]{2,0,1:T(4,128)S(1)}, u32[]{:S(2)}, u32[]{:S(2)}) collective-permute-start(s32[4,12,256]{2,0,1:T(4,128)S(1)} %pad_add_fusion), channel_id=1, source_target_pairs={{0,64},{16,80},{32,96},{48,112},{64,0},{80,16},{96,32},{112,48},{1... | collective-permute-start | bytes 147464 | tf_op jit(solution)/shard_map/ppermute | solution.py:286

commit v9 on v8

--- a/solution.py
+++ b/solution.py
@@ -142,10 +142,14 @@
 
 def folded(rows, axis, half, bits):
     place = lax.broadcasted_iota(jnp.int32, rows[0].shape, axis)
-    upper = (place & half) != 0
-    facing = [jnp.take_along_axis(x, place ^ half, axis=axis) for x in rows]
-    lower_rows = [jnp.where(upper, y, x) for x, y in zip(rows, facing)]
-    higher_rows = [jnp.where(upper, x, y) for x, y in zip(rows, facing)]
+    if axis == 0:
+        lower_rows = [jnp.take_along_axis(x, place & ~half, axis=axis) for x in rows]
+        higher_rows = [jnp.take_along_axis(x, place | half, axis=axis) for x in rows]
+    else:
+        upper = (place & half) != 0
+        facing = [jnp.take_along_axis(x, place ^ half, axis=axis) for x in rows]
+        lower_rows = [jnp.where(upper, y, x) for x, y in zip(rows, facing)]
+        higher_rows = [jnp.where(upper, x, y) for x, y in zip(rows, facing)]
     return merged(lower_rows, higher_rows, bits)
 
 

time: 77.3 us -> 77.2 us (level)
  no operation moved by 1% of the time
where the time goes in v9:
time: 77.2 us; the launch traced here: 77 us
  blocking collectives  31.7 us (41%)
  starting transfers between devices  17.1 us (22%)
  waiting for transfers between devices  14.2 us (18%)
  Pallas kernels  6.68 us (9%)
  other arithmetic  6.4 us (8%)
    all_to_all x2, blocking collectives, exchanged(): return lax.all_to_all(block, axes, split_axis=0, concat_axis=0, tiled=True)  31.7 us
    all_to_all x1, starting transfers between devices, exchanged(): return lax.all_to_all(block, axes, split_axis=0, concat_axis=0, tiled=True)  9.99 us
    ppermute x6, starting transfers between devices, gathered(): lax.ppermute(whole, axis, [(i, i ^ k * step) for i in range(count)])  7.14 us
    ppermute x6, waiting for transfers between devices, gathered(): lax.ppermute(whole, axis, [(i, i ^ k * step) for i in range(count)])  7.14 us
    all_to_all x1, waiting for transfers between devices, exchanged(): return lax.all_to_all(block, axes, split_axis=0, concat_axis=0, tiled=True)  7.09 us
    convert_element_type x1, other arithmetic, steering(): return value.astype(jnp.bfloat16)  6.08 us
    pallas_call x1, Pallas kernels, calibrate(): pl.pallas_call(calibrate_kernel, in_specs=[pl.BlockSpec(memory_space=pl.A...  2.42 us
  transfers between devices with their start and end apart: 7, of which 6 were waited for; matrix products, arithmetic and copies ran while one was open for 8% of the time, Pallas kernels for 0%

profile of v9, /device:TPU:1, one launch (start us, length us, event | category | flops | bytes accessed | tf_op | source)
XLA Modules:
  0.0 77.0 jit_solution(14380698853801112624)
XLA Ops:
  0.6 2.4 %calibrate.1 = bf16[16,32,1024]{2,1,0:T(8,128)(2,1)} custom-call(bf16[2,16,16,1024]{3,2,1,0:T(8,128)(2,1)} %volt_hbm.1, f32[2,16,1024]{2,1,0:T(8,128)} %gain_hbm.1), custom_call_target="tpu_custom_call" | custom-call | tf_op jit(solution)/shard_map/calibrate/pallas_call | solution.py:76
  3.1 10.0 %all-to-all-start = ((bf16[16,32,1024]{2,1,0:T(8,128)(2,1)}), bf16[16,32,1024]{2,1,0:T(8,128)(2,1)S(1)}, u32[]{:S(2)}, u32[]{:S(2)}) async-start(bf16[16,32,1024]{2,1,0:T(8,128)(2,1)} %calibrate.1), calls=%async_computation | async-start | bytes 2097152 | tf_op jit(solution)/shard_map/all_to_all | solution.py:300
  13.1 0.0 copy-start
  13.2 6.1 %fusion.7.matrix_ref = bf16[512,512]{1,0:T(8,128)(2,1)S(1)} fusion(s32[512]{0:T(512)S(1)} %get-tuple-element.23, s32[512]{0:T(512)S(1)} %get-tuple-element.27, s32[512]{0:T(512)S(1)} %get-tuple-element.21, s32[512]{0:T(512)S(1)} %get-tuple-element.28, s32[512]{0:T(512)S(1)} %get-tuple-element.25, s32[512]{0:T(512)S(1)} %get-tuple-element.26, ...), kind=kLoop, calls=%fused_computation.25 | loop fusion | flops 15204352 | bytes 547328 | tf_op jit(solution)/shard_map/convert_element_type | solution.py:33
  19.3 2.6 %collective-permute-start = (s32[1,12,256]{2,0,1:T(1,128)S(1)}, s32[1,12,256]{2,0,1:T(1,128)S(1)}, u32[]{:S(2)}, u32[]{:S(2)}) collective-permute-start(s32[1,12,256]{2,0,1:T(1,128)S(1)} %broadcast_in_dim.3), channel_id=1, source_target_pairs={{0,48},{16,32},{32,16},{48,0},{64,112},{80,96},{96,80},{112,64},{1... | collective-permute-start | bytes 36872 | tf_op jit(solution)/shard_map/ppermute | solution.py:290
  21.9 0.5 collective-permute-start.1
  22.4 0.3 collective-permute-start.2
  22.6 0.8 %collective-permute-done = s32[1,12,256]{2,0,1:T(1,128)S(1)} collective-permute-done((s32[1,12,256]{2,0,1:T(1,128)S(1)}, s32[1,12,256]{2,0,1:T(1,128)S(1)}, u32[]{:S(2)}, u32[]{:S(2)}) %collective-permute-start) | collective-permute-done | bytes 12320 | tf_op jit(solution)/shard_map/ppermute | solution.py:290
  23.4 2.8 %collective-permute-done.1 = s32[1,12,256]{2,0,1:T(1,128)S(1)} collective-permute-done((s32[1,12,256]{2,0,1:T(1,128)S(1)}, s32[1,12,256]{2,0,1:T(1,128)S(1)}, u32[]{:S(2)}, u32[]{:S(2)}) %collective-permute-start.1) | collective-permute-done | bytes 12320 | tf_op jit(solution)/shard_map/ppermute | solution.py:290
  26.3 0.0 copy-start.1
  26.3 0.1 pad_add_fusion
  26.3 3.0 %collective-permute-start.4 = (s32[4,12,256]{2,0,1:T(4,128)S(1)}, s32[4,12,256]{2,0,1:T(4,128)S(1)}, u32[]{:S(2)}, u32[]{:S(2)}) collective-permute-start(s32[4,12,256]{2,0,1:T(4,128)S(1)} %pad_add_fusion), channel_id=1, source_target_pairs={{0,128},{16,144},{32,160},{48,176},{64,192},{80,208},{96,224},{112... | collective-permute-start | bytes 147464 | tf_op jit(solution)/shard_map/ppermute | solution.py:290
  29.3 0.8 %collective-permute-start.3 = (s32[4,12,256]{2,0,1:T(4,128)S(1)}, s32[4,12,256]{2,0,1:T(4,128)S(1)}, u32[]{:S(2)}, u32[]{:S(2)}) collective-permute-start(s32[4,12,256]{2,0,1:T(4,128)S(1)} %pad_add_fusion), channel_id=1, source_target_pairs={{0,192},{16,208},{32,224},{48,240},{64,128},{80,144},{96,160},{112... | collective-permute-start | bytes 147464 | tf_op jit(solution)/shard_map/ppermute | solution.py:290
  30.1 0.9 %collective-permute-done.4 = s32[4,12,256]{2,0,1:T(4,128)S(1)} collective-permute-done((s32[4,12,256]{2,0,1:T(4,128)S(1)}, s32[4,12,256]{2,0,1:T(4,128)S(1)}, u32[]{:S(2)}, u32[]{:S(2)}) %collective-permute-start.4) | collective-permute-done | bytes 49184 | tf_op jit(solution)/shard_map/ppermute | solution.py:290
  31.0 2.6 %collective-permute-done.3 = s32[4,12,256]{2,0,1:T(4,128)S(1)} collective-permute-done((s32[4,12,256]{2,0,1:T(4,128)S(1)}, s32[4,12,256]{2,0,1:T(4,128)S(1)}, u32[]{:S(2)}, u32[]{:S(2)}) %collective-permute-start.3) | collective-permute-done | bytes 49184 | tf_op jit(solution)/shard_map/ppermute | solution.py:290
  33.6 0.1 collective-permute-done.5
  33.7 0.1 broadcast_select_fusion.12
  33.8 0.1 broadcast_select_fusion.15
  33.9 7.1 %all-to-all-done = bf16[16,32,1024]{2,1,0:T(8,128)(2,1)S(1)} async-done(((bf16[16,32,1024]{2,1,0:T(8,128)(2,1)}), bf16[16,32,1024]{2,1,0:T(8,128)(2,1)S(1)}, u32[]{:S(2)}, u32[]{:S(2)}) %all-to-all-start) | async-done | bytes 1048608 | tf_op jit(solution)/shard_map/all_to_all | solution.py:300
  41.0 1.5 %detect.1 = bf16[512,128]{1,0:T(8,128)(2,1)S(1)} custom-call(bf16[512,512]{1,0:T(8,128)(2,1)S(1)} %fusion.7.matrix_ref, bf16[512,1024]{1,0:T(8,128)(2,1)S(1)} %bitcast.5), custom_call_target="tpu_custom_call" | custom-call | tf_op jit(solution)/shard_map/detect/pallas_call | solution.py:117
  42.5 21.9 %all_to_all.15 = bf16[256,2,128]{2,1,0:T(2,128)(2,1)S(1)} all-to-all(bf16[256,2,128]{2,1,0:T(2,128)(2,1)S(1)} %bitcast.7), channel_id=1, replica_groups=mesh['freq'=16,'beam'=16] {'freq','beam'}, dimensions={0} | all-to-all | bytes 262144 | tf_op jit(solution)/shard_map/all_to_all | solution.py:300
  64.4 1.3 %tree.1 = bf16[16,16,256]{2,1,0:T(8,128)(2,1)S(1)} custom-call(bf16[512,128]{1,0:T(8,128)(2,1)S(1)} %bitcast.6, s32[12,16,256]{2,1,0:T(8,128)S(1)} %add_bitcast_fusion.shifts_ref), custom_call_target="tpu_custom_call" | custom-call | tf_op jit(solution)/shard_map/tree/pallas_call | solution.py:211
  65.8 9.8 %all_to_all.16.series_ref = bf16[16,16,256]{2,1,0:T(8,128)(2,1)S(1)} all-to-all(bf16[16,16,256]{2,1,0:T(8,128)(2,1)S(1)} %tree.1), channel_id=1, replica_groups=mesh['freq'=16,'beam'=16] {'freq'}, dimensions={0} | all-to-all | bytes 262144 | tf_op jit(solution)/shard_map/all_to_all | solution.py:300
  75.6 1.4 %peaks.1 = (bf16[16,16,256]{2,1,0:T(8,128)(2,1)}, f32[8,16,256]{2,1,0:T(8,128)}) custom-call(s32[8]{0:T(128)S(1)} %broadcast_maximum_fusion.widths_ref, bf16[16,16,256]{2,1,0:T(8,128)(2,1)S(1)} %all_to_all.16.series_ref), custom_call_target="tpu_custom_call" | custom-call | tf_op jit(solution)/shard_map/peaks/pallas_call | solution.py:262
  (16 shorter events, 0.2 us)
Async XLA Ops:
  3.1 37.9 %all-to-all-start = ((bf16[16,32,1024]{2,1,0:T(8,128)(2,1)}), bf16[16,32,1024]{2,1,0:T(8,128)(2,1)S(1)}, u32[]{:S(2)}, u32[]{:S(2)}) async-start(bf16[16,32,1024]{2,1,0:T(8,128)(2,1)} %calibrate.1), calls=%async_computation | async-start | bytes 2097152 | tf_op jit(solution)/shard_map/all_to_all | solution.py:300
  13.1 6.1 %copy-start = (s32[12,256]{1,0:T(8,128)S(1)}, s32[12,256]{1,0:T(8,128)}, u32[]{:S(2)}) copy-start(s32[12,256]{1,0:T(8,128)} %param.6) | copy-start | bytes 36868
  19.3 4.2 %collective-permute-start = (s32[1,12,256]{2,0,1:T(1,128)S(1)}, s32[1,12,256]{2,0,1:T(1,128)S(1)}, u32[]{:S(2)}, u32[]{:S(2)}) collective-permute-start(s32[1,12,256]{2,0,1:T(1,128)S(1)} %broadcast_in_dim.3), channel_id=1, source_target_pairs={{0,48},{16,32},{32,16},{48,0},{64,112},{80,96},{96,80},{112,64},{1... | collective-permute-start | bytes 36872 | tf_op jit(solution)/shard_map/ppermute | solution.py:290
  21.9 4.3 %collective-permute-start.1 = (s32[1,12,256]{2,0,1:T(1,128)S(1)}, s32[1,12,256]{2,0,1:T(1,128)S(1)}, u32[]{:S(2)}, u32[]{:S(2)}) collective-permute-start(s32[1,12,256]{2,0,1:T(1,128)S(1)} %broadcast_in_dim.3), channel_id=1, source_target_pairs={{0,32},{16,48},{32,0},{48,16},{64,96},{80,112},{96,64},{112,80},{1... | collective-permute-start | bytes 36872 | tf_op jit(solution)/shard_map/ppermute | solution.py:290
  22.4 3.8 %collective-permute-start.2 = (s32[1,12,256]{2,0,1:T(1,128)S(1)}, s32[1,12,256]{2,0,1:T(1,128)S(1)}, u32[]{:S(2)}, u32[]{:S(2)}) collective-permute-start(s32[1,12,256]{2,0,1:T(1,128)S(1)} %broadcast_in_dim.3), channel_id=1, source_target_pairs={{0,16},{16,0},{32,48},{48,32},{64,80},{80,64},{96,112},{112,96},{1... | collective-permute-start | bytes 36872 | tf_op jit(solution)/shard_map/ppermute | solution.py:290
  26.3 3.9 %copy-start.1 = (s32[8]{0:T(128)S(1)}, s32[8]{0:T(128)}, u32[]{:S(2)}) copy-start(s32[8]{0:T(128)} %param.7) | copy-start | bytes 100
  26.3 4.7 %collective-permute-start.4 = (s32[4,12,256]{2,0,1:T(4,128)S(1)}, s32[4,12,256]{2,0,1:T(4,128)S(1)}, u32[]{:S(2)}, u32[]{:S(2)}) collective-permute-start(s32[4,12,256]{2,0,1:T(4,128)S(1)} %pad_add_fusion), channel_id=1, source_target_pairs={{0,128},{16,144},{32,160},{48,176},{64,192},{80,208},{96,224},{112... | collective-permute-start | bytes 147464 | tf_op jit(solution)/shard_map/ppermute | solution.py:290
  29.3 4.3 %collective-permute-start.3 = (s32[4,12,256]{2,0,1:T(4,128)S(1)}, s32[4,12,256]{2,0,1:T(4,128)S(1)}, u32[]{:S(2)}, u32[]{:S(2)}) collective-permute-start(s32[4,12,256]{2,0,1:T(4,128)S(1)} %pad_add_fusion), channel_id=1, source_target_pairs={{0,192},{16,208},{32,224},{48,240},{64,128},{80,144},{96,160},{112... | collective-permute-start | bytes 147464 | tf_op jit(solution)/shard_map/ppermute | solution.py:290
  30.1 3.6 %collective-permute-start.5 = (s32[4,12,256]{2,0,1:T(4,128)S(1)}, s32[4,12,256]{2,0,1:T(4,128)S(1)}, u32[]{:S(2)}, u32[]{:S(2)}) collective-permute-start(s32[4,12,256]{2,0,1:T(4,128)S(1)} %pad_add_fusion), channel_id=1, source_target_pairs={{0,64},{16,80},{32,96},{48,112},{64,0},{80,16},{96,32},{112,48},{1... | collective-permute-start | bytes 147464 | tf_op jit(solution)/shard_map/ppermute | solution.py:290
